TPU v7x, 128 devices: a whole 4x4x4 slice. The times are simulated.
128 devices in a mesh: pb: 16 (over y_lo, x, core), kv: 8 (over y_hi, z).
Axes of the slice: x: 4, y: 4 (y_hi: 2, y_lo: 2; y = y_hi * 2 + y_lo), z: 4, core: 2. Of those that a mesh axis runs over, the one named last changes fastest.
Arguments:
- queries: bfloat16 [16384, 1024], P(('pb', 'kv')), may hold values from -6 to 6
- key_rows: bfloat16 [16384, 128], P(('kv', 'pb')), may hold values from -6 to 6
- value_rows: bfloat16 [16384, 128], P(('kv', 'pb')), may hold values from -0.59765625 to 0.59765625
- output: bfloat16 [16384, 1024], P(('pb', 'kv')), may hold values from -1.796875 to 1.796875
- out_grad: bfloat16 [16384, 1024], P(('pb', 'kv')), may hold values from -6 to 6
- log_norm: float32 [8, 16384], P(None, ('pb', 'kv')), as said below
- positions: int32 [16384], replicated, may hold values from 0 to 16383, as said below
Outputs:
- query_grad: float32 [16384, 1024], P(('pb', 'kv'))
- key_grad: float32 [16384, 128], P(('kv', 'pb'))
- value_grad: float32 [16384, 128], P(('kv', 'pb'))
Inputs may be any that keep to these rules, and one draw needn't show every extreme that they name: A permutation of 0 to 16383: row r holds the token at position positions[r]. log_norm[h, r] - log(1 + positions[r]) lies between 0.25 and 0.75.
All inputs are finite; a program needn't handle non-finite values.
Results may differ from a plain program's by a relative error of at most 0.0041.
Values may be sent and summed in bfloat16 or wider, within the bound.
No kernel may reach another device: no remote copies, remote signals or barrier semaphores. Data moves between devices by JAX's collectives and lax.ppermute only.
A program may use at most 64 MiB of HBM per device.

v0:
```python
import math

import jax
import jax.numpy as jnp
from jax import lax
from jax.sharding import PartitionSpec as P


def block_grads(query_all, grad_all, norm_all, delta_all, query_pos, key_part, value_part, key_pos):
    query_count = query_all.shape[0]
    head_count = norm_all.shape[0]
    head_width = key_part.shape[1]
    inv_root = 1.0 / math.sqrt(head_width)
    rows_block = min(query_count, 128)
    count_blocks = query_count // rows_block
    query_blocks = query_all.reshape(count_blocks, rows_block, head_count, head_width)
    grad_blocks = grad_all.reshape(count_blocks, rows_block, head_count, head_width)
    norm_blocks = norm_all.T.reshape(count_blocks, rows_block, head_count)
    delta_blocks = delta_all.T.reshape(count_blocks, rows_block, head_count)
    pos_blocks = query_pos.reshape(count_blocks, rows_block)

    def one_block(running, inputs):
        key_sum, value_sum = running
        query_block, grad_block, norm_block, delta_block, pos_block = inputs
        scores = (
            jnp.einsum("tgd,cd->tgc", query_block, key_part, preferred_element_type=jnp.float32)
            * inv_root
        )
        visible = (key_pos[None, :] <= pos_block[:, None])[:, None, :]
        probs_full = jnp.where(visible, jnp.exp(scores - norm_block[:, :, None]), 0.0)
        probs_low = probs_full.astype(jnp.bfloat16)
        value_sum = value_sum + jnp.einsum(
            "tgc,tgd->cd", probs_low, grad_block, preferred_element_type=jnp.float32
        )
        grad_probs = jnp.einsum(
            "tgd,cd->tgc", grad_block, value_part, preferred_element_type=jnp.float32
        )
        grad_scores = (probs_full * (grad_probs - delta_block[:, :, None]) * inv_root).astype(
            jnp.bfloat16
        )
        query_part = jnp.einsum(
            "tgc,cd->tgd", grad_scores, key_part, preferred_element_type=jnp.float32
        )
        key_sum = key_sum + jnp.einsum(
            "tgc,tgd->cd", grad_scores, query_block, preferred_element_type=jnp.float32
        )
        return ((key_sum, value_sum), query_part.reshape(rows_block, head_count * head_width))

    empty_grad = jnp.zeros((key_part.shape[0], head_width), jnp.float32)
    (key_sum, value_sum), query_parts = lax.scan(
        one_block,
        (empty_grad, empty_grad),
        (query_blocks, grad_blocks, norm_blocks, delta_blocks, pos_blocks),
    )
    return (query_parts.reshape(query_count, head_count * head_width), key_sum, value_sum)


def row_terms(grad_rows, saved_rows, head_count, head_width):
    local_rows = grad_rows.shape[0]
    product = grad_rows.astype(jnp.float32) * saved_rows.astype(jnp.float32)
    return jnp.sum(product.reshape(local_rows, head_count, head_width), axis=2).T


def shards(queries, key_rows, value_rows, output, out_grad, log_norm, positions):
    head_count = log_norm.shape[0]
    head_width = key_rows.shape[1]
    query_count = queries.shape[0] * lax.axis_size("kv")
    key_count = key_rows.shape[0] * lax.axis_size("pb")
    query_pos = lax.dynamic_slice_in_dim(positions, lax.axis_index("pb") * query_count, query_count)
    key_pos = lax.dynamic_slice_in_dim(positions, lax.axis_index("kv") * key_count, key_count)
    query_all, grad_all, saved_all = (
        lax.all_gather(queries, "kv", axis=0, tiled=True),
        lax.all_gather(out_grad, "kv", axis=0, tiled=True),
        lax.all_gather(output, "kv", axis=0, tiled=True),
    )
    norm_all = lax.all_gather(log_norm, "kv", axis=1, tiled=True)
    delta_all = row_terms(grad_all, saved_all, head_count, head_width)
    key_all, value_all = (
        lax.all_gather(key_rows, "pb", axis=0, tiled=True),
        lax.all_gather(value_rows, "pb", axis=0, tiled=True),
    )
    query_sum, key_sum, value_sum = block_grads(
        query_all, grad_all, norm_all, delta_all, query_pos, key_all, value_all, key_pos
    )
    query_grad = lax.psum_scatter(query_sum, "kv", scatter_dimension=0, tiled=True)
    key_grad, value_grad = (
        lax.psum_scatter(key_sum, "pb", scatter_dimension=0, tiled=True),
        lax.psum_scatter(value_sum, "pb", scatter_dimension=0, tiled=True),
    )
    return (query_grad, key_grad, value_grad)


def solution(mesh):
    return jax.shard_map(
        shards,
        mesh=mesh,
        in_specs=(
            P(("pb", "kv"), None),
            P(("kv", "pb"), None),
            P(("kv", "pb"), None),
            P(("pb", "kv"), None),
            P(("pb", "kv"), None),
            P(None, ("pb", "kv")),
            P(),
        ),
        out_specs=(P(("pb", "kv"), None), P(("kv", "pb"), None), P(("kv", "pb"), None)),
        check_vma=False,
    )
```

profile of v0, /device:TPU:0, one launch (start us, length us, event | category | flops | bytes accessed | tf_op | source)
XLA Modules:
  0.0 520.1 jit_solution(14944379486052491062)
XLA Ops:
  9.5 0.9 copy.25
  10.3 35.7 %all_gather.20 = f32[8,1024]{1,0:T(8,128)S(1)} all-gather(f32[8,128]{1,0:T(8,128)} %param.14), channel_id=1, replica_groups=mesh['pb'=16,'kv'=8] {'kv'}, dimensions={1}, use_global_device_ids=true | all-gather | bytes 36864 | tf_op jit(solution)/shard_map/all_gather | solution.py:76
  46.7 20.4 %all_gather.19 = bf16[2048,128]{0,1:T(8,128)(2,1)S(1)} all-gather(bf16[128,128]{0,1:T(8,128)(2,1)S(1)} %copy.25), channel_id=1, replica_groups=mesh['pb'=16,'kv'=8] {'pb'}, dimensions={0}, use_global_device_ids=true | all-gather | bytes 557056 | tf_op jit(solution)/shard_map/all_gather | solution.py:79
  67.2 18.0 %all_gather.22 = bf16[2048,128]{1,0:T(8,128)(2,1)S(1)} all-gather(bf16[128,128]{1,0:T(8,128)(2,1)} %param.11), channel_id=1, replica_groups=mesh['pb'=16,'kv'=8] {'pb'}, dimensions={0}, use_global_device_ids=true | all-gather | bytes 557056 | tf_op jit(solution)/shard_map/all_gather | solution.py:80
  85.2 3.6 copy.39
  88.8 33.8 %all-gather.6.cloned.1.call-done = bf16[1024,1024]{1,0:T(8,128)(2,1)} async-done(((bf16[128,1024]{1,0:T(8,128)(2,1)}), bf16[1024,1024]{1,0:T(8,128)(2,1)}) %all-gather.6.cloned.1.call-update) | async-done | bytes 2097168 | tf_op jit(solution)/shard_map/all_gather | solution.py:73
  122.6 3.5 copy.40
  126.2 50.7 %all-gather.8.cloned.1.call-done = bf16[1024,1024]{1,0:T(8,128)(2,1)} async-done(((bf16[128,1024]{1,0:T(8,128)(2,1)}), bf16[1024,1024]{1,0:T(8,128)(2,1)}) %all-gather.8.cloned.1.call-update) | async-done | bytes 2097168 | tf_op jit(solution)/shard_map/all_gather | solution.py:74
  176.9 3.1 multiply_bitcast_fusion
  180.0 3.0 copy.41
  183.0 3.4 reduce_sum.9
  186.5 116.3 %while.15 = (s32[]{:T(128)}, f32[2048,128]{1,0:T(8,128)S(1)}, f32[2048,128]{1,0:T(8,128)}, f32[8,128,1024]{2,1,0:T(8,128)}, s32[2048]{0:T(1024)S(1)}, /*index=5*...) while((s32[]{:T(128)}, f32[2048,128]{1,0:T(8,128)S(1)}, ...), condition=%wide.region_2.3_spmd.clone, body=%wide.region_1.2_spmd.clone.sunk | while | flops 2708733952 | bytes 49059492 | solution.py:50
  186.9 1.1 constant_dynamic-slice_fusion.4
  188.0 1.2 fusion.38
  189.3 3.6 fusion.41
  192.8 3.2 multiply_convert_fusion.2
  196.1 1.5 fusion.42
  197.6 1.5 fusion.40
  200.4 1.1 constant_dynamic-slice_fusion.4
  201.5 1.2 fusion.38
  202.7 4.8 fusion.41
  207.5 3.2 multiply_convert_fusion.2
  210.7 1.5 fusion.42
  212.2 1.5 fusion.40
  215.0 1.1 constant_dynamic-slice_fusion.4
  216.1 1.2 fusion.38
  217.4 4.8 fusion.41
  222.2 3.2 multiply_convert_fusion.2
  225.4 1.5 fusion.42
  226.9 1.5 fusion.40
  229.7 1.1 constant_dynamic-slice_fusion.4
  230.8 1.2 fusion.38
  232.0 4.8 fusion.41
  236.8 3.2 multiply_convert_fusion.2
  240.0 1.5 fusion.42
  241.6 1.5 fusion.40
  244.4 1.1 constant_dynamic-slice_fusion.4
  245.5 1.2 fusion.38
  246.7 4.8 fusion.41
  251.5 3.2 multiply_convert_fusion.2
  254.7 1.5 fusion.42
  256.2 1.5 fusion.40
  259.0 1.1 constant_dynamic-slice_fusion.4
  260.1 1.2 fusion.38
  261.4 4.8 fusion.41
  266.1 3.2 multiply_convert_fusion.2
  269.4 1.5 fusion.42
  270.9 1.5 fusion.40
  273.7 1.1 constant_dynamic-slice_fusion.4
  274.8 1.2 fusion.38
  276.0 4.8 fusion.41
  280.8 3.2 multiply_convert_fusion.2
  284.0 1.5 fusion.42
  285.6 1.5 fusion.40
  288.4 1.1 constant_dynamic-slice_fusion.4
  289.5 1.2 fusion.38
  290.7 4.8 fusion.41
  295.5 3.2 multiply_convert_fusion.2
  298.7 1.5 fusion.42
  300.2 1.5 fusion.40
  302.8 1.0 copy-done
  305.0 58.0 %reduce-scatter.6.cloned.1.call-done = f32[128,128]{1,0:T(8,128)} async-done(((f32[2048,128]{1,0:T(8,128)}), f32[128,128]{1,0:T(8,128)}) %reduce-scatter.6.cloned.1.call-update) | async-done | bytes 65552 | tf_op jit(solution)/shard_map/reduce_scatter | solution.py:87
  362.9 62.8 %reduce-scatter.8.cloned.1.call-done = f32[128,128]{1,0:T(8,128)} async-done(((f32[2048,128]{1,0:T(8,128)}), f32[128,128]{1,0:T(8,128)}) %reduce-scatter.8.cloned.1.call-update) | async-done | bytes 65552 | tf_op jit(solution)/shard_map/reduce_scatter | solution.py:88
  425.7 87.5 %reduce-scatter.4.cloned.1.call-done = f32[128,1024]{1,0:T(8,128)} async-done(((f32[1024,1024]{1,0:T(8,128)}), f32[128,1024]{1,0:T(8,128)}) %reduce-scatter.4.cloned.1.call-update) | async-done | bytes 524304 | tf_op jit(solution)/shard_map/reduce_scatter | solution.py:85
  (61 shorter events, 14.4 us)
Async XLA Ops:
  7.2 78.0 %all-gather.4.cloned.1.call-start = ((), (), s32[]{:S(2)}) async-start(), calls=%async_computation.3 | async-start | bytes 2359296 | tf_op jit(solution)/shard_map/all_gather | solution.py:72
  7.9 114.7 %all-gather.6.cloned.1.call-start = ((), (), s32[]{:S(2)}) async-start(), calls=%async_computation.4 | async-start | bytes 2359296 | tf_op jit(solution)/shard_map/all_gather | solution.py:73
  8.6 168.2 %all-gather.8.cloned.1.call-start = ((), (), s32[]{:S(2)}) async-start(), calls=%async_computation.5 | async-start | bytes 2359296 | tf_op jit(solution)/shard_map/all_gather | solution.py:74
  9.4 353.6 %reduce-scatter.6.cloned.1.call-start = ((), (), s32[]{:S(2)}) async-start(), calls=%async_computation.7 | async-start | bytes 1114112 | tf_op jit(solution)/shard_map/reduce_scatter | solution.py:87
  183.0 3.5 dynamic-slice-start
  302.8 1.0 copy-start
  303.8 121.9 %reduce-scatter.8.cloned.1.call-start = ((), (), s32[]{:S(2)}) async-start(), calls=%async_computation.8 | async-start | bytes 1114112 | tf_op jit(solution)/shard_map/reduce_scatter | solution.py:88
  304.4 208.9 %reduce-scatter.4.cloned.1.call-start = ((), (), s32[]{:S(2)}) async-start(), calls=%async_computation.6 | async-start | bytes 4718592 | tf_op jit(solution)/shard_map/reduce_scatter | solution.py:85
Sparse Core Ops, SparseCore 0:
  10.4 57.8 all-gather.3
  70.6 51.9 all-gather.5
  125.0 51.8 all-gather.7
  303.9 58.9 reduce-scatter.5
  365.9 59.8 reduce-scatter.7
  430.0 83.2 reduce-scatter.3
where the time goes:
time: 521 us; the launch traced here: 520 us
  waiting for transfers between devices  296 us (57%)
  matrix products  97 us (19%)
  blocking collectives  74.2 us (14%)
  local copies, waits for them, and re-layouts  29.8 us (6%)
  between operations  14.2 us (3%)
  other arithmetic  8.19 us (2%)
    reduce_scatter x1, waiting for transfers between devices, shards(): lax.psum_scatter(query_sum, 'kv', scatter_dimension=0, tiled=True)  87.5 us
    reduce_scatter x1, waiting for transfers between devices, shards(): lax.psum_scatter(value_sum, 'pb', scatter_dimension=0, tiled=True)  62.8 us
    reduce_scatter x1, waiting for transfers between devices, shards(): lax.psum_scatter(key_sum, 'pb', scatter_dimension=0, tiled=True)  58 us
    all_gather x1, waiting for transfers between devices, shards(): lax.all_gather(output, 'kv', axis=0, tiled=True)  50.7 us
    dot_general x8, matrix products, one_block(): jnp.einsum('tgc,tgd->cd', probs_low, grad_block, preferred_element_type=j...  37.1 us
    all_gather x1, blocking collectives, shards(): norm_all = lax.all_gather(log_norm, 'kv', axis=1, tiled=True)  35.7 us
    all_gather x1, waiting for transfers between devices, shards(): lax.all_gather(out_grad, 'kv', axis=0, tiled=True)  33.8 us
    dot_general x8, matrix products, one_block(): jnp.einsum('tgd,cd->tgc', grad_block, value_part, preferred_element_type=...  25.7 us
  transfers between devices with their start and end apart: 6, of which 5 were waited for; matrix products, arithmetic and copies ran while one was open for 2% of the time, Pallas kernels for 0%

commit v1 on v0

v1 whole, which is shorter than its diff:
```python
import math

import jax
import jax.numpy as jnp
from jax import lax
from jax.experimental import pallas as pl
from jax.experimental.pallas import tpu as pltpu
from jax.sharding import Mesh, PartitionSpec as P

AXES = ("ylo", "x", "core", "yhi", "z")
SIZES = (2, 4, 2, 2, 4)
PLANE = ("yhi", "ylo", "x")
HEADS = 8
WIDTH = 128
RUN = 128
BAND = 16
BANDS = RUN // BAND
QRUNS = 4
KRUNS = 32
QROWS = QRUNS * BAND * HEADS
KROWS = KRUNS * BAND
HALF = 1024 + 32
LOG2E = math.log2(math.e)
INV_ROOT = 1.0 / math.sqrt(WIDTH)
F32 = jnp.float32
BF16 = jnp.bfloat16
HIGH = lax.Precision.HIGHEST


def rank_matrices(pos_row):
    by_lane = jnp.broadcast_to(pos_row, (RUN, RUN))
    by_row = by_lane.T
    rank_lane = jnp.sum((by_row < by_lane).astype(F32), axis=0, keepdims=True)
    row_id = lax.broadcasted_iota(jnp.int32, (RUN, RUN), 0).astype(F32)
    place = (rank_lane == row_id).astype(F32)
    return place, rank_lane


def split3(x):
    hi = x.astype(BF16)
    rest = x - hi.astype(F32)
    mid = rest.astype(BF16)
    low = (rest - mid.astype(F32)).astype(BF16)
    return hi, mid, low


def pack_rows(values, place, rank_lane):
    ordered = lax.dot_general(
        values, place, (((1,), (1,)), ((), ())), precision=HIGH, preferred_element_type=F32
    )
    pieces = []
    for band in range(BANDS):
        row = jnp.concatenate(
            [ordered[h : h + 1, band * BAND : (band + 1) * BAND] for h in range(HEADS)], axis=1
        )
        pieces.append(row)
    return jnp.concatenate(pieces, axis=0)


def prep_kernel(q_ref, g_ref, o_ref, ln_ref, k_ref, v_ref, qpos_ref, kpos_ref, pay_ref, kv_ref):
    place_q, rank_q = rank_matrices(qpos_ref[...].astype(F32))
    place_k, _ = rank_matrices(kpos_ref[...].astype(F32))
    low_q = place_q.astype(BF16)
    low_k = place_k.astype(BF16)
    q_sorted = jnp.dot(low_q, q_ref[...], preferred_element_type=F32).astype(BF16)
    g_sorted = jnp.dot(low_q, g_ref[...], preferred_element_type=F32).astype(BF16)
    for h in range(HEADS):
        for band in range(BANDS):
            at = (band * HEADS + h) * BAND
            rows = slice(band * BAND, (band + 1) * BAND)
            cols = slice(h * WIDTH, (h + 1) * WIDTH)
            pay_ref[at : at + BAND, :] = q_sorted[rows, cols]
            pay_ref[HALF + at : HALF + at + BAND, :] = g_sorted[rows, cols]
    product = g_ref[...].astype(F32) * o_ref[...].astype(F32)
    columns = [
        jnp.sum(product[:, h * WIDTH : (h + 1) * WIDTH], axis=1, keepdims=True)
        for h in range(HEADS)
    ]
    lane_id = lax.broadcasted_iota(jnp.int32, (RUN, RUN), 1)
    delta_wide = jnp.zeros((RUN, RUN), F32)
    for h in range(HEADS):
        delta_wide = jnp.where(lane_id == h, columns[h], delta_wide)
    delta = delta_wide.T[:HEADS]
    fill = jnp.zeros((BANDS, RUN), BF16)
    ln_hi, ln_mid, ln_low = split3(pack_rows(ln_ref[...] * LOG2E, place_q, rank_q))
    pay_ref[1024:1056, :] = jnp.concatenate([ln_hi, ln_mid, ln_low, fill], axis=0)
    d_hi, d_mid, d_low = split3(pack_rows(delta, place_q, rank_q))
    pay_ref[HALF + 1024 : HALF + 1056, :] = jnp.concatenate([d_hi, d_mid, d_low, fill], axis=0)
    k_sorted = jnp.dot(low_k, k_ref[...], preferred_element_type=F32).astype(BF16)
    v_sorted = jnp.dot(low_k, v_ref[...], preferred_element_type=F32).astype(BF16)
    kv = jnp.concatenate([k_sorted, v_sorted], axis=1)
    for i in range(16):
        kv_ref[i] = kv


def prep(q, g, o, ln, k, v, qpos, kpos):
    return pl.pallas_call(
        prep_kernel,
        out_shape=(
            jax.ShapeDtypeStruct((2 * HALF, WIDTH), BF16),
            jax.ShapeDtypeStruct((16, RUN, 2 * WIDTH), BF16),
        ),
        compiler_params=pltpu.CompilerParams(vmem_limit_bytes=32 * 1024 * 1024),
        name="prep",
    )(q, g, o, ln, k, v, qpos, kpos)


def sorted_kernel(pos_ref, out_ref):
    pos = pos_ref[...].astype(F32)
    rank = jnp.zeros_like(pos)
    for s in range(1, RUN):
        rank = rank + (pltpu.roll(pos, s, 1) < pos).astype(F32)
    lane = lax.broadcasted_iota(jnp.int32, pos.shape, 1).astype(F32)
    ordered = jnp.where(rank == lane, pos, 0.0)
    for s in range(1, RUN):
        ordered = ordered + jnp.where(
            pltpu.roll(rank, s, 1) == lane, pltpu.roll(pos, s, 1), 0.0
        )
    out_ref[...] = ordered


def sort_runs(pos):
    return pl.pallas_call(
        sorted_kernel, out_shape=jax.ShapeDtypeStruct(pos.shape, F32), name="sort_runs"
    )(pos)


def main_kernel(
    pos_ref, a_ref, r_ref, l_ref, oq_ref, og_ref, kva_ref, kvb_ref,
    dq_ref, dkva_ref, dkvb_ref,
    qs, gs, ks, vs, lns, ds, qps, kps, dqs, dks, dvs,
):
    for band in range(BANDS):
        rows = slice(band * RUN, (band + 1) * RUN)
        g_rows = slice(HALF + band * RUN, HALF + (band + 1) * RUN)
        for run, (qr, gr, grows) in enumerate((
            (a_ref, a_ref, g_rows), (r_ref, r_ref, g_rows),
            (l_ref, l_ref, g_rows), (oq_ref, og_ref, rows),
        )):
            at = slice(run * RUN, (run + 1) * RUN)
            qs[band, at, :] = qr[rows, :]
            gs[band, at, :] = gr[grows, :]
    for run, (qr, gr, base) in enumerate((
        (a_ref, a_ref, HALF), (r_ref, r_ref, HALF), (l_ref, l_ref, HALF), (oq_ref, og_ref, 0),
    )):
        ln3 = qr[1024:1056, :].astype(F32)
        d3 = gr[base + 1024 : base + 1056, :].astype(F32)
        lns[:, run * RUN : (run + 1) * RUN] = (ln3[16:24] + ln3[8:16]) + ln3[0:8]
        ds[:, run * RUN : (run + 1) * RUN] = (d3[16:24] + d3[8:16]) + d3[0:8]
        row = pos_ref[KRUNS + run : KRUNS + run + 1, :]
        for band in range(BANDS):
            piece = row[:, band * BAND : (band + 1) * BAND]
            qps[band : band + 1, run * RUN : (run + 1) * RUN] = jnp.concatenate(
                [piece] * HEADS, axis=1
            )
    key_pos = pos_ref[0:KRUNS, :].T
    for run in range(KRUNS):
        ref = kva_ref if run < 16 else kvb_ref
        for band in range(BANDS):
            rows = slice(band * BAND, (band + 1) * BAND)
            at = slice(run * BAND, (run + 1) * BAND)
            ks[band, at, :] = ref[run % 16, rows, :WIDTH]
            vs[band, at, :] = ref[run % 16, rows, WIDTH:]
            kps[band, at, :] = jnp.broadcast_to(key_pos[rows, run : run + 1], (BAND, WIDTH))
    dqs[...] = jnp.zeros_like(dqs)
    dks[...] = jnp.zeros_like(dks)
    dvs[...] = jnp.zeros_like(dvs)

    def key_band(t, carry):
        key = ks[t]
        value = vs[t]
        first_key = jnp.min(kps[t])

        def query_band(u, inner):
            @pl.when(jnp.max(qps[pl.ds(u, 1), :]) >= first_key)
            def _():
                q = qs[u]
                g = gs[u]
                scores = lax.dot_general(
                    key, q, (((1,), (1,)), ((), ())), preferred_element_type=F32
                )
                ln = lns[pl.ds(u, 1), :]
                visible = kps[t][:, 0:1] <= qps[pl.ds(u, 1), :]
                probs = jnp.where(visible, jnp.exp2(scores * (INV_ROOT * LOG2E) - ln), 0.0)
                dvs[t] += jnp.dot(probs.astype(BF16), g, preferred_element_type=F32)
                grad_probs = lax.dot_general(
                    value, g, (((1,), (1,)), ((), ())), preferred_element_type=F32
                )
                grad_scores = (probs * (grad_probs - ds[pl.ds(u, 1), :])).astype(BF16)
                dks[t] += jnp.dot(grad_scores, q, preferred_element_type=F32)
                dqs[u] += lax.dot_general(
                    grad_scores, key, (((0,), (0,)), ((), ())), preferred_element_type=F32
                )

            return inner

        return lax.fori_loop(0, BANDS, query_band, carry)

    lax.fori_loop(0, BANDS, key_band, 0)

    for band in range(BANDS):
        for run in range(QRUNS):
            dq_ref[run, band * RUN : (band + 1) * RUN, :] = (
                dqs[band, run * RUN : (run + 1) * RUN, :] * INV_ROOT
            ).astype(BF16)
    for run in range(KRUNS):
        ref = dkva_ref if run < 16 else dkvb_ref
        for band in range(BANDS):
            rows = slice(band * BAND, (band + 1) * BAND)
            at = slice(run * BAND, (run + 1) * BAND)
            ref[run % 16, rows, :WIDTH] = (dks[band, at, :] * INV_ROOT).astype(BF16)
            ref[run % 16, rows, WIDTH:] = dvs[band, at, :].astype(BF16)


def main(pos, a, r, l, oq, og, kva, kvb):
    return pl.pallas_call(
        main_kernel,
        out_shape=(
            jax.ShapeDtypeStruct((QRUNS, 1024, WIDTH), BF16),
            jax.ShapeDtypeStruct((16, RUN, 2 * WIDTH), BF16),
            jax.ShapeDtypeStruct((16, RUN, 2 * WIDTH), BF16),
        ),
        scratch_shapes=[
            pltpu.VMEM((BANDS, QROWS, WIDTH), BF16),
            pltpu.VMEM((BANDS, QROWS, WIDTH), BF16),
            pltpu.VMEM((BANDS, KROWS, WIDTH), BF16),
            pltpu.VMEM((BANDS, KROWS, WIDTH), BF16),
            pltpu.VMEM((BANDS, QROWS), F32),
            pltpu.VMEM((BANDS, QROWS), F32),
            pltpu.VMEM((BANDS, QROWS), F32),
            pltpu.VMEM((BANDS, KROWS, WIDTH), F32),
            pltpu.VMEM((BANDS, QROWS, WIDTH), F32),
            pltpu.VMEM((BANDS, KROWS, WIDTH), F32),
            pltpu.VMEM((BANDS, KROWS, WIDTH), F32),
        ],
        compiler_params=pltpu.CompilerParams(vmem_limit_bytes=56 * 1024 * 1024),
        name="block_grads",
    )(pos, a, r, l, oq, og, kva, kvb)


def query_kernel(own_ref, b_ref, c_ref, d_ref, pos_ref, out_ref):
    place, _ = rank_matrices(pos_ref[...].astype(F32))
    total = (
        own_ref[...].astype(F32) + b_ref[...].astype(F32)
        + c_ref[...].astype(F32) + d_ref[...].astype(F32)
    ).reshape(BANDS, HEADS, BAND, WIDTH)
    for h in range(HEADS):
        out_ref[:, h * WIDTH : (h + 1) * WIDTH] = lax.dot_general(
            place, total[:, h].reshape(RUN, WIDTH), (((0,), (0,)), ((), ())),
            precision=HIGH, preferred_element_type=F32,
        )


def key_kernel(parts_ref, pos_ref, dk_ref, dv_ref):
    place, _ = rank_matrices(pos_ref[...].astype(F32))
    total = parts_ref[0].astype(F32)
    for i in range(1, 16):
        total = total + parts_ref[i].astype(F32)
    result = lax.dot_general(
        place, total, (((0,), (0,)), ((), ())), precision=HIGH, preferred_element_type=F32
    )
    dk_ref[...] = result[:, :WIDTH]
    dv_ref[...] = result[:, WIDTH:]


def shards(queries, key_rows, value_rows, output, out_grad, log_norm, positions):
    ylo, x, core, yhi, z = (lax.axis_index(name) for name in AXES)
    pb = (ylo * 4 + x) * 2 + core
    q_block = pb * 8 + yhi * 4 + z
    k_block = (yhi * 4 + z) * 16 + pb
    pos = positions.reshape(128, RUN)
    qpos = lax.dynamic_slice_in_dim(pos, q_block, 1)
    kpos = lax.dynamic_slice_in_dim(pos, k_block, 1)
    payload, kv_out = prep(
        queries, out_grad, output, log_norm, key_rows, value_rows, qpos, kpos
    )

    def along_z(array, step):
        return lax.ppermute(array, "z", [(i, (i + step) % 4) for i in range(4)])

    from_left = along_z(payload, 1)
    from_right = along_z(payload, 3)
    far_q = along_z(from_left[:HALF], 1)
    far_g = along_z(from_right[HALF:], 3)
    kv_mine = lax.all_to_all(kv_out, PLANE, 0, 0, tiled=True)
    kv_other = lax.ppermute(kv_mine, "core", [(0, 1), (1, 0)])

    plane = pos.reshape(2, 4, 2, 4, 2, RUN)
    plane = lax.dynamic_slice_in_dim(plane, z, 1, axis=1)[:, 0]
    mine = lax.dynamic_slice_in_dim(plane, core, 1, axis=3).reshape(16, RUN)
    other = lax.dynamic_slice_in_dim(plane, 1 - core, 1, axis=3).reshape(16, RUN)
    line = lax.dynamic_slice_in_dim(pos, q_block - z, 4)
    line = jnp.concatenate([line, line], axis=0)
    line = lax.dynamic_slice_in_dim(line, z, 4)
    line = jnp.stack([line[0], line[3], line[1], line[2]])
    runs = sort_runs(jnp.concatenate([mine, other, line, line], axis=0))

    dq, dkv_mine, dkv_other = main(
        runs, payload, from_left, from_right, far_q, far_g, kv_mine, kv_other
    )
    dq_left = along_z(dq[1], 3)
    dq_right = along_z(dq[2], 1)
    dq_far = along_z(dq[3], 2)
    dkv_in = lax.ppermute(dkv_other, "core", [(0, 1), (1, 0)])
    dkv_sum = (dkv_mine.astype(F32) + dkv_in.astype(F32)).astype(BF16)
    dkv_parts = lax.all_to_all(dkv_sum, PLANE, 0, 0, tiled=True)
    query_grad = pl.pallas_call(
        query_kernel, out_shape=jax.ShapeDtypeStruct((RUN, HEADS * WIDTH), F32), name="query_sum",
        compiler_params=pltpu.CompilerParams(vmem_limit_bytes=32 * 1024 * 1024),
    )(dq[0], dq_left, dq_right, dq_far, qpos)
    key_grad, value_grad = pl.pallas_call(
        key_kernel,
        out_shape=(
            jax.ShapeDtypeStruct((RUN, WIDTH), F32),
            jax.ShapeDtypeStruct((RUN, WIDTH), F32),
        ),
        name="key_sum",
        compiler_params=pltpu.CompilerParams(vmem_limit_bytes=32 * 1024 * 1024),
    )(dkv_parts, kpos)
    return query_grad, key_grad, value_grad


def solution(mesh):
    fine = Mesh(mesh.devices.reshape(SIZES), AXES)
    by_query = P(AXES, None)
    by_key = P(("yhi", "z", "ylo", "x", "core"), None)
    return jax.shard_map(
        shards,
        mesh=fine,
        in_specs=(by_query, by_key, by_key, by_query, by_query, P(None, AXES), P()),
        out_specs=(by_query, by_key, by_key),
        check_vma=False,
    )
```

time: 521 us -> 148 us (0.28)
  waiting for transfers between devices: 296 us -> 30.3 us
  matrix products: 97 us -> 0 us
  Pallas kernels: 0 us -> 63 us
  blocking collectives: 74.2 us -> 24 us
  local copies, waits for them, and re-layouts: 29.8 us -> 9.98 us
  starting transfers between devices: 0.23 us -> 17.4 us
  between operations: 14.2 us -> 0.79 us
  other arithmetic: 8.19 us -> 2.54 us
    reduce_scatter x3 -> x0, waiting for transfers between devices: 208 us -> none  [the longest x1 87.5 us: shards(): lax.psum_scatter(query_sum, 'kv', scatter_dimension=0, tiled=True)]
    dot_general x40 -> x0, matrix products: 97 us -> none  [the longest x8 37.1 us: one_block(): jnp.einsum('tgc,tgd->cd', probs_low, grad_block, preferred_element_type=j...]
    all_gather x3 -> x0, waiting for transfers between devices: 84.6 us -> none  [the longest x1 50.7 us: shards(): lax.all_gather(output, 'kv', axis=0, tiled=True)]
    all_gather x3 -> x0, blocking collectives: 74.2 us -> none  [the longest x1 35.7 us: shards(): norm_all = lax.all_gather(log_norm, 'kv', axis=1, tiled=True)]
    pallas_call x0 -> x5, Pallas kernels: none -> 63 us  [the longest x1 56.7 us: main(): pl.pallas_call(main_kernel, out_shape=(jax.ShapeDtypeStruct((QRUNS, 1024,...]
    ppermute x0 -> x9, waiting for transfers between devices: none -> 29.2 us  [the longest x7 26.7 us: along_z(): return lax.ppermute(array, 'z', [(i, (i + step) % 4) for i in range(4)])]
    all_to_all x0 -> x1, blocking collectives: none -> 24 us  [shards(): kv_mine = lax.all_to_all(kv_out, PLANE, 0, 0, tiled=True)]
    ppermute x0 -> x9, starting transfers between devices: none -> 11.6 us  [the longest x7 11.3 us: along_z(): return lax.ppermute(array, 'z', [(i, (i + step) % 4) for i in range(4)])]
  transfers between devices with their start and end apart: 6 -> 10, of which waited for: 5 -> 7; matrix products, arithmetic and copies ran while one was open for 2% -> 2% of each run, Pallas kernels for 0% -> 3%
where the time goes in v1:
time: 148 us
  Pallas kernels  63 us (43%)
  waiting for transfers between devices  30.3 us (20%)
  blocking collectives  24 us (16%)
  starting transfers between devices  17.4 us (12%)
  local copies, waits for them, and re-layouts  9.98 us (7%)
  other arithmetic  2.54 us (2%)
    pallas_call x1, Pallas kernels, main(): pl.pallas_call(main_kernel, out_shape=(jax.ShapeDtypeStruct((QRUNS, 1024,...  56.7 us
    ppermute x7, waiting for transfers between devices, along_z(): return lax.ppermute(array, 'z', [(i, (i + step) % 4) for i in range(4)])  26.7 us
    all_to_all x1, blocking collectives, shards(): kv_mine = lax.all_to_all(kv_out, PLANE, 0, 0, tiled=True)  24 us
    ppermute x7, starting transfers between devices, along_z(): return lax.ppermute(array, 'z', [(i, (i + step) % 4) for i in range(4)])  11.3 us
    unnamed x26, local copies, waits for them, and re-layouts  5.74 us
    all_to_all x1, starting transfers between devices, shards(): dkv_parts = lax.all_to_all(dkv_sum, PLANE, 0, 0, tiled=True)  5.72 us
  transfers between devices with their start and end apart: 10, of which 7 were waited for; matrix products, arithmetic and copies ran while one was open for 2% of the time, Pallas kernels for 3%

profile of v1, /device:TPU:0, one launch (start us, length us, event | category | flops | bytes accessed | tf_op | source)
XLA Modules:
  0.0 148.0 jit_solution(11026872643638698775)
XLA Ops:
  0.7 0.8 constant_dynamic-slice_fusion
  1.4 0.0 copy-start.1
  1.4 0.9 copy-done.1
  2.4 0.0 copy-start.2
  2.4 0.9 copy-done.2
  3.3 0.0 copy-start.3
  3.3 0.9 copy-done.3
  4.3 0.0 copy-start.4
  4.3 0.8 copy-done.4
  5.0 0.0 copy-start.5
  5.0 0.8 copy-done.5
  5.8 0.0 copy-start.6
  5.8 0.7 copy-done.6
  6.5 0.8 prep.1
  7.3 0.0 copy-start
  7.3 24.0 %all_to_all.10.kva_ref = bf16[16,128,256]{2,1,0:T(8,128)(2,1)S(1)} all-to-all(bf16[16,128,256]{2,1,0:T(8,128)(2,1)S(1)} %get-tuple-element.11), channel_id=1, replica_groups=mesh['ylo'=2,'x'=4,'core'=2,'yhi'=2,'z'=4] {'yhi','ylo','x'}, dimensions={0} | all-to-all | bytes 2097152 | tf_op jit(solution)/shard_map/all_to_all | solution.py:285
  31.3 0.0 copy-start.7
  31.3 0.0 collective-permute-start.4
  31.3 4.1 %collective-permute-start.1 = (bf16[2112,128]{1,0:T(8,128)(2,1)S(1)}, bf16[2112,128]{1,0:T(8,128)(2,1)S(1)}, u32[]{:S(2)}, u32[]{:S(2)}) collective-permute-start(bf16[2112,128]{1,0:T(8,128)(2,1)S(1)} %get-tuple-element.10.a_ref), channel_id=1, source_target_pairs={{0,3},{1,0},{2,1},{3,2},{4,7},{5,4},{6,5},{7,6},{8,11},{9,8},{10,9... | collective-permute-start | bytes 1622024 | tf_op jit(solution)/shard_map/ppermute | solution.py:279
  35.4 0.0 copy-done
  35.4 0.0 collective-permute-start
  35.4 0.7 constant_dynamic-slice_fusion.3
  36.1 0.8 constant_dynamic-slice_fusion.4
  36.9 10.7 %collective-permute-done.1.l_ref = bf16[2112,128]{1,0:T(8,128)(2,1)S(1)} collective-permute-done((bf16[2112,128]{1,0:T(8,128)(2,1)S(1)}, bf16[2112,128]{1,0:T(8,128)(2,1)S(1)}, u32[]{:S(2)}, u32[]{:S(2)}) %collective-permute-start.1) | collective-permute-done | bytes 540704 | tf_op jit(solution)/shard_map/ppermute | solution.py:279
  47.6 0.0 copy-start.8
  47.6 3.8 %collective-permute-start.3 = (bf16[1056,128]{1,0:T(8,128)(2,1)S(1)}, bf16[1056,128]{1,0:T(8,128)(2,1)S(1)}, u32[]{:S(2)}, u32[]{:S(2)}) collective-permute-start(bf16[1056,128]{1,0:T(8,128)(2,1)S(1)} %slice.40), channel_id=1, source_target_pairs={{0,3},{1,0},{2,1},{3,2},{4,7},{5,4},{6,5},{7,6},{8,11},{9,8},{10,9... | collective-permute-start | bytes 811016 | tf_op jit(solution)/shard_map/ppermute | solution.py:279
  51.4 0.0 collective-permute-done.r_ref
  51.4 0.0 copy-start.9
  51.4 0.1 collective-permute-start.2
  51.5 1.8 %concatenate.8.pos_ref = s32[40,128]{1,0:T(8,128)} concatenate(s32[16,128]{1,0:T(8,128)S(1)} %bitcast.13, s32[16,128]{1,0:T(8,128)S(1)} %bitcast.12, s32[1,128]{1,0:T(1,128)S(1)} %get-tuple-element.26, s32[1,128]{1,0:T(1,128)S(1)} %get-tuple-element.25, s32[2,128]{1,0:T(2,128)S(1)} %slice.32, s32[1,128]{1,0:T(1,128)S(1)} %get-tuple-element.26, s32[1,128]{1,0:T(1,128)S(1)} %get-tuple-element.25, ...), dimensions={0} | concatenate | bytes 40960 | tf_op jit(solution)/shard_map/concatenate | solution.py:296
  53.4 2.8 %sort_runs.1.pos_ref = f32[40,128]{1,0:T(8,128)} custom-call(s32[40,128]{1,0:T(8,128)} %concatenate.8.pos_ref), custom_call_target="tpu_custom_call" | custom-call | tf_op jit(solution)/shard_map/sort_runs/pallas_call | solution.py:123
  56.2 0.8 collective-permute-done.3.og_ref
  57.0 0.0 copy-start.11
  57.0 3.5 %collective-permute-done.2.oq_ref = bf16[1056,128]{1,0:T(8,128)(2,1)S(1)} collective-permute-done((bf16[1056,128]{1,0:T(8,128)(2,1)S(1)}, bf16[1056,128]{1,0:T(8,128)(2,1)S(1)}, u32[]{:S(2)}, u32[]{:S(2)}) %collective-permute-start.2) | collective-permute-done | bytes 270368 | tf_op jit(solution)/shard_map/ppermute | solution.py:279
  60.5 0.0 copy-start.12
  60.5 0.0 collective-permute-done.4.kvb_ref
  60.5 0.0 copy-done.7
  60.5 0.0 copy-done.8
  60.5 0.0 copy-done.9
  60.5 0.0 copy-done.11
  60.6 0.7 copy-done.12
  61.2 56.7 %block_grads.1 = (bf16[4,1024,128]{2,1,0:T(8,128)(2,1)}, bf16[16,128,256]{2,1,0:T(8,128)(2,1)}, bf16[16,128,256]{2,1,0:T(8,128)(2,1)}) custom-call(f32[40,128]{1,0:T(8,128)} %sort_runs.1.pos_ref, bf16[2112,128]{1,0:T(8,128)(2,1)} %copy-done, bf16[2112,128]{1,0:T(8,128)(2,1)} %copy-done.9, bf16[2112,128]{1,0:T(8,128)(2,1)} %copy-done.8, ...), custom_call_target="tpu_custom_call" | custom-call | tf_op jit(solution)/shard_map/block_grads/pallas_call | solution.py:216
  117.9 0.4 collective-permute-start.8
  118.3 2.5 %collective-permute-done.8 = bf16[16,128,256]{2,1,0:T(8,128)(2,1)S(1)} collective-permute-done((bf16[16,128,256]{2,1,0:T(8,128)(2,1)}, bf16[16,128,256]{2,1,0:T(8,128)(2,1)S(1)}, u32[]{:S(2)}, u32[]{:S(2)}) %collective-permute-start.8) | collective-permute-done | bytes 1048608 | tf_op jit(solution)/shard_map/ppermute | solution.py:304
  120.8 2.5 %add_convert_fusion = bf16[16,128,256]{2,1,0:T(8,128)(2,1)} fusion(bf16[16,128,256]{2,1,0:T(8,128)(2,1)S(1)} %collective-permute-done.8, bf16[16,128,256]{2,1,0:T(8,128)(2,1)} %get-tuple-element.13), kind=kLoop, calls=%fused_computation | loop fusion | flops 2097152 | bytes 3145728 | tf_op jit(solution)/shard_map/convert_element_type | solution.py:305
  123.3 0.0 copy-start.10
  123.3 5.7 %all-to-all-start.1 = ((bf16[16,128,256]{2,1,0:T(8,128)(2,1)}), bf16[16,128,256]{2,1,0:T(8,128)(2,1)S(1)}, u32[]{:S(2)}, u32[]{:S(2)}) async-start(bf16[16,128,256]{2,1,0:T(8,128)(2,1)} %add_convert_fusion), calls=%async_computation.1 | async-start | bytes 2097152 | tf_op jit(solution)/shard_map/all_to_all | solution.py:306
  129.0 0.0 copy-done.10
  129.1 0.1 slice_bitcast_fusion
  129.1 0.1 collective-permute-start.7
  129.2 0.5 collective-permute-start.6
  129.7 2.8 %collective-permute-start.5 = (bf16[1024,128]{1,0:T(8,128)(2,1)S(1)}, bf16[1024,128]{1,0:T(8,128)(2,1)S(1)}, u32[]{:S(2)}, u32[]{:S(2)}) collective-permute-start(bf16[1024,128]{1,0:T(8,128)(2,1)S(1)} %get-tuple-element.19), channel_id=1, source_target_pairs={{0,3},{1,0},{2,1},{3,2},{4,7},{5,4},{6,5},{7,6},{8,11},{9,8},{10,9... | collective-permute-start | bytes 786440 | tf_op jit(solution)/shard_map/ppermute | solution.py:279
  132.5 7.4 %collective-permute-done.7.d_ref = bf16[1024,128]{1,0:T(8,128)(2,1)S(1)} collective-permute-done((bf16[1024,128]{1,0:T(8,128)(2,1)S(1)}, bf16[1024,128]{1,0:T(8,128)(2,1)S(1)}, u32[]{:S(2)}, u32[]{:S(2)}) %collective-permute-start.7) | collective-permute-done | bytes 262176 | tf_op jit(solution)/shard_map/ppermute | solution.py:279
  139.9 4.3 %collective-permute-done.6.c_ref = bf16[1024,128]{1,0:T(8,128)(2,1)S(1)} collective-permute-done((bf16[1024,128]{1,0:T(8,128)(2,1)S(1)}, bf16[1024,128]{1,0:T(8,128)(2,1)S(1)}, u32[]{:S(2)}, u32[]{:S(2)}) %collective-permute-start.6) | collective-permute-done | bytes 262176 | tf_op jit(solution)/shard_map/ppermute | solution.py:279
  144.2 0.0 collective-permute-done.5.b_ref
  144.2 1.6 %query_sum.1 = f32[128,1024]{1,0:T(8,128)} custom-call(bf16[1024,128]{1,0:T(8,128)(2,1)S(1)} %get-tuple-element.20.own_ref, bf16[1024,128]{1,0:T(8,128)(2,1)S(1)} %collective-permute-done.5.b_ref, bf16[1024,128]{1,0:T(8,128)(2,1)S(1)} %collective-permute-done.6.c_ref, bf16[1024,128]{1,0:T(8,128)(2,1)S(1)} %collective-permute-done.7.d_ref, ...), custom_call_target="tpu_custom_call" | custom-call | tf_op jit(solution)/shard_map/query_sum/pallas_call | solution.py:307
  145.8 1.1 all-to-all-done.1.parts_ref
  146.8 1.1 key_sum.1
  (6 shorter events, 0.1 us)
Async XLA Ops:
  1.4 0.9 copy-start.1
  2.4 0.9 copy-start.2
  3.3 0.9 copy-start.3
  4.3 0.8 copy-start.4
  5.0 0.8 copy-start.5
  5.8 0.7 copy-start.6
  7.3 28.1 %copy-start = (bf16[2112,128]{1,0:T(8,128)(2,1)}, bf16[2112,128]{1,0:T(8,128)(2,1)S(1)}, u32[]{:S(2)}) copy-start(bf16[2112,128]{1,0:T(8,128)(2,1)S(1)} %get-tuple-element.10.a_ref) | copy-start | bytes 1622020
  31.3 29.2 %copy-start.7 = (bf16[16,128,256]{2,1,0:T(8,128)(2,1)}, bf16[16,128,256]{2,1,0:T(8,128)(2,1)S(1)}, u32[]{:S(2)}) copy-start(bf16[16,128,256]{2,1,0:T(8,128)(2,1)S(1)} %all_to_all.10.kva_ref) | copy-start | bytes 3145732
  31.3 29.2 %collective-permute-start.4 = (bf16[16,128,256]{2,1,0:T(8,128)(2,1)S(1)}, bf16[16,128,256]{2,1,0:T(8,128)(2,1)}, u32[]{:S(2)}, u32[]{:S(2)}) collective-permute-start(bf16[16,128,256]{2,1,0:T(8,128)(2,1)S(1)} %all_to_all.10.kva_ref), channel_id=1, source_target_pairs={{0,8},{8,0},{1,9},{9,1},{2,10},{10,2},{3,11},{11,3},{4,12},{12,4},... | collective-permute-start | bytes 3145736 | tf_op jit(solution)/shard_map/ppermute | solution.py:286
  31.3 16.3 %collective-permute-start.1 = (bf16[2112,128]{1,0:T(8,128)(2,1)S(1)}, bf16[2112,128]{1,0:T(8,128)(2,1)S(1)}, u32[]{:S(2)}, u32[]{:S(2)}) collective-permute-start(bf16[2112,128]{1,0:T(8,128)(2,1)S(1)} %get-tuple-element.10.a_ref), channel_id=1, source_target_pairs={{0,3},{1,0},{2,1},{3,2},{4,7},{5,4},{6,5},{7,6},{8,11},{9,8},{10,9... | collective-permute-start | bytes 1622024 | tf_op jit(solution)/shard_map/ppermute | solution.py:279
  35.4 16.0 %collective-permute-start = (bf16[2112,128]{1,0:T(8,128)(2,1)S(1)}, bf16[2112,128]{1,0:T(8,128)(2,1)S(1)}, u32[]{:S(2)}, u32[]{:S(2)}) collective-permute-start(bf16[2112,128]{1,0:T(8,128)(2,1)S(1)} %get-tuple-element.10.a_ref), channel_id=1, source_target_pairs={{0,1},{1,2},{2,3},{3,0},{4,5},{5,6},{6,7},{7,4},{8,9},{9,10},{10,1... | collective-permute-start | bytes 1622024 | tf_op jit(solution)/shard_map/ppermute | solution.py:279
  47.6 12.9 %copy-start.8 = (bf16[2112,128]{1,0:T(8,128)(2,1)}, bf16[2112,128]{1,0:T(8,128)(2,1)S(1)}, u32[]{:S(2)}) copy-start(bf16[2112,128]{1,0:T(8,128)(2,1)S(1)} %collective-permute-done.1.l_ref) | copy-start | bytes 1622020
  47.6 9.4 %collective-permute-start.3 = (bf16[1056,128]{1,0:T(8,128)(2,1)S(1)}, bf16[1056,128]{1,0:T(8,128)(2,1)S(1)}, u32[]{:S(2)}, u32[]{:S(2)}) collective-permute-start(bf16[1056,128]{1,0:T(8,128)(2,1)S(1)} %slice.40), channel_id=1, source_target_pairs={{0,3},{1,0},{2,1},{3,2},{4,7},{5,4},{6,5},{7,6},{8,11},{9,8},{10,9... | collective-permute-start | bytes 811016 | tf_op jit(solution)/shard_map/ppermute | solution.py:279
  51.4 9.2 %copy-start.9 = (bf16[2112,128]{1,0:T(8,128)(2,1)}, bf16[2112,128]{1,0:T(8,128)(2,1)S(1)}, u32[]{:S(2)}) copy-start(bf16[2112,128]{1,0:T(8,128)(2,1)S(1)} %collective-permute-done.r_ref) | copy-start | bytes 1622020
  51.4 9.1 %collective-permute-start.2 = (bf16[1056,128]{1,0:T(8,128)(2,1)S(1)}, bf16[1056,128]{1,0:T(8,128)(2,1)S(1)}, u32[]{:S(2)}, u32[]{:S(2)}) collective-permute-start(bf16[1056,128]{1,0:T(8,128)(2,1)S(1)} %slice.39), channel_id=1, source_target_pairs={{0,1},{1,2},{2,3},{3,0},{4,5},{5,6},{6,7},{7,4},{8,9},{9,10},{10,1... | collective-permute-start | bytes 811016 | tf_op jit(solution)/shard_map/ppermute | solution.py:279
  57.0 3.5 %copy-start.11 = (bf16[1056,128]{1,0:T(8,128)(2,1)}, bf16[1056,128]{1,0:T(8,128)(2,1)S(1)}, u32[]{:S(2)}) copy-start(bf16[1056,128]{1,0:T(8,128)(2,1)S(1)} %collective-permute-done.3.og_ref) | copy-start | bytes 811012
  60.5 0.7 copy-start.12
  117.9 2.9 %collective-permute-start.8 = (bf16[16,128,256]{2,1,0:T(8,128)(2,1)}, bf16[16,128,256]{2,1,0:T(8,128)(2,1)S(1)}, u32[]{:S(2)}, u32[]{:S(2)}) collective-permute-start(bf16[16,128,256]{2,1,0:T(8,128)(2,1)} %get-tuple-element.14), channel_id=1, source_target_pairs={{0,8},{8,0},{1,9},{9,1},{2,10},{10,2},{3,11},{11,3},{4,12},{12,4},... | collective-permute-start | bytes 3145736 | tf_op jit(solution)/shard_map/ppermute | solution.py:304
  123.3 5.7 %copy-start.10 = (bf16[4,1024,128]{2,1,0:T(8,128)(2,1)S(1)}, bf16[4,1024,128]{2,1,0:T(8,128)(2,1)}, u32[]{:S(2)}) copy-start(bf16[4,1024,128]{2,1,0:T(8,128)(2,1)} %get-tuple-element.12) | copy-start | bytes 3145732
  123.3 23.5 %all-to-all-start.1 = ((bf16[16,128,256]{2,1,0:T(8,128)(2,1)}), bf16[16,128,256]{2,1,0:T(8,128)(2,1)S(1)}, u32[]{:S(2)}, u32[]{:S(2)}) async-start(bf16[16,128,256]{2,1,0:T(8,128)(2,1)} %add_convert_fusion), calls=%async_computation.1 | async-start | bytes 2097152 | tf_op jit(solution)/shard_map/all_to_all | solution.py:306
  129.1 10.8 %collective-permute-start.7 = (bf16[1024,128]{1,0:T(8,128)(2,1)S(1)}, bf16[1024,128]{1,0:T(8,128)(2,1)S(1)}, u32[]{:S(2)}, u32[]{:S(2)}) collective-permute-start(bf16[1024,128]{1,0:T(8,128)(2,1)S(1)} %get-tuple-element.17), channel_id=1, source_target_pairs={{0,2},{1,3},{2,0},{3,1},{4,6},{5,7},{6,4},{7,5},{8,10},{9,11},{10,... | collective-permute-start | bytes 786440 | tf_op jit(solution)/shard_map/ppermute | solution.py:279
  129.2 15.0 %collective-permute-start.6 = (bf16[1024,128]{1,0:T(8,128)(2,1)S(1)}, bf16[1024,128]{1,0:T(8,128)(2,1)S(1)}, u32[]{:S(2)}, u32[]{:S(2)}) collective-permute-start(bf16[1024,128]{1,0:T(8,128)(2,1)S(1)} %get-tuple-element.18), channel_id=1, source_target_pairs={{0,1},{1,2},{2,3},{3,0},{4,5},{5,6},{6,7},{7,4},{8,9},{9,10},{10,1... | collective-permute-start | bytes 786440 | tf_op jit(solution)/shard_map/ppermute | solution.py:279
  129.7 14.5 %collective-permute-start.5 = (bf16[1024,128]{1,0:T(8,128)(2,1)S(1)}, bf16[1024,128]{1,0:T(8,128)(2,1)S(1)}, u32[]{:S(2)}, u32[]{:S(2)}) collective-permute-start(bf16[1024,128]{1,0:T(8,128)(2,1)S(1)} %get-tuple-element.19), channel_id=1, source_target_pairs={{0,3},{1,0},{2,1},{3,2},{4,7},{5,4},{6,5},{7,6},{8,11},{9,8},{10,9... | collective-permute-start | bytes 786440 | tf_op jit(solution)/shard_map/ppermute | solution.py:279

commit v2 on v1

v2 whole, which is shorter than its diff:
```python
import math

import jax
import jax.numpy as jnp
from jax import lax
from jax.experimental import pallas as pl
from jax.experimental.pallas import tpu as pltpu
from jax.sharding import Mesh, PartitionSpec as P

AXES = ("ylo", "x", "core", "yhi", "z")
SIZES = (2, 4, 2, 2, 4)
PLANE = ("yhi", "ylo", "x")
HEADS = 8
WIDTH = 128
RUN = 128
BAND = 16
BANDS = RUN // BAND
QRUNS = 8
KRUNS = 16
QROWS = QRUNS * BAND * HEADS
KROWS = KRUNS * BAND
MERGE = 4
PART = 256
PCOL = 256
HALF = 1024 + 32
LOG2E = math.log2(math.e)
INV_ROOT = 1.0 / math.sqrt(WIDTH)
F32 = jnp.float32
BF16 = jnp.bfloat16
HIGH = lax.Precision.HIGHEST


def rank_matrices(pos_row):
    by_lane = jnp.broadcast_to(pos_row, (RUN, RUN))
    by_row = by_lane.T
    rank_lane = jnp.sum((by_row < by_lane).astype(F32), axis=0, keepdims=True)
    row_id = lax.broadcasted_iota(jnp.int32, (RUN, RUN), 0).astype(F32)
    place = (rank_lane == row_id).astype(F32)
    return place, rank_lane


def split3(x):
    hi = x.astype(BF16)
    rest = x - hi.astype(F32)
    mid = rest.astype(BF16)
    low = (rest - mid.astype(F32)).astype(BF16)
    return hi, mid, low


def pack_rows(values, place, rank_lane):
    ordered = lax.dot_general(
        values, place, (((1,), (1,)), ((), ())), precision=HIGH, preferred_element_type=F32
    )
    pieces = []
    for band in range(BANDS):
        row = jnp.concatenate(
            [ordered[h : h + 1, band * BAND : (band + 1) * BAND] for h in range(HEADS)], axis=1
        )
        pieces.append(row)
    return jnp.concatenate(pieces, axis=0)


def placed(index):
    ylo, x, core, yhi, z = index
    pb = (ylo * 4 + x) * 2 + core
    return pb * 8 + yhi * 4 + z, (yhi * 4 + z) * 16 + pb


def own_index():
    return tuple(lax.axis_index(name) for name in AXES)


def prep_kernel(
    q_hbm, g_hbm, o_hbm, ln_hbm, k_hbm, v_hbm, pos_hbm, pay_ref, kv_ref,
    q_ref, g_ref, o_ref, ln_ref, k_ref, v_ref, pos_ref, sems,
):
    copies = [
        pltpu.make_async_copy(src, dst, sems.at[i])
        for i, (src, dst) in enumerate((
            (pos_hbm, pos_ref), (k_hbm, k_ref), (v_hbm, v_ref), (q_hbm, q_ref),
            (g_hbm, g_ref), (o_hbm, o_ref), (ln_hbm, ln_ref),
        ))
    ]
    for copy in copies:
        copy.start()
    for copy in copies:
        copy.wait()
    q_block, k_block = placed(own_index())
    place_q, rank_q = rank_matrices(pos_ref[pl.ds(q_block, 1), :].astype(F32))
    place_k, _ = rank_matrices(pos_ref[pl.ds(k_block, 1), :].astype(F32))
    low_q = place_q.astype(BF16)
    low_k = place_k.astype(BF16)
    q_sorted = jnp.dot(low_q, q_ref[...], preferred_element_type=F32).astype(BF16)
    g_sorted = jnp.dot(low_q, g_ref[...], preferred_element_type=F32).astype(BF16)
    for h in range(HEADS):
        for band in range(BANDS):
            at = (band * HEADS + h) * BAND
            rows = slice(band * BAND, (band + 1) * BAND)
            cols = slice(h * WIDTH, (h + 1) * WIDTH)
            pay_ref[at : at + BAND, :] = q_sorted[rows, cols]
            pay_ref[HALF + at : HALF + at + BAND, :] = g_sorted[rows, cols]
    product = g_ref[...].astype(F32) * o_ref[...].astype(F32)
    columns = [
        jnp.sum(product[:, h * WIDTH : (h + 1) * WIDTH], axis=1, keepdims=True)
        for h in range(HEADS)
    ]
    lane_id = lax.broadcasted_iota(jnp.int32, (RUN, RUN), 1)
    delta_wide = jnp.zeros((RUN, RUN), F32)
    for h in range(HEADS):
        delta_wide = jnp.where(lane_id == h, columns[h], delta_wide)
    delta = delta_wide.T[:HEADS]
    fill = jnp.zeros((BANDS, RUN), BF16)
    ln_hi, ln_mid, ln_low = split3(pack_rows(ln_ref[...] * (-1.0 / INV_ROOT), place_q, rank_q))
    pay_ref[1024:1056, :] = jnp.concatenate([ln_hi, ln_mid, ln_low, fill], axis=0)
    d_hi, d_mid, d_low = split3(pack_rows(-delta, place_q, rank_q))
    pay_ref[HALF + 1024 : HALF + 1056, :] = jnp.concatenate([d_hi, d_mid, d_low, fill], axis=0)
    k_sorted = jnp.dot(low_k, k_ref[...], preferred_element_type=F32).astype(BF16)
    v_sorted = jnp.dot(low_k, v_ref[...], preferred_element_type=F32).astype(BF16)
    kv = jnp.concatenate([k_sorted, v_sorted], axis=1)
    for i in range(16):
        kv_ref[i] = kv


def prep(q, g, o, ln, k, v, pos):
    return pl.pallas_call(
        prep_kernel,
        in_specs=[pl.BlockSpec(memory_space=pl.ANY)] * 7,
        out_shape=(
            jax.ShapeDtypeStruct((2 * HALF, WIDTH), BF16),
            jax.ShapeDtypeStruct((16, RUN, 2 * WIDTH), BF16),
        ),
        scratch_shapes=[
            pltpu.VMEM((RUN, HEADS * WIDTH), BF16),
            pltpu.VMEM((RUN, HEADS * WIDTH), BF16),
            pltpu.VMEM((RUN, HEADS * WIDTH), BF16),
            pltpu.VMEM((HEADS, RUN), F32),
            pltpu.VMEM((RUN, WIDTH), BF16),
            pltpu.VMEM((RUN, WIDTH), BF16),
            pltpu.VMEM((128, RUN), jnp.int32),
            pltpu.SemaphoreType.DMA((7,)),
        ],
        compiler_params=pltpu.CompilerParams(vmem_limit_bytes=60 * 1024 * 1024),
        name="prep",
    )(q, g, o, ln, k, v, pos)


def sorted_kernel(pos_ref, out_ref):
    ylo, x, core, yhi, z = own_index()
    rows = []
    for key_yhi in range(2):
        for key_ylo in range(2):
            for key_x in range(4):
                rows.append(placed((key_ylo, key_x, core, key_yhi, z))[1])
    for query_core in (core, 1 - core):
        for query_z in (z, (z + 3) % 4, (z + 1) % 4, (z + 2) % 4):
            rows.append(placed((ylo, x, query_core, yhi, query_z))[0])
    pos = jnp.concatenate([pos_ref[pl.ds(row, 1), :] for row in rows], axis=0).astype(F32)
    rank = jnp.zeros_like(pos)
    for s in range(1, RUN):
        rank = rank + (pltpu.roll(pos, s, 1) < pos).astype(F32)
    lane = lax.broadcasted_iota(jnp.int32, pos.shape, 1).astype(F32)
    ordered = jnp.where(rank == lane, pos, 0.0)
    for s in range(1, RUN):
        ordered = ordered + jnp.where(
            pltpu.roll(rank, s, 1) == lane, pltpu.roll(pos, s, 1), 0.0
        )
    out_ref[...] = ordered


def sort_runs(pos):
    return pl.pallas_call(
        sorted_kernel,
        out_shape=jax.ShapeDtypeStruct((KRUNS + QRUNS, RUN), F32),
        name="sort_runs",
    )(pos)


def main_kernel(*refs):
    pos_ref, spos = refs[:2]
    runs = refs[2:10]
    kv_ref = refs[10]
    dq_near, dq_own, dq_other, dkv_ref = refs[11:15]
    qpt, kps, dqs, dks, dvs, tx, kx, vx = refs[15:]
    for run, pay in enumerate(runs):
        terms = jnp.concatenate(
            [
                pay[1024:1056, :].astype(F32),
                pay[HALF + 1024 : HALF + 1056, :].astype(F32),
                jnp.zeros((RUN - 64, RUN), F32),
            ],
            axis=0,
        )
        tx[run * RUN : (run + 1) * RUN, :] = terms.T.astype(BF16)
    query_pos = pos_ref[KRUNS : KRUNS + QRUNS, :].T
    lane = lax.broadcasted_iota(jnp.int32, (BAND, WIDTH), 1)
    for band in range(BANDS):
        rows = slice(band * BAND, (band + 1) * BAND)
        kx[band] = ((lane % 8 == band) & (lane < 24)).astype(F32).astype(BF16)
        vx[band] = ((lane % 8 == band) & (lane >= 32) & (lane < 56)).astype(F32).astype(BF16)
        for run in range(QRUNS):
            qpt[band, run * BAND : (run + 1) * BAND, :] = jnp.broadcast_to(
                query_pos[rows, run : run + 1], (BAND, WIDTH)
            )
        kps[band : band + 1, :] = jnp.concatenate(
            [pos_ref[run : run + 1, rows] for run in range(KRUNS)], axis=1
        )
    dks[...] = jnp.zeros_like(dks)
    dvs[...] = jnp.zeros_like(dvs)
    by_cols = (((1,), (1,)), ((), ()))
    by_rows = (((0,), (0,)), ((), ()))

    def block(u, first, bands):
        at = pl.ds(pl.multiple_of(u * RUN, RUN), RUN)
        g_at = pl.ds(pl.multiple_of(HALF + u * RUN, 16), RUN)
        q = jnp.concatenate([pay[at, :] for pay in runs], axis=0)
        g = jnp.concatenate([pay[g_at, :] for pay in runs], axis=0)
        terms = tx[...]
        rows = [
            pl.ds(pl.multiple_of((first + i) * BAND, BAND), BAND) for i in range(bands)
        ]
        key = jnp.concatenate(
            [kv_ref[run, r, :WIDTH] for r in rows for run in range(KRUNS)], axis=0
        )
        value = jnp.concatenate(
            [kv_ref[run, r, WIDTH:] for r in rows for run in range(KRUNS)], axis=0
        )
        key_pick = jnp.concatenate([kx[u]] * (KRUNS * bands), axis=0)
        value_pick = jnp.concatenate([vx[u]] * (KRUNS * bands), axis=0)
        q_terms = jnp.concatenate([q, terms], axis=1)
        g_terms = jnp.concatenate([g, terms], axis=1)
        key_terms = jnp.concatenate([key, key_pick], axis=1)
        value_terms = jnp.concatenate([value, value_pick], axis=1)
        wide = KROWS * bands
        key_pos = jnp.concatenate([kps[pl.ds(first + i, 1), :] for i in range(bands)], axis=1)
        probs_low, grads_low = [], []
        for part in range(QROWS // PART):
            mine = slice(part * PART, (part + 1) * PART)
            lows = []
            for c in range(0, wide, PCOL):
                cs = slice(c, c + PCOL)
                scores = lax.dot_general(
                    q_terms[mine], key_terms[cs], by_cols, preferred_element_type=F32
                )
                grad_probs = lax.dot_general(
                    g_terms[mine], value_terms[cs], by_cols, preferred_element_type=F32
                )
                column = jnp.concatenate(
                    [
                        qpt[u, run * BAND : (run + 1) * BAND, :]
                        for run in range(part * PART // RUN, ((part + 1) * PART + RUN - 1) // RUN)
                        for _ in range(min(PART, RUN) // BAND)
                    ],
                    axis=0,
                )
                visible = key_pos[:, cs] <= jnp.concatenate([column] * (PCOL // WIDTH), axis=1)
                probs = jnp.where(visible, jnp.exp2(scores * (INV_ROOT * LOG2E)), 0.0)
                lows.append((probs.astype(BF16), (probs * grad_probs).astype(BF16)))
            probs_low.append(jnp.concatenate([x[0] for x in lows], axis=1))
            grads_low.append(jnp.concatenate([x[1] for x in lows], axis=1))
        probs_low = jnp.concatenate(probs_low, axis=0)
        grad_scores = jnp.concatenate(grads_low, axis=0)
        dv = lax.dot_general(g, probs_low, by_rows, preferred_element_type=F32)
        dk = lax.dot_general(q, grad_scores, by_rows, preferred_element_type=F32)
        for i in range(bands):
            cols = slice(i * KROWS, (i + 1) * KROWS)
            dvs[first + i] += dv[:, cols]
            dks[first + i] += dk[:, cols]
        dqs[...] += jnp.dot(grad_scores, key, preferred_element_type=F32)

    def query_band(u, carry):
        last = spos[KRUNS, u * BAND + BAND - 1]
        for run in range(1, QRUNS):
            last = jnp.maximum(last, spos[KRUNS + run, u * BAND + BAND - 1])
        seen = 0
        for t in range(BANDS):
            first = spos[0, t * BAND]
            for run in range(1, KRUNS):
                first = jnp.minimum(first, spos[run, t * BAND])
            seen = seen + jnp.where(last >= first, 1, 0)
        dqs[...] = jnp.zeros_like(dqs)
        done = lax.div(seen, MERGE) * MERGE

        def many(j, carry):
            block(u, j * MERGE, MERGE)
            return carry

        lax.fori_loop(0, lax.div(seen, MERGE), many, 0)

        def single(j, carry):
            block(u, j, 1)
            return carry

        lax.fori_loop(done, seen, single, 0)
        rows = pl.ds(pl.multiple_of(u * RUN, RUN), RUN)
        dq_near[rows, :] = dqs[0:RUN, :] * INV_ROOT
        for run in range(1, 4):
            dq_own[run - 1, rows, :] = dqs[run * RUN : (run + 1) * RUN, :] * INV_ROOT
        for run in range(4):
            dq_other[run, rows, :] = (
                dqs[(4 + run) * RUN : (5 + run) * RUN, :] * INV_ROOT
            ).astype(BF16)
        return carry

    lax.fori_loop(0, BANDS, query_band, 0)
    for band in range(BANDS):
        rows = slice(band * BAND, (band + 1) * BAND)
        key_part = (dks[band] * INV_ROOT).T.astype(BF16)
        value_part = dvs[band].T.astype(BF16)
        for run in range(KRUNS):
            dkv_ref[run, rows, :WIDTH] = key_part[run * BAND : (run + 1) * BAND]
            dkv_ref[run, rows, WIDTH:] = value_part[run * BAND : (run + 1) * BAND]


def main(runs, payloads, kv):
    vmem = pl.BlockSpec(memory_space=pltpu.VMEM)
    return pl.pallas_call(
        main_kernel,
        in_specs=[vmem, pl.BlockSpec(memory_space=pltpu.SMEM)] + [vmem] * 9,
        out_shape=(
            jax.ShapeDtypeStruct((1024, WIDTH), F32),
            jax.ShapeDtypeStruct((3, 1024, WIDTH), F32),
            jax.ShapeDtypeStruct((4, 1024, WIDTH), BF16),
            jax.ShapeDtypeStruct((16, RUN, 2 * WIDTH), BF16),
        ),
        scratch_shapes=[
            pltpu.VMEM((BANDS, QRUNS * BAND, WIDTH), F32),
            pltpu.VMEM((BANDS, KROWS), F32),
            pltpu.VMEM((QROWS, WIDTH), F32),
            pltpu.VMEM((BANDS, WIDTH, KROWS), F32),
            pltpu.VMEM((BANDS, WIDTH, KROWS), F32),
            pltpu.VMEM((QROWS, WIDTH), BF16),
            pltpu.VMEM((BANDS, BAND, WIDTH), BF16),
            pltpu.VMEM((BANDS, BAND, WIDTH), BF16),
        ],
        compiler_params=pltpu.CompilerParams(vmem_limit_bytes=56 * 1024 * 1024),
        name="block_grads",
    )(runs, runs, *payloads, kv)


def query_kernel(own_ref, in_ref, b_ref, c_ref, d_ref, pos_ref, out_ref):
    q_block, _ = placed(own_index())
    place, _ = rank_matrices(pos_ref[pl.ds(q_block, 1), :].astype(F32))
    total = own_ref[...] + in_ref[0].astype(F32)
    for ref in (b_ref, c_ref, d_ref):
        total = total + ref[...].astype(F32)
    total = total.reshape(BANDS, HEADS, BAND, WIDTH)
    for h in range(HEADS):
        out_ref[:, h * WIDTH : (h + 1) * WIDTH] = lax.dot_general(
            place, total[:, h].reshape(RUN, WIDTH), (((0,), (0,)), ((), ())),
            precision=HIGH, preferred_element_type=F32,
        )


def key_kernel(parts_ref, pos_ref, dk_ref, dv_ref):
    _, k_block = placed(own_index())
    place, _ = rank_matrices(pos_ref[pl.ds(k_block, 1), :].astype(F32))
    total = parts_ref[0].astype(F32)
    for i in range(1, 16):
        total = total + parts_ref[i].astype(F32)
    result = lax.dot_general(
        place, total, (((0,), (0,)), ((), ())), precision=HIGH, preferred_element_type=F32
    )
    dk_ref[...] = result[:, :WIDTH]
    dv_ref[...] = result[:, WIDTH:]


def shards(queries, key_rows, value_rows, output, out_grad, log_norm, positions):
    pos = positions.reshape(128, RUN)
    payload, kv_out = prep(queries, out_grad, output, log_norm, key_rows, value_rows, pos)

    def along_z(array, step):
        return lax.ppermute(array, "z", [(i, (i + step) % 4) for i in range(4)])

    def cross(array):
        return lax.ppermute(array, "core", [(0, 1), (1, 0)])

    from_left = along_z(payload, 1)
    from_right = along_z(payload, 3)
    from_far = along_z(payload, 2)
    mine = (payload, from_left, from_right, from_far)
    payloads = mine + tuple(cross(array) for array in mine)
    kv = lax.all_to_all(kv_out, PLANE, 0, 0, tiled=True)
    dq_near, dq_own, dq_other, dkv = main(sort_runs(pos), payloads, kv)
    dkv_parts = lax.all_to_all(dkv, PLANE, 0, 0, tiled=True)
    dq_in = cross(dq_other)
    dq_sum = (dq_own + dq_in[1:].astype(F32)).astype(BF16)
    dq_left = along_z(dq_sum[0], 3)
    dq_right = along_z(dq_sum[1], 1)
    dq_far = along_z(dq_sum[2], 2)
    query_grad = pl.pallas_call(
        query_kernel, out_shape=jax.ShapeDtypeStruct((RUN, HEADS * WIDTH), F32), name="query_sum",
        compiler_params=pltpu.CompilerParams(vmem_limit_bytes=32 * 1024 * 1024),
    )(dq_near, dq_in, dq_left, dq_right, dq_far, pos)
    key_grad, value_grad = pl.pallas_call(
        key_kernel,
        out_shape=(
            jax.ShapeDtypeStruct((RUN, WIDTH), F32),
            jax.ShapeDtypeStruct((RUN, WIDTH), F32),
        ),
        name="key_sum",
        compiler_params=pltpu.CompilerParams(vmem_limit_bytes=32 * 1024 * 1024),
    )(dkv_parts, pos)
    return query_grad, key_grad, value_grad


def solution(mesh):
    fine = Mesh(mesh.devices.reshape(SIZES), AXES)
    by_query = P(AXES, None)
    by_key = P(("yhi", "z", "ylo", "x", "core"), None)
    return jax.shard_map(
        shards,
        mesh=fine,
        in_specs=(by_query, by_key, by_key, by_query, by_query, P(None, AXES), P()),
        out_specs=(by_query, by_key, by_key),
        check_vma=False,
    )
```

time: 148 us -> 104 us (0.70)
  blocking collectives: 24 us -> 0 us
  Pallas kernels: 63 us -> 45.2 us
  starting transfers between devices: 17.4 us -> 27.2 us
  local copies, waits for them, and re-layouts: 9.98 us -> 1.85 us
  waiting for transfers between devices: 30.3 us -> 27 us
    all_to_all x1 -> x0, blocking collectives: 24 us -> none  [shards(): kv_mine = lax.all_to_all(kv_out, PLANE, 0, 0, tiled=True)]
    pallas_call x3, Pallas kernels: 60.3 us -> 42.5 us  [the longest x1 37 us: main(): pl.pallas_call(main_kernel, in_specs=[vmem, pl.BlockSpec(memory_space=plt...]
    ppermute x7 -> x6, waiting for transfers between devices: 26.7 us -> 15.7 us  [along_z(): return lax.ppermute(array, 'z', [(i, (i + step) % 4) for i in range(4)])]
    all_to_all x1 -> x2, waiting for transfers between devices: 1.09 us -> 11.3 us  [the longest x1 11.3 us: shards(): dkv_parts = lax.all_to_all(dkv, PLANE, 0, 0, tiled=True)]
    all_to_all x1 -> x2, starting transfers between devices: 5.72 us -> 15.5 us  [the longest x1 8.47 us: shards(): dkv_parts = lax.all_to_all(dkv, PLANE, 0, 0, tiled=True)]
    unnamed x26 -> x14, local copies, waits for them, and re-layouts: 5.74 us -> 0.95 us
    ppermute x2 -> x5, waiting for transfers between devices: 2.52 us -> 0.01 us  [cross(): return lax.ppermute(array, 'core', [(0, 1), (1, 0)])]
    dynamic_slice x4 -> x0, local copies, waits for them, and re-layouts: 2.3 us -> none  [the longest x1 0.82 us: shards(): lax.dynamic_slice_in_dim(plane, 1 - core, 1, axis=3).reshape(16, RUN)]
  transfers between devices with their start and end apart: 10 -> 13, of which waited for: 7 -> 3; matrix products, arithmetic and copies ran while one was open for 2% -> 2% of each run, Pallas kernels for 3% -> 3%
where the time goes in v2:
time: 104 us
  Pallas kernels  45.2 us (43%)
  starting transfers between devices  27.2 us (26%)
  waiting for transfers between devices  27 us (26%)
  local copies, waits for them, and re-layouts  1.85 us (2%)
  other arithmetic  1.56 us (2%)
    pallas_call x1, Pallas kernels, main(): pl.pallas_call(main_kernel, in_specs=[vmem, pl.BlockSpec(memory_space=plt...  37 us
    ppermute x6, waiting for transfers between devices, along_z(): return lax.ppermute(array, 'z', [(i, (i + step) % 4) for i in range(4)])  15.7 us
    all_to_all x1, waiting for transfers between devices, shards(): dkv_parts = lax.all_to_all(dkv, PLANE, 0, 0, tiled=True)  11.3 us
    ppermute x6, starting transfers between devices, along_z(): return lax.ppermute(array, 'z', [(i, (i + step) % 4) for i in range(4)])  11 us
    all_to_all x1, starting transfers between devices, shards(): dkv_parts = lax.all_to_all(dkv, PLANE, 0, 0, tiled=True)  8.47 us
    all_to_all x1, starting transfers between devices, shards(): kv = lax.all_to_all(kv_out, PLANE, 0, 0, tiled=True)  7.03 us
    pallas_call x1, Pallas kernels, prep(): pl.pallas_call(prep_kernel, in_specs=[pl.BlockSpec(memory_space=pl.ANY)]...  3.14 us
    pallas_call x1, Pallas kernels, sort_runs(): pl.pallas_call(sorted_kernel, out_shape=jax.ShapeDtypeStruct((KRUNS + QRU...  2.39 us
  transfers between devices with their start and end apart: 13, of which 3 were waited for; matrix products, arithmetic and copies ran while one was open for 2% of the time, Pallas kernels for 3%

profile of v2, /device:TPU:0, one launch (start us, length us, event | category | flops | bytes accessed | tf_op | source)
XLA Modules:
  0.0 103.6 jit_solution(16492701155605012546)
XLA Ops:
  0.6 3.1 %prep.1 = (bf16[2112,128]{1,0:T(8,128)(2,1)}, bf16[16,128,256]{2,1,0:T(8,128)(2,1)}) custom-call(bf16[128,1024]{1,0:T(8,128)(2,1)} %q_hbm.1, bf16[128,1024]{1,0:T(8,128)(2,1)} %g_hbm.1, bf16[128,1024]{1,0:T(8,128)(2,1)} %o_hbm.1, f32[8,128]{1,0:T(8,128)} %ln_hbm.1, bf16[128,128]{1,0:T(8,128)(2,1)} %k_hbm.1, bf16[128,128]{1,0:T(8,128)(2,1)} %v_hbm.1, ...), custom_call_target="tpu_custom_call" | custom-call | tf_op jit(solution)/shard_map/prep/pallas_call | solution.py:125
  3.8 0.0 copy-start.3
  3.8 4.0 %collective-permute-start.2 = (bf16[2112,128]{1,0:T(8,128)(2,1)}, bf16[2112,128]{1,0:T(8,128)(2,1)S(1)}, u32[]{:S(2)}, u32[]{:S(2)}) collective-permute-start(bf16[2112,128]{1,0:T(8,128)(2,1)} %get-tuple-element.11.refs_2_), channel_id=1, source_target_pairs={{0,2},{1,3},{2,0},{3,1},{4,6},{5,7},{6,4},{7,5},{8,10},{9,11},{10,... | collective-permute-start | bytes 1622024 | tf_op jit(solution)/shard_map/ppermute | solution.py:372
  7.8 0.7 collective-permute-start.1
  8.5 1.3 %collective-permute-start = (bf16[2112,128]{1,0:T(8,128)(2,1)}, bf16[2112,128]{1,0:T(8,128)(2,1)S(1)}, u32[]{:S(2)}, u32[]{:S(2)}) collective-permute-start(bf16[2112,128]{1,0:T(8,128)(2,1)} %get-tuple-element.11.refs_2_), channel_id=1, source_target_pairs={{0,1},{1,2},{2,3},{3,0},{4,5},{5,6},{6,7},{7,4},{8,9},{9,10},{10,1... | collective-permute-start | bytes 1622024 | tf_op jit(solution)/shard_map/ppermute | solution.py:372
  9.9 7.0 %all-to-all-start = ((bf16[16,128,256]{2,1,0:T(8,128)(2,1)}), bf16[16,128,256]{2,1,0:T(8,128)(2,1)S(1)}, u32[]{:S(2)}, u32[]{:S(2)}) async-start(bf16[16,128,256]{2,1,0:T(8,128)(2,1)} %get-tuple-element.12), calls=%async_computation | async-start | bytes 2097152 | tf_op jit(solution)/shard_map/all_to_all | solution.py:382
  16.9 0.0 copy-done.3
  16.9 0.1 collective-permute-start.3
  17.0 4.2 %collective-permute-done.2.refs_5_ = bf16[2112,128]{1,0:T(8,128)(2,1)S(1)} collective-permute-done((bf16[2112,128]{1,0:T(8,128)(2,1)}, bf16[2112,128]{1,0:T(8,128)(2,1)S(1)}, u32[]{:S(2)}, u32[]{:S(2)}) %collective-permute-start.2) | collective-permute-done | bytes 540704 | tf_op jit(solution)/shard_map/ppermute | solution.py:372
  21.2 0.0 copy-start.4
  21.2 0.0 collective-permute-start.6
  21.2 11.5 %collective-permute-done.1.refs_4_ = bf16[2112,128]{1,0:T(8,128)(2,1)S(1)} collective-permute-done((bf16[2112,128]{1,0:T(8,128)(2,1)}, bf16[2112,128]{1,0:T(8,128)(2,1)S(1)}, u32[]{:S(2)}, u32[]{:S(2)}) %collective-permute-start.1) | collective-permute-done | bytes 540704 | tf_op jit(solution)/shard_map/ppermute | solution.py:372
  32.7 0.0 copy-start.5
  32.7 0.0 collective-permute-start.5
  32.7 0.0 collective-permute-done.refs_3_
  32.7 0.0 copy-start.6
  32.7 0.5 collective-permute-start.4
  33.2 2.4 %sort_runs.1.refs_0_.refs_1_ = f32[24,128]{1,0:T(8,128)} custom-call(s32[128,128]{1,0:T(8,128)} %bitcast.8), custom_call_target="tpu_custom_call" | custom-call | tf_op jit(solution)/shard_map/sort_runs/pallas_call | solution.py:171
  35.6 0.0 collective-permute-done.3.refs_6_
  35.6 0.0 all-to-all-done.refs_10_
  35.6 0.0 copy-start.2
  35.6 0.0 collective-permute-done.6.refs_9_
  35.6 0.0 collective-permute-done.5.refs_8_
  35.6 0.0 collective-permute-done.4.refs_7_
  35.6 0.0 copy-done.4
  35.6 0.0 copy-done.5
  35.7 0.0 copy-done.6
  35.7 0.9 copy-done.2
  36.6 37.0 %block_grads.1 = (f32[1024,128]{1,0:T(8,128)}, f32[3,1024,128]{2,1,0:T(8,128)}, bf16[4,1024,128]{2,1,0:T(8,128)(2,1)}, bf16[16,128,256]{2,1,0:T(8,128)(2,1)}) custom-call(f32[24,128]{1,0:T(8,128)} %sort_runs.1.refs_0_.refs_1_, f32[24,128]{1,0:T(8,128)} %sort_runs.1.refs_0_.refs_1_, bf16[2112,128]{1,0:T(8,128)(2,1)} %get-tuple-element.11.refs_2_, ...), custom_call_target="tpu_custom_call" | custom-call | tf_op jit(solution)/shard_map/block_grads/pallas_call | solution.py:316
  73.5 0.2 collective-permute-start.7
  73.7 8.5 %all-to-all-start.1 = ((bf16[16,128,256]{2,1,0:T(8,128)(2,1)}), bf16[16,128,256]{2,1,0:T(8,128)(2,1)S(1)}, u32[]{:S(2)}, u32[]{:S(2)}) async-start(bf16[16,128,256]{2,1,0:T(8,128)(2,1)} %get-tuple-element.16), calls=%async_computation.1 | async-start | bytes 2097152 | tf_op jit(solution)/shard_map/all_to_all | solution.py:384
  82.2 0.0 collective-permute-done.7.in_ref
  82.2 1.6 %add_convert_fusion = bf16[3,1024,128]{2,1,0:T(8,128)(2,1)S(1)} fusion(f32[3,1024,128]{2,1,0:T(8,128)} %get-tuple-element.15, bf16[4,1024,128]{2,1,0:T(8,128)(2,1)S(1)} %collective-permute-done.7.in_ref), kind=kLoop, calls=%fused_computation | loop fusion | flops 1179648 | bytes 3145728 | tf_op jit(solution)/shard_map/convert_element_type | solution.py:386
  83.8 0.0 copy-start
  83.8 0.0 copy-start.1
  83.8 0.9 slice_bitcast_fusion
  84.7 1.6 %collective-permute-start.10 = (bf16[1024,128]{1,0:T(8,128)(2,1)}, bf16[1024,128]{1,0:T(8,128)(2,1)S(1)}, u32[]{:S(2)}, u32[]{:S(2)}) collective-permute-start(bf16[1024,128]{1,0:T(8,128)(2,1)} %get-tuple-element.19), channel_id=1, source_target_pairs={{0,2},{1,3},{2,0},{3,1},{4,6},{5,7},{6,4},{7,5},{8,10},{9,11},{10,... | collective-permute-start | bytes 786440 | tf_op jit(solution)/shard_map/ppermute | solution.py:372
  86.3 0.4 collective-permute-start.9
  86.7 2.9 %collective-permute-start.8 = (bf16[1024,128]{1,0:T(8,128)(2,1)}, bf16[1024,128]{1,0:T(8,128)(2,1)S(1)}, u32[]{:S(2)}, u32[]{:S(2)}) collective-permute-start(bf16[1024,128]{1,0:T(8,128)(2,1)} %get-tuple-element.21), channel_id=1, source_target_pairs={{0,3},{1,0},{2,1},{3,2},{4,7},{5,4},{6,5},{7,6},{8,11},{9,8},{10,9... | collective-permute-start | bytes 786440 | tf_op jit(solution)/shard_map/ppermute | solution.py:372
  89.6 11.3 %all-to-all-done.1.parts_ref = bf16[16,128,256]{2,1,0:T(8,128)(2,1)S(1)} async-done(((bf16[16,128,256]{2,1,0:T(8,128)(2,1)}), bf16[16,128,256]{2,1,0:T(8,128)(2,1)S(1)}, u32[]{:S(2)}, u32[]{:S(2)}) %all-to-all-start.1) | async-done | bytes 1048608 | tf_op jit(solution)/shard_map/all_to_all | solution.py:384
  100.9 0.0 copy-done
  100.9 1.1 %key_sum.1 = (f32[128,128]{1,0:T(8,128)}, f32[128,128]{1,0:T(8,128)}) custom-call(bf16[16,128,256]{2,1,0:T(8,128)(2,1)S(1)} %all-to-all-done.1.parts_ref, s32[128,128]{1,0:T(8,128)S(1)} %bitcast.9), custom_call_target="tpu_custom_call" | custom-call | tf_op jit(solution)/shard_map/key_sum/pallas_call | solution.py:394
  102.0 0.0 collective-permute-done.10.d_ref
  102.0 0.0 collective-permute-done.9.c_ref
  102.0 0.0 collective-permute-done.8.b_ref
  102.0 0.0 copy-done.1
  102.0 1.6 %query_sum.1 = f32[128,1024]{1,0:T(8,128)} custom-call(f32[1024,128]{1,0:T(8,128)S(1)} %copy-done.1, bf16[4,1024,128]{2,1,0:T(8,128)(2,1)S(1)} %collective-permute-done.7.in_ref, bf16[1024,128]{1,0:T(8,128)(2,1)S(1)} %collective-permute-done.8.b_ref, bf16[1024,128]{1,0:T(8,128)(2,1)S(1)} %collective-permute-done.9.c_ref, ...), custom_call_target="tpu_custom_call" | custom-call | tf_op jit(solution)/shard_map/query_sum/pallas_call | solution.py:390
Async XLA Ops:
  3.8 13.1 %copy-start.3 = (bf16[2112,128]{1,0:T(8,128)(2,1)S(1)}, bf16[2112,128]{1,0:T(8,128)(2,1)}, u32[]{:S(2)}) copy-start(bf16[2112,128]{1,0:T(8,128)(2,1)} %get-tuple-element.11.refs_2_) | copy-start | bytes 1622020
  3.8 17.4 %collective-permute-start.2 = (bf16[2112,128]{1,0:T(8,128)(2,1)}, bf16[2112,128]{1,0:T(8,128)(2,1)S(1)}, u32[]{:S(2)}, u32[]{:S(2)}) collective-permute-start(bf16[2112,128]{1,0:T(8,128)(2,1)} %get-tuple-element.11.refs_2_), channel_id=1, source_target_pairs={{0,2},{1,3},{2,0},{3,1},{4,6},{5,7},{6,4},{7,5},{8,10},{9,11},{10,... | collective-permute-start | bytes 1622024 | tf_op jit(solution)/shard_map/ppermute | solution.py:372
  7.8 24.8 %collective-permute-start.1 = (bf16[2112,128]{1,0:T(8,128)(2,1)}, bf16[2112,128]{1,0:T(8,128)(2,1)S(1)}, u32[]{:S(2)}, u32[]{:S(2)}) collective-permute-start(bf16[2112,128]{1,0:T(8,128)(2,1)} %get-tuple-element.11.refs_2_), channel_id=1, source_target_pairs={{0,3},{1,0},{2,1},{3,2},{4,7},{5,4},{6,5},{7,6},{8,11},{9,8},{10,9... | collective-permute-start | bytes 1622024 | tf_op jit(solution)/shard_map/ppermute | solution.py:372
  8.5 24.1 %collective-permute-start = (bf16[2112,128]{1,0:T(8,128)(2,1)}, bf16[2112,128]{1,0:T(8,128)(2,1)S(1)}, u32[]{:S(2)}, u32[]{:S(2)}) collective-permute-start(bf16[2112,128]{1,0:T(8,128)(2,1)} %get-tuple-element.11.refs_2_), channel_id=1, source_target_pairs={{0,1},{1,2},{2,3},{3,0},{4,5},{5,6},{6,7},{7,4},{8,9},{9,10},{10,1... | collective-permute-start | bytes 1622024 | tf_op jit(solution)/shard_map/ppermute | solution.py:372
  9.9 25.7 %all-to-all-start = ((bf16[16,128,256]{2,1,0:T(8,128)(2,1)}), bf16[16,128,256]{2,1,0:T(8,128)(2,1)S(1)}, u32[]{:S(2)}, u32[]{:S(2)}) async-start(bf16[16,128,256]{2,1,0:T(8,128)(2,1)} %get-tuple-element.12), calls=%async_computation | async-start | bytes 2097152 | tf_op jit(solution)/shard_map/all_to_all | solution.py:382
  16.9 18.7 %collective-permute-start.3 = (bf16[2112,128]{1,0:T(8,128)(2,1)S(1)}, bf16[2112,128]{1,0:T(8,128)(2,1)}, u32[]{:S(2)}, u32[]{:S(2)}) collective-permute-start(bf16[2112,128]{1,0:T(8,128)(2,1)S(1)} %copy-done.3), channel_id=1, source_target_pairs={{0,8},{8,0},{1,9},{9,1},{2,10},{10,2},{3,11},{11,3},{4,12},{12,4},... | collective-permute-start | bytes 1622024 | tf_op jit(solution)/shard_map/ppermute | solution.py:375
  21.2 14.4 %copy-start.4 = (bf16[2112,128]{1,0:T(8,128)(2,1)}, bf16[2112,128]{1,0:T(8,128)(2,1)S(1)}, u32[]{:S(2)}) copy-start(bf16[2112,128]{1,0:T(8,128)(2,1)S(1)} %collective-permute-done.2.refs_5_) | copy-start | bytes 1622020
  21.2 14.4 %collective-permute-start.6 = (bf16[2112,128]{1,0:T(8,128)(2,1)S(1)}, bf16[2112,128]{1,0:T(8,128)(2,1)}, u32[]{:S(2)}, u32[]{:S(2)}) collective-permute-start(bf16[2112,128]{1,0:T(8,128)(2,1)S(1)} %collective-permute-done.2.refs_5_), channel_id=1, source_target_pairs={{0,8},{8,0},{1,9},{9,1},{2,10},{10,2},{3,11},{11,3},{4,12},{12,4},... | collective-permute-start | bytes 1622024 | tf_op jit(solution)/shard_map/ppermute | solution.py:375
  32.7 3.0 %copy-start.5 = (bf16[2112,128]{1,0:T(8,128)(2,1)}, bf16[2112,128]{1,0:T(8,128)(2,1)S(1)}, u32[]{:S(2)}) copy-start(bf16[2112,128]{1,0:T(8,128)(2,1)S(1)} %collective-permute-done.1.refs_4_) | copy-start | bytes 1622020
  32.7 2.9 %collective-permute-start.5 = (bf16[2112,128]{1,0:T(8,128)(2,1)S(1)}, bf16[2112,128]{1,0:T(8,128)(2,1)}, u32[]{:S(2)}, u32[]{:S(2)}) collective-permute-start(bf16[2112,128]{1,0:T(8,128)(2,1)S(1)} %collective-permute-done.1.refs_4_), channel_id=1, source_target_pairs={{0,8},{8,0},{1,9},{9,1},{2,10},{10,2},{3,11},{11,3},{4,12},{12,4},... | collective-permute-start | bytes 1622024 | tf_op jit(solution)/shard_map/ppermute | solution.py:375
  32.7 3.0 %copy-start.6 = (bf16[2112,128]{1,0:T(8,128)(2,1)}, bf16[2112,128]{1,0:T(8,128)(2,1)S(1)}, u32[]{:S(2)}) copy-start(bf16[2112,128]{1,0:T(8,128)(2,1)S(1)} %collective-permute-done.refs_3_) | copy-start | bytes 1622020
  32.7 2.9 %collective-permute-start.4 = (bf16[2112,128]{1,0:T(8,128)(2,1)S(1)}, bf16[2112,128]{1,0:T(8,128)(2,1)}, u32[]{:S(2)}, u32[]{:S(2)}) collective-permute-start(bf16[2112,128]{1,0:T(8,128)(2,1)S(1)} %collective-permute-done.refs_3_), channel_id=1, source_target_pairs={{0,8},{8,0},{1,9},{9,1},{2,10},{10,2},{3,11},{11,3},{4,12},{12,4},... | collective-permute-start | bytes 1622024 | tf_op jit(solution)/shard_map/ppermute | solution.py:375
  35.6 1.0 copy-start.2
  73.5 8.7 %collective-permute-start.7 = (bf16[4,1024,128]{2,1,0:T(8,128)(2,1)}, bf16[4,1024,128]{2,1,0:T(8,128)(2,1)S(1)}, u32[]{:S(2)}, u32[]{:S(2)}) collective-permute-start(bf16[4,1024,128]{2,1,0:T(8,128)(2,1)} %get-tuple-element.14), channel_id=1, source_target_pairs={{0,8},{8,0},{1,9},{9,1},{2,10},{10,2},{3,11},{11,3},{4,12},{12,4},... | collective-permute-start | bytes 3145736 | tf_op jit(solution)/shard_map/ppermute | solution.py:375
  73.7 27.1 %all-to-all-start.1 = ((bf16[16,128,256]{2,1,0:T(8,128)(2,1)}), bf16[16,128,256]{2,1,0:T(8,128)(2,1)S(1)}, u32[]{:S(2)}, u32[]{:S(2)}) async-start(bf16[16,128,256]{2,1,0:T(8,128)(2,1)} %get-tuple-element.16), calls=%async_computation.1 | async-start | bytes 2097152 | tf_op jit(solution)/shard_map/all_to_all | solution.py:384
  83.8 17.1 %copy-start = (s32[16384]{0:T(1024)S(1)}, s32[16384]{0:T(1024)}, u32[]{:S(2)}) copy-start(s32[16384]{0:T(1024)} %param.13) | copy-start | bytes 196612
  83.8 18.2 %copy-start.1 = (f32[1024,128]{1,0:T(8,128)S(1)}, f32[1024,128]{1,0:T(8,128)}, u32[]{:S(2)}) copy-start(f32[1024,128]{1,0:T(8,128)} %get-tuple-element.13.own_ref) | copy-start | bytes 1572868
  84.7 17.3 %collective-permute-start.10 = (bf16[1024,128]{1,0:T(8,128)(2,1)}, bf16[1024,128]{1,0:T(8,128)(2,1)S(1)}, u32[]{:S(2)}, u32[]{:S(2)}) collective-permute-start(bf16[1024,128]{1,0:T(8,128)(2,1)} %get-tuple-element.19), channel_id=1, source_target_pairs={{0,2},{1,3},{2,0},{3,1},{4,6},{5,7},{6,4},{7,5},{8,10},{9,11},{10,... | collective-permute-start | bytes 786440 | tf_op jit(solution)/shard_map/ppermute | solution.py:372
  86.3 15.7 %collective-permute-start.9 = (bf16[1024,128]{1,0:T(8,128)(2,1)}, bf16[1024,128]{1,0:T(8,128)(2,1)S(1)}, u32[]{:S(2)}, u32[]{:S(2)}) collective-permute-start(bf16[1024,128]{1,0:T(8,128)(2,1)} %get-tuple-element.20), channel_id=1, source_target_pairs={{0,1},{1,2},{2,3},{3,0},{4,5},{5,6},{6,7},{7,4},{8,9},{9,10},{10,1... | collective-permute-start | bytes 786440 | tf_op jit(solution)/shard_map/ppermute | solution.py:372
  86.7 15.3 %collective-permute-start.8 = (bf16[1024,128]{1,0:T(8,128)(2,1)}, bf16[1024,128]{1,0:T(8,128)(2,1)S(1)}, u32[]{:S(2)}, u32[]{:S(2)}) collective-permute-start(bf16[1024,128]{1,0:T(8,128)(2,1)} %get-tuple-element.21), channel_id=1, source_target_pairs={{0,3},{1,0},{2,1},{3,2},{4,7},{5,4},{6,5},{7,6},{8,11},{9,8},{10,9... | collective-permute-start | bytes 786440 | tf_op jit(solution)/shard_map/ppermute | solution.py:372

commit v3 on v2

--- a/solution.py
+++ b/solution.py
@@ -144,7 +144,7 @@
     )(q, g, o, ln, k, v, pos)
 
 
-def sorted_kernel(pos_ref, out_ref):
+def sorted_kernel(pos_ref, pay_ref, out_ref, copy_ref, qpt, kps, kx, vx):
     ylo, x, core, yhi, z = own_index()
     rows = []
     for key_yhi in range(2):
@@ -165,33 +165,10 @@
             pltpu.roll(rank, s, 1) == lane, pltpu.roll(pos, s, 1), 0.0
         )
     out_ref[...] = ordered
-
-
-def sort_runs(pos):
-    return pl.pallas_call(
-        sorted_kernel,
-        out_shape=jax.ShapeDtypeStruct((KRUNS + QRUNS, RUN), F32),
-        name="sort_runs",
-    )(pos)
-
-
-def main_kernel(*refs):
-    pos_ref, spos = refs[:2]
-    runs = refs[2:10]
-    kv_ref = refs[10]
-    dq_near, dq_own, dq_other, dkv_ref = refs[11:15]
-    qpt, kps, dqs, dks, dvs, tx, kx, vx = refs[15:]
-    for run, pay in enumerate(runs):
-        terms = jnp.concatenate(
-            [
-                pay[1024:1056, :].astype(F32),
-                pay[HALF + 1024 : HALF + 1056, :].astype(F32),
-                jnp.zeros((RUN - 64, RUN), F32),
-            ],
-            axis=0,
-        )
-        tx[run * RUN : (run + 1) * RUN, :] = terms.T.astype(BF16)
-    query_pos = pos_ref[KRUNS : KRUNS + QRUNS, :].T
+    copy_ref[...] = pay_ref[...]
+    query_pos = jnp.concatenate(
+        [ordered[KRUNS : KRUNS + QRUNS, :], jnp.zeros((RUN - QRUNS, RUN), F32)], axis=0
+    ).T
     lane = lax.broadcasted_iota(jnp.int32, (BAND, WIDTH), 1)
     for band in range(BANDS):
         rows = slice(band * BAND, (band + 1) * BAND)
@@ -202,8 +179,45 @@
                 query_pos[rows, run : run + 1], (BAND, WIDTH)
             )
         kps[band : band + 1, :] = jnp.concatenate(
-            [pos_ref[run : run + 1, rows] for run in range(KRUNS)], axis=1
-        )
+            [ordered[run : run + 1, rows] for run in range(KRUNS)], axis=1
+        )
+
+
+def sort_runs(pos, payload):
+    return pl.pallas_call(
+        sorted_kernel,
+        out_shape=(
+            jax.ShapeDtypeStruct((KRUNS + QRUNS, RUN), F32),
+            jax.ShapeDtypeStruct(payload.shape, payload.dtype),
+            jax.ShapeDtypeStruct((BANDS, QRUNS * BAND, WIDTH), F32),
+            jax.ShapeDtypeStruct((BANDS, KROWS), F32),
+            jax.ShapeDtypeStruct((BANDS, BAND, WIDTH), BF16),
+            jax.ShapeDtypeStruct((BANDS, BAND, WIDTH), BF16),
+        ),
+        compiler_params=pltpu.CompilerParams(vmem_limit_bytes=32 * 1024 * 1024),
+        name="sort_runs",
+    )(pos, payload)
+
+
+def main_kernel(*refs):
+    spos, qpt, kps, kx, vx = refs[:5]
+    runs = []
+    for core in range(2):
+        near, left, right, far_q, far_g = refs[5 + core * 5 : 10 + core * 5]
+        runs += [(near, near, HALF), (left, left, HALF), (right, right, HALF), (far_q, far_g, 0)]
+    kv_ref = refs[15]
+    dq_near, dq_own, dq_other, dkv_ref = refs[16:20]
+    dqs, dks, dvs, tx = refs[20:]
+    for run, (q_pay, g_pay, base) in enumerate(runs):
+        terms = jnp.concatenate(
+            [
+                q_pay[1024:1056, :].astype(F32),
+                g_pay[base + 1024 : base + 1056, :].astype(F32),
+                jnp.zeros((RUN - 64, RUN), F32),
+            ],
+            axis=0,
+        )
+        tx[run * RUN : (run + 1) * RUN, :] = terms.T.astype(BF16)
     dks[...] = jnp.zeros_like(dks)
     dvs[...] = jnp.zeros_like(dvs)
     by_cols = (((1,), (1,)), ((), ()))
@@ -211,9 +225,14 @@
 
     def block(u, first, bands):
         at = pl.ds(pl.multiple_of(u * RUN, RUN), RUN)
-        g_at = pl.ds(pl.multiple_of(HALF + u * RUN, 16), RUN)
-        q = jnp.concatenate([pay[at, :] for pay in runs], axis=0)
-        g = jnp.concatenate([pay[g_at, :] for pay in runs], axis=0)
+        q = jnp.concatenate([pay[at, :] for pay, _, _ in runs], axis=0)
+        g = jnp.concatenate(
+            [
+                pay[pl.ds(pl.multiple_of(base + u * RUN, 16), RUN), :]
+                for _, pay, base in runs
+            ],
+            axis=0,
+        )
         terms = tx[...]
         rows = [
             pl.ds(pl.multiple_of((first + i) * BAND, BAND), BAND) for i in range(bands)
@@ -294,7 +313,9 @@
         rows = pl.ds(pl.multiple_of(u * RUN, RUN), RUN)
         dq_near[rows, :] = dqs[0:RUN, :] * INV_ROOT
         for run in range(1, 4):
-            dq_own[run - 1, rows, :] = dqs[run * RUN : (run + 1) * RUN, :] * INV_ROOT
+            dq_own[run - 1, rows, :] = (
+                dqs[run * RUN : (run + 1) * RUN, :] * INV_ROOT
+            ).astype(BF16)
         for run in range(4):
             dq_other[run, rows, :] = (
                 dqs[(4 + run) * RUN : (5 + run) * RUN, :] * INV_ROOT
@@ -311,48 +332,47 @@
             dkv_ref[run, rows, WIDTH:] = value_part[run * BAND : (run + 1) * BAND]
 
 
-def main(runs, payloads, kv):
+def main(runs, tables, payloads, kv):
     vmem = pl.BlockSpec(memory_space=pltpu.VMEM)
     return pl.pallas_call(
         main_kernel,
-        in_specs=[vmem, pl.BlockSpec(memory_space=pltpu.SMEM)] + [vmem] * 9,
+        in_specs=[pl.BlockSpec(memory_space=pltpu.SMEM)] + [vmem] * 15,
         out_shape=(
             jax.ShapeDtypeStruct((1024, WIDTH), F32),
-            jax.ShapeDtypeStruct((3, 1024, WIDTH), F32),
+            jax.ShapeDtypeStruct((3, 1024, WIDTH), BF16),
             jax.ShapeDtypeStruct((4, 1024, WIDTH), BF16),
             jax.ShapeDtypeStruct((16, RUN, 2 * WIDTH), BF16),
         ),
         scratch_shapes=[
-            pltpu.VMEM((BANDS, QRUNS * BAND, WIDTH), F32),
-            pltpu.VMEM((BANDS, KROWS), F32),
             pltpu.VMEM((QROWS, WIDTH), F32),
             pltpu.VMEM((BANDS, WIDTH, KROWS), F32),
             pltpu.VMEM((BANDS, WIDTH, KROWS), F32),
             pltpu.VMEM((QROWS, WIDTH), BF16),
-            pltpu.VMEM((BANDS, BAND, WIDTH), BF16),
-            pltpu.VMEM((BANDS, BAND, WIDTH), BF16),
         ],
         compiler_params=pltpu.CompilerParams(vmem_limit_bytes=56 * 1024 * 1024),
         name="block_grads",
-    )(runs, runs, *payloads, kv)
-
-
-def query_kernel(own_ref, in_ref, b_ref, c_ref, d_ref, pos_ref, out_ref):
-    q_block, _ = placed(own_index())
+    )(runs, *tables, *payloads, kv)
+
+
+def add_kernel(own_ref, in_ref, *out_refs):
+    for run, out_ref in enumerate(out_refs):
+        out_ref[...] = (own_ref[run].astype(F32) + in_ref[run + 1].astype(F32)).astype(BF16)
+
+
+def final_kernel(
+    own_ref, in_ref, b_ref, c_ref, d_ref, parts_ref, pos_ref, dq_ref, dk_ref, dv_ref
+):
+    q_block, k_block = placed(own_index())
     place, _ = rank_matrices(pos_ref[pl.ds(q_block, 1), :].astype(F32))
     total = own_ref[...] + in_ref[0].astype(F32)
     for ref in (b_ref, c_ref, d_ref):
         total = total + ref[...].astype(F32)
     total = total.reshape(BANDS, HEADS, BAND, WIDTH)
     for h in range(HEADS):
-        out_ref[:, h * WIDTH : (h + 1) * WIDTH] = lax.dot_general(
+        dq_ref[:, h * WIDTH : (h + 1) * WIDTH] = lax.dot_general(
             place, total[:, h].reshape(RUN, WIDTH), (((0,), (0,)), ((), ())),
             precision=HIGH, preferred_element_type=F32,
         )
-
-
-def key_kernel(parts_ref, pos_ref, dk_ref, dv_ref):
-    _, k_block = placed(own_index())
     place, _ = rank_matrices(pos_ref[pl.ds(k_block, 1), :].astype(F32))
     total = parts_ref[0].astype(F32)
     for i in range(1, 16):
@@ -376,31 +396,34 @@
 
     from_left = along_z(payload, 1)
     from_right = along_z(payload, 3)
-    from_far = along_z(payload, 2)
-    mine = (payload, from_left, from_right, from_far)
-    payloads = mine + tuple(cross(array) for array in mine)
+    far_q = along_z(from_left[:HALF], 1)
+    far_g = along_z(from_right[HALF:], 3)
+    mine = (payload, from_left, from_right, far_q, far_g)
+    runs, handed, *tables = sort_runs(pos, payload)
+    payloads = mine + (cross(handed),) + tuple(cross(array) for array in mine[1:])
     kv = lax.all_to_all(kv_out, PLANE, 0, 0, tiled=True)
-    dq_near, dq_own, dq_other, dkv = main(sort_runs(pos), payloads, kv)
+    dq_near, dq_own, dq_other, dkv = main(runs, tables, payloads, kv)
     dkv_parts = lax.all_to_all(dkv, PLANE, 0, 0, tiled=True)
     dq_in = cross(dq_other)
-    dq_sum = (dq_own + dq_in[1:].astype(F32)).astype(BF16)
-    dq_left = along_z(dq_sum[0], 3)
-    dq_right = along_z(dq_sum[1], 1)
-    dq_far = along_z(dq_sum[2], 2)
-    query_grad = pl.pallas_call(
-        query_kernel, out_shape=jax.ShapeDtypeStruct((RUN, HEADS * WIDTH), F32), name="query_sum",
+    sums = pl.pallas_call(
+        add_kernel,
+        out_shape=[jax.ShapeDtypeStruct((1024, WIDTH), BF16)] * 3,
         compiler_params=pltpu.CompilerParams(vmem_limit_bytes=32 * 1024 * 1024),
-    )(dq_near, dq_in, dq_left, dq_right, dq_far, pos)
-    key_grad, value_grad = pl.pallas_call(
-        key_kernel,
+        name="core_sum",
+    )(dq_own, dq_in)
+    dq_left = along_z(sums[0], 3)
+    dq_right = along_z(sums[1], 1)
+    dq_far = along_z(sums[2], 2)
+    return pl.pallas_call(
+        final_kernel,
         out_shape=(
+            jax.ShapeDtypeStruct((RUN, HEADS * WIDTH), F32),
             jax.ShapeDtypeStruct((RUN, WIDTH), F32),
             jax.ShapeDtypeStruct((RUN, WIDTH), F32),
         ),
-        name="key_sum",
         compiler_params=pltpu.CompilerParams(vmem_limit_bytes=32 * 1024 * 1024),
-    )(dkv_parts, pos)
-    return query_grad, key_grad, value_grad
+        name="final_sums",
+    )(dq_near, dq_in, dq_left, dq_right, dq_far, dkv_parts, pos)
 
 
 def solution(mesh):

time: 104 us -> 98 us (0.942)
  starting transfers between devices: 27.2 us -> 25 us
  other arithmetic: 1.56 us -> 0 us
  Pallas kernels: 45.2 us -> 43.7 us
    ppermute x6 -> x7, waiting for transfers between devices: 15.7 us -> 9.12 us  [along_z(): return lax.ppermute(array, 'z', [(i, (i + step) % 4) for i in range(4)])]
    all_to_all x1, waiting for transfers between devices: 11.3 us -> 15.5 us  [shards(): dkv_parts = lax.all_to_all(dkv, PLANE, 0, 0, tiled=True)]
    pallas_call x4, Pallas kernels: 42 us -> 40.5 us  [the longest x1 36.4 us: main(): pl.pallas_call(main_kernel, in_specs=[pl.BlockSpec(memory_space=pltpu.SME...]
    convert_element_type x1 -> x0, other arithmetic: 1.56 us -> none  [shards(): dq_sum = (dq_own + dq_in[1:].astype(F32)).astype(BF16)]
    ppermute x5 -> x6, waiting for transfers between devices: 0.01 us -> 1.41 us  [cross(): return lax.ppermute(array, 'core', [(0, 1), (1, 0)])]
    all_to_all x1, starting transfers between devices: 8.47 us -> 7.21 us  [shards(): dkv_parts = lax.all_to_all(dkv, PLANE, 0, 0, tiled=True)]
    ppermute x6 -> x7, starting transfers between devices: 11 us -> 10 us  [along_z(): return lax.ppermute(array, 'z', [(i, (i + step) % 4) for i in range(4)])]
  transfers between devices with their start and end apart: 13 -> 15, of which waited for: 3 -> 6; matrix products, arithmetic and copies ran while one was open for 2% -> 0% of each run, Pallas kernels for 3% -> 3%
where the time goes in v3:
time: 98 us; the launch traced here: 97.9 us
  Pallas kernels  43.7 us (45%)
  waiting for transfers between devices  26.5 us (27%)
  starting transfers between devices  25 us (26%)
  local copies, waits for them, and re-layouts  1.9 us (2%)
    pallas_call x1, Pallas kernels, main(): pl.pallas_call(main_kernel, in_specs=[pl.BlockSpec(memory_space=pltpu.SME...  36.4 us
    all_to_all x1, waiting for transfers between devices, shards(): dkv_parts = lax.all_to_all(dkv, PLANE, 0, 0, tiled=True)  15.5 us
    ppermute x7, starting transfers between devices, along_z(): return lax.ppermute(array, 'z', [(i, (i + step) % 4) for i in range(4)])  10 us
    ppermute x7, waiting for transfers between devices, along_z(): return lax.ppermute(array, 'z', [(i, (i + step) % 4) for i in range(4)])  9.12 us
    all_to_all x1, starting transfers between devices, shards(): dkv_parts = lax.all_to_all(dkv, PLANE, 0, 0, tiled=True)  7.21 us
    all_to_all x1, starting transfers between devices, shards(): kv = lax.all_to_all(kv_out, PLANE, 0, 0, tiled=True)  7.17 us
    pallas_call x1, Pallas kernels, prep(): pl.pallas_call(prep_kernel, in_specs=[pl.BlockSpec(memory_space=pl.ANY)]...  3.2 us
  transfers between devices with their start and end apart: 15, of which 6 were waited for; matrix products, arithmetic and copies ran while one was open for 0% of the time, Pallas kernels for 3%

profile of v3, /device:TPU:0, one launch (start us, length us, event | category | flops | bytes accessed | tf_op | source)
XLA Modules:
  0.0 97.9 jit_solution(6047135358485023382)
XLA Ops:
  0.6 3.2 %prep.1 = (bf16[2112,128]{1,0:T(8,128)(2,1)}, bf16[16,128,256]{2,1,0:T(8,128)(2,1)}) custom-call(bf16[128,1024]{1,0:T(8,128)(2,1)} %q_hbm.1, bf16[128,1024]{1,0:T(8,128)(2,1)} %g_hbm.1, bf16[128,1024]{1,0:T(8,128)(2,1)} %o_hbm.1, f32[8,128]{1,0:T(8,128)} %ln_hbm.1, bf16[128,128]{1,0:T(8,128)(2,1)} %k_hbm.1, bf16[128,128]{1,0:T(8,128)(2,1)} %v_hbm.1, ...), custom_call_target="tpu_custom_call" | custom-call | tf_op jit(solution)/shard_map/prep/pallas_call | solution.py:125
  3.8 4.2 %collective-permute-start.1 = (bf16[2112,128]{1,0:T(8,128)(2,1)}, bf16[2112,128]{1,0:T(8,128)(2,1)S(1)}, u32[]{:S(2)}, u32[]{:S(2)}) collective-permute-start(bf16[2112,128]{1,0:T(8,128)(2,1)} %get-tuple-element.18.pay_ref.refs_5_), channel_id=1, source_target_pairs={{0,3},{1,0},{2,1},{3,2},{4,7},{5,4},{6,5},{7,6},{8,11},{9,8},{10,9... | collective-permute-start | bytes 1622024 | tf_op jit(solution)/shard_map/ppermute | solution.py:392
  8.0 0.0 collective-permute-start
  8.0 0.0 copy-start
  8.0 0.0 copy-start.2
  8.0 7.2 %all-to-all-start = ((bf16[16,128,256]{2,1,0:T(8,128)(2,1)}), bf16[16,128,256]{2,1,0:T(8,128)(2,1)S(1)}, u32[]{:S(2)}, u32[]{:S(2)}) async-start(bf16[16,128,256]{2,1,0:T(8,128)(2,1)} %get-tuple-element.25), calls=%async_computation | async-start | bytes 2097152 | tf_op jit(solution)/shard_map/all_to_all | solution.py:404
  15.2 0.0 copy-done
  15.2 0.0 copy-done.2
  15.2 1.5 %sort_runs.1 = (f32[24,128]{1,0:T(8,128)S(1)}, bf16[2112,128]{1,0:T(8,128)(2,1)S(1)}, f32[8,128,128]{2,1,0:T(8,128)S(1)}, f32[8,256]{1,0:T(8,128)S(1)}, bf16[8,1...) custom-call(s32[128,128]{1,0:T(8,128)S(1)} %bitcast.2, bf16[2112,128]{1,0:T(8,128)(2,1)S(1)} %copy-done), custom_call_target="tpu_custom_call" | custom-call | tf_op jit(solution)/shard_map/sort_runs/pallas_call | solution.py:187
  16.7 0.0 copy-start.5
  16.7 0.6 copy-done.5
  17.3 0.0 copy-start.6
  17.3 0.6 copy-done.6
  17.9 0.0 copy-start.8
  17.9 0.6 copy-done.8
  18.5 0.0 copy-start.7
  18.5 0.0 copy-start.3
  18.5 0.0 collective-permute-start.4
  18.5 1.3 %collective-permute-done.1.refs_7_ = bf16[2112,128]{1,0:T(8,128)(2,1)S(1)} collective-permute-done((bf16[2112,128]{1,0:T(8,128)(2,1)}, bf16[2112,128]{1,0:T(8,128)(2,1)S(1)}, u32[]{:S(2)}, u32[]{:S(2)}) %collective-permute-start.1) | collective-permute-done | bytes 540704 | tf_op jit(solution)/shard_map/ppermute | solution.py:392
  19.9 0.0 copy-start.10
  19.9 0.0 copy-done.7
  19.9 3.7 %collective-permute-start.3 = (bf16[1056,128]{1,0:T(8,128)(2,1)S(1)}, bf16[1056,128]{1,0:T(8,128)(2,1)S(1)}, u32[]{:S(2)}, u32[]{:S(2)}) collective-permute-start(bf16[1056,128]{1,0:T(8,128)(2,1)S(1)} %slice.9), channel_id=1, source_target_pairs={{0,3},{1,0},{2,1},{3,2},{4,7},{5,4},{6,5},{7,6},{8,11},{9,8},{10,9... | collective-permute-start | bytes 811016 | tf_op jit(solution)/shard_map/ppermute | solution.py:392
  23.6 0.0 collective-permute-done.refs_6_
  23.6 0.0 copy-start.11
  23.6 0.0 copy-done.3
  23.6 0.1 collective-permute-start.2
  23.7 0.0 copy-done.10
  23.7 0.1 collective-permute-start.6
  23.8 0.5 collective-permute-start.5
  24.3 4.1 %collective-permute-done.3.refs_9_ = bf16[1056,128]{1,0:T(8,128)(2,1)S(1)} collective-permute-done((bf16[1056,128]{1,0:T(8,128)(2,1)S(1)}, bf16[1056,128]{1,0:T(8,128)(2,1)S(1)}, u32[]{:S(2)}, u32[]{:S(2)}) %collective-permute-start.3) | collective-permute-done | bytes 270368 | tf_op jit(solution)/shard_map/ppermute | solution.py:392
  28.4 0.0 copy-start.14
  28.4 0.0 collective-permute-start.8
  28.4 3.6 %collective-permute-done.2.refs_8_ = bf16[1056,128]{1,0:T(8,128)(2,1)} collective-permute-done((bf16[1056,128]{1,0:T(8,128)(2,1)S(1)}, bf16[1056,128]{1,0:T(8,128)(2,1)}, u32[]{:S(2)}, u32[]{:S(2)}) %collective-permute-start.2) | collective-permute-done | bytes 270368 | tf_op jit(solution)/shard_map/ppermute | solution.py:392
  32.1 0.0 collective-permute-start.7
  32.1 0.0 collective-permute-done.4.refs_10_
  32.1 0.0 copy-start.12
  32.1 0.5 all-to-all-done.refs_15_
  32.5 0.0 collective-permute-done.8.refs_14_
  32.5 0.0 collective-permute-done.6.refs_12_
  32.5 0.0 copy-start.13
  32.6 1.4 %collective-permute-done.7.refs_13_ = bf16[1056,128]{1,0:T(8,128)(2,1)} collective-permute-done((bf16[1056,128]{1,0:T(8,128)(2,1)}, bf16[1056,128]{1,0:T(8,128)(2,1)}, u32[]{:S(2)}, u32[]{:S(2)}) %collective-permute-start.7) | collective-permute-done | bytes 270368 | tf_op jit(solution)/shard_map/ppermute | solution.py:395
  33.9 0.0 collective-permute-done.5.refs_11_
  34.0 0.0 copy-done.11
  34.0 0.0 copy-done.14
  34.0 0.0 copy-done.12
  34.0 0.0 copy-done.9
  34.0 0.0 copy-done.13
  34.0 36.4 %block_grads.1 = (f32[1024,128]{1,0:T(8,128)}, bf16[3,1024,128]{2,1,0:T(8,128)(2,1)}, bf16[4,1024,128]{2,1,0:T(8,128)(2,1)}, bf16[16,128,256]{2,1,0:T(8,128)(2,1)}) custom-call(f32[24,128]{1,0:T(8,128)} %copy-done.7, f32[8,128,128]{2,1,0:T(8,128)} %copy-done.3, f32[8,256]{1,0:T(8,128)} %copy-done.8, bf16[8,16,128]{2,1,0:T(8,128)(2,1)} %copy-done.5, ...), custom_call_target="tpu_custom_call" | custom-call | tf_op jit(solution)/shard_map/block_grads/pallas_call | solution.py:337
  70.4 0.0 collective-permute-start.9
  70.4 0.0 copy-start.1
  70.4 7.2 %all-to-all-start.1 = ((bf16[16,128,256]{2,1,0:T(8,128)(2,1)}), bf16[16,128,256]{2,1,0:T(8,128)(2,1)S(1)}, u32[]{:S(2)}, u32[]{:S(2)}) async-start(bf16[16,128,256]{2,1,0:T(8,128)(2,1)} %get-tuple-element.32), calls=%async_computation.1 | async-start | bytes 2097152 | tf_op jit(solution)/shard_map/all_to_all | solution.py:406
  77.6 0.0 collective-permute-done.9.in_ref
  77.6 0.0 copy-done.1
  77.6 0.0 copy-start.4
  77.6 1.0 %core_sum.1 = (bf16[1024,128]{1,0:T(8,128)(2,1)}, bf16[1024,128]{1,0:T(8,128)(2,1)}, bf16[1024,128]{1,0:T(8,128)(2,1)}) custom-call(bf16[3,1024,128]{2,1,0:T(8,128)(2,1)S(1)} %copy-done.1, bf16[4,1024,128]{2,1,0:T(8,128)(2,1)S(1)} %collective-permute-done.9.in_ref), custom_call_target="tpu_custom_call" | custom-call | tf_op jit(solution)/shard_map/core_sum/pallas_call | solution.py:408
  78.6 0.6 collective-permute-start.10
  79.2 1.4 %collective-permute-start.11 = (bf16[1024,128]{1,0:T(8,128)(2,1)}, bf16[1024,128]{1,0:T(8,128)(2,1)S(1)}, u32[]{:S(2)}, u32[]{:S(2)}) collective-permute-start(bf16[1024,128]{1,0:T(8,128)(2,1)} %get-tuple-element.30), channel_id=1, source_target_pairs={{0,1},{1,2},{2,3},{3,0},{4,5},{5,6},{6,7},{7,4},{8,9},{9,10},{10,1... | collective-permute-start | bytes 786440 | tf_op jit(solution)/shard_map/ppermute | solution.py:392
  80.7 0.0 collective-permute-start.12
  80.7 15.5 %all-to-all-done.1.parts_ref = bf16[16,128,256]{2,1,0:T(8,128)(2,1)S(1)} async-done(((bf16[16,128,256]{2,1,0:T(8,128)(2,1)}), bf16[16,128,256]{2,1,0:T(8,128)(2,1)S(1)}, u32[]{:S(2)}, u32[]{:S(2)}) %all-to-all-start.1) | async-done | bytes 1048608 | tf_op jit(solution)/shard_map/all_to_all | solution.py:406
  96.2 0.0 collective-permute-done.10.b_ref
  96.2 0.0 collective-permute-done.11.c_ref
  96.2 0.0 collective-permute-done.12.d_ref
  96.2 0.0 copy-done.4
  96.2 1.6 %final_sums.1 = (f32[128,1024]{1,0:T(8,128)}, f32[128,128]{1,0:T(8,128)}, f32[128,128]{1,0:T(8,128)}) custom-call(f32[1024,128]{1,0:T(8,128)S(1)} %copy-done.4, bf16[4,1024,128]{2,1,0:T(8,128)(2,1)S(1)} %collective-permute-done.9.in_ref, bf16[1024,128]{1,0:T(8,128)(2,1)S(1)} %collective-permute-done.10.b_ref, ...), custom_call_target="tpu_custom_call" | custom-call | tf_op jit(solution)/shard_map/final_sums/pallas_call | solution.py:417
  (3 shorter events, 0.0 us)
Async XLA Ops:
  3.8 16.0 %collective-permute-start.1 = (bf16[2112,128]{1,0:T(8,128)(2,1)}, bf16[2112,128]{1,0:T(8,128)(2,1)S(1)}, u32[]{:S(2)}, u32[]{:S(2)}) collective-permute-start(bf16[2112,128]{1,0:T(8,128)(2,1)} %get-tuple-element.18.pay_ref.refs_5_), channel_id=1, source_target_pairs={{0,3},{1,0},{2,1},{3,2},{4,7},{5,4},{6,5},{7,6},{8,11},{9,8},{10,9... | collective-permute-start | bytes 1622024 | tf_op jit(solution)/shard_map/ppermute | solution.py:392
  8.0 15.5 %collective-permute-start = (bf16[2112,128]{1,0:T(8,128)(2,1)}, bf16[2112,128]{1,0:T(8,128)(2,1)S(1)}, u32[]{:S(2)}, u32[]{:S(2)}) collective-permute-start(bf16[2112,128]{1,0:T(8,128)(2,1)} %get-tuple-element.18.pay_ref.refs_5_), channel_id=1, source_target_pairs={{0,1},{1,2},{2,3},{3,0},{4,5},{5,6},{6,7},{7,4},{8,9},{9,10},{10,1... | collective-permute-start | bytes 1622024 | tf_op jit(solution)/shard_map/ppermute | solution.py:392
  8.0 7.2 %copy-start = (bf16[2112,128]{1,0:T(8,128)(2,1)S(1)}, bf16[2112,128]{1,0:T(8,128)(2,1)}, u32[]{:S(2)}) copy-start(bf16[2112,128]{1,0:T(8,128)(2,1)} %get-tuple-element.18.pay_ref.refs_5_) | copy-start | bytes 1622020
  8.0 7.2 %copy-start.2 = (s32[16384]{0:T(1024)S(1)}, s32[16384]{0:T(1024)}, u32[]{:S(2)}) copy-start(s32[16384]{0:T(1024)} %param.13) | copy-start | bytes 196612
  8.0 24.5 %all-to-all-start = ((bf16[16,128,256]{2,1,0:T(8,128)(2,1)}), bf16[16,128,256]{2,1,0:T(8,128)(2,1)S(1)}, u32[]{:S(2)}, u32[]{:S(2)}) async-start(bf16[16,128,256]{2,1,0:T(8,128)(2,1)} %get-tuple-element.25), calls=%async_computation | async-start | bytes 2097152 | tf_op jit(solution)/shard_map/all_to_all | solution.py:404
  16.7 0.6 copy-start.5
  17.3 0.6 copy-start.6
  17.9 0.6 copy-start.8
  18.5 1.4 %copy-start.7 = (f32[24,128]{1,0:T(8,128)}, f32[24,128]{1,0:T(8,128)S(1)}, u32[]{:S(2)}) copy-start(f32[24,128]{1,0:T(8,128)S(1)} %get-tuple-element.19.refs_0_) | copy-start | bytes 36868
  18.5 5.1 %copy-start.3 = (f32[8,128,128]{2,1,0:T(8,128)}, f32[8,128,128]{2,1,0:T(8,128)S(1)}, u32[]{:S(2)}) copy-start(f32[8,128,128]{2,1,0:T(8,128)S(1)} %get-tuple-element.20.refs_1_) | copy-start | bytes 1572868
  18.5 13.5 %collective-permute-start.4 = (bf16[2112,128]{1,0:T(8,128)(2,1)S(1)}, bf16[2112,128]{1,0:T(8,128)(2,1)S(1)}, u32[]{:S(2)}, u32[]{:S(2)}) collective-permute-start(bf16[2112,128]{1,0:T(8,128)(2,1)S(1)} %get-tuple-element.24), channel_id=1, source_target_pairs={{0,8},{8,0},{1,9},{9,1},{2,10},{10,2},{3,11},{11,3},{4,12},{12,4},... | collective-permute-start | bytes 1622024 | tf_op jit(solution)/shard_map/ppermute | solution.py:395
  19.9 3.8 %copy-start.10 = (bf16[2112,128]{1,0:T(8,128)(2,1)}, bf16[2112,128]{1,0:T(8,128)(2,1)S(1)}, u32[]{:S(2)}) copy-start(bf16[2112,128]{1,0:T(8,128)(2,1)S(1)} %collective-permute-done.1.refs_7_) | copy-start | bytes 1622020
  19.9 8.5 %collective-permute-start.3 = (bf16[1056,128]{1,0:T(8,128)(2,1)S(1)}, bf16[1056,128]{1,0:T(8,128)(2,1)S(1)}, u32[]{:S(2)}, u32[]{:S(2)}) collective-permute-start(bf16[1056,128]{1,0:T(8,128)(2,1)S(1)} %slice.9), channel_id=1, source_target_pairs={{0,3},{1,0},{2,1},{3,2},{4,7},{5,4},{6,5},{7,6},{8,11},{9,8},{10,9... | collective-permute-start | bytes 811016 | tf_op jit(solution)/shard_map/ppermute | solution.py:392
  23.6 10.4 %copy-start.11 = (bf16[2112,128]{1,0:T(8,128)(2,1)}, bf16[2112,128]{1,0:T(8,128)(2,1)S(1)}, u32[]{:S(2)}) copy-start(bf16[2112,128]{1,0:T(8,128)(2,1)S(1)} %collective-permute-done.refs_6_) | copy-start | bytes 1622020
  23.6 8.5 %collective-permute-start.2 = (bf16[1056,128]{1,0:T(8,128)(2,1)S(1)}, bf16[1056,128]{1,0:T(8,128)(2,1)}, u32[]{:S(2)}, u32[]{:S(2)}) collective-permute-start(bf16[1056,128]{1,0:T(8,128)(2,1)S(1)} %slice.8), channel_id=1, source_target_pairs={{0,1},{1,2},{2,3},{3,0},{4,5},{5,6},{6,7},{7,4},{8,9},{9,10},{10,1... | collective-permute-start | bytes 811016 | tf_op jit(solution)/shard_map/ppermute | solution.py:392
  23.7 8.8 %collective-permute-start.6 = (bf16[2112,128]{1,0:T(8,128)(2,1)S(1)}, bf16[2112,128]{1,0:T(8,128)(2,1)S(1)}, u32[]{:S(2)}, u32[]{:S(2)}) collective-permute-start(bf16[2112,128]{1,0:T(8,128)(2,1)S(1)} %collective-permute-done.1.refs_7_), channel_id=1, source_target_pairs={{0,8},{8,0},{1,9},{9,1},{2,10},{10,2},{3,11},{11,3},{4,12},{12,4},... | collective-permute-start | bytes 1622024 | tf_op jit(solution)/shard_map/ppermute | solution.py:395
  23.8 10.2 %collective-permute-start.5 = (bf16[2112,128]{1,0:T(8,128)(2,1)S(1)}, bf16[2112,128]{1,0:T(8,128)(2,1)}, u32[]{:S(2)}, u32[]{:S(2)}) collective-permute-start(bf16[2112,128]{1,0:T(8,128)(2,1)S(1)} %collective-permute-done.refs_6_), channel_id=1, source_target_pairs={{0,8},{8,0},{1,9},{9,1},{2,10},{10,2},{3,11},{11,3},{4,12},{12,4},... | collective-permute-start | bytes 1622024 | tf_op jit(solution)/shard_map/ppermute | solution.py:395
  28.4 5.5 %copy-start.14 = (bf16[1056,128]{1,0:T(8,128)(2,1)}, bf16[1056,128]{1,0:T(8,128)(2,1)S(1)}, u32[]{:S(2)}) copy-start(bf16[1056,128]{1,0:T(8,128)(2,1)S(1)} %collective-permute-done.3.refs_9_) | copy-start | bytes 811012
  28.4 4.1 %collective-permute-start.8 = (bf16[1056,128]{1,0:T(8,128)(2,1)S(1)}, bf16[1056,128]{1,0:T(8,128)(2,1)}, u32[]{:S(2)}, u32[]{:S(2)}) collective-permute-start(bf16[1056,128]{1,0:T(8,128)(2,1)S(1)} %collective-permute-done.3.refs_9_), channel_id=1, source_target_pairs={{0,8},{8,0},{1,9},{9,1},{2,10},{10,2},{3,11},{11,3},{4,12},{12,4},... | collective-permute-start | bytes 811016 | tf_op jit(solution)/shard_map/ppermute | solution.py:395
  32.1 1.9 %collective-permute-start.7 = (bf16[1056,128]{1,0:T(8,128)(2,1)}, bf16[1056,128]{1,0:T(8,128)(2,1)}, u32[]{:S(2)}, u32[]{:S(2)}) collective-permute-start(bf16[1056,128]{1,0:T(8,128)(2,1)} %collective-permute-done.2.refs_8_), channel_id=1, source_target_pairs={{0,8},{8,0},{1,9},{9,1},{2,10},{10,2},{3,11},{11,3},{4,12},{12,4},... | collective-permute-start | bytes 811016 | tf_op jit(solution)/shard_map/ppermute | solution.py:395
  32.1 1.9 %copy-start.12 = (bf16[2112,128]{1,0:T(8,128)(2,1)}, bf16[2112,128]{1,0:T(8,128)(2,1)S(1)}, u32[]{:S(2)}) copy-start(bf16[2112,128]{1,0:T(8,128)(2,1)S(1)} %collective-permute-done.4.refs_10_) | copy-start | bytes 1622020
  32.5 1.4 %copy-start.9 = (bf16[16,128,256]{2,1,0:T(8,128)(2,1)}, bf16[16,128,256]{2,1,0:T(8,128)(2,1)S(1)}, u32[]{:S(2)}) copy-start(bf16[16,128,256]{2,1,0:T(8,128)(2,1)S(1)} %all-to-all-done.refs_15_) | copy-start | bytes 3145732
  32.5 1.4 %copy-start.13 = (bf16[2112,128]{1,0:T(8,128)(2,1)}, bf16[2112,128]{1,0:T(8,128)(2,1)S(1)}, u32[]{:S(2)}) copy-start(bf16[2112,128]{1,0:T(8,128)(2,1)S(1)} %collective-permute-done.6.refs_12_) | copy-start | bytes 1622020
  70.4 7.2 %collective-permute-start.9 = (bf16[4,1024,128]{2,1,0:T(8,128)(2,1)}, bf16[4,1024,128]{2,1,0:T(8,128)(2,1)S(1)}, u32[]{:S(2)}, u32[]{:S(2)}) collective-permute-start(bf16[4,1024,128]{2,1,0:T(8,128)(2,1)} %get-tuple-element.27), channel_id=1, source_target_pairs={{0,8},{8,0},{1,9},{9,1},{2,10},{10,2},{3,11},{11,3},{4,12},{12,4},... | collective-permute-start | bytes 3145736 | tf_op jit(solution)/shard_map/ppermute | solution.py:395
  70.4 7.2 %copy-start.1 = (bf16[3,1024,128]{2,1,0:T(8,128)(2,1)S(1)}, bf16[3,1024,128]{2,1,0:T(8,128)(2,1)}, u32[]{:S(2)}) copy-start(bf16[3,1024,128]{2,1,0:T(8,128)(2,1)} %get-tuple-element.28.own_ref) | copy-start | bytes 2359300
  70.4 25.8 %all-to-all-start.1 = ((bf16[16,128,256]{2,1,0:T(8,128)(2,1)}), bf16[16,128,256]{2,1,0:T(8,128)(2,1)S(1)}, u32[]{:S(2)}, u32[]{:S(2)}) async-start(bf16[16,128,256]{2,1,0:T(8,128)(2,1)} %get-tuple-element.32), calls=%async_computation.1 | async-start | bytes 2097152 | tf_op jit(solution)/shard_map/all_to_all | solution.py:406
  77.6 18.6 %copy-start.4 = (f32[1024,128]{1,0:T(8,128)S(1)}, f32[1024,128]{1,0:T(8,128)}, u32[]{:S(2)}) copy-start(f32[1024,128]{1,0:T(8,128)} %get-tuple-element.26.own_ref) | copy-start | bytes 1572868
  78.6 17.6 %collective-permute-start.10 = (bf16[1024,128]{1,0:T(8,128)(2,1)}, bf16[1024,128]{1,0:T(8,128)(2,1)S(1)}, u32[]{:S(2)}, u32[]{:S(2)}) collective-permute-start(bf16[1024,128]{1,0:T(8,128)(2,1)} %get-tuple-element.29), channel_id=1, source_target_pairs={{0,3},{1,0},{2,1},{3,2},{4,7},{5,4},{6,5},{7,6},{8,11},{9,8},{10,9... | collective-permute-start | bytes 786440 | tf_op jit(solution)/shard_map/ppermute | solution.py:392
  79.2 17.0 %collective-permute-start.11 = (bf16[1024,128]{1,0:T(8,128)(2,1)}, bf16[1024,128]{1,0:T(8,128)(2,1)S(1)}, u32[]{:S(2)}, u32[]{:S(2)}) collective-permute-start(bf16[1024,128]{1,0:T(8,128)(2,1)} %get-tuple-element.30), channel_id=1, source_target_pairs={{0,1},{1,2},{2,3},{3,0},{4,5},{5,6},{6,7},{7,4},{8,9},{9,10},{10,1... | collective-permute-start | bytes 786440 | tf_op jit(solution)/shard_map/ppermute | solution.py:392
  80.7 15.6 %collective-permute-start.12 = (bf16[1024,128]{1,0:T(8,128)(2,1)}, bf16[1024,128]{1,0:T(8,128)(2,1)S(1)}, u32[]{:S(2)}, u32[]{:S(2)}) collective-permute-start(bf16[1024,128]{1,0:T(8,128)(2,1)} %get-tuple-element.31), channel_id=1, source_target_pairs={{0,2},{1,3},{2,0},{3,1},{4,6},{5,7},{6,4},{7,5},{8,10},{9,11},{10,... | collective-permute-start | bytes 786440 | tf_op jit(solution)/shard_map/ppermute | solution.py:392

commit v4 on v3

--- a/solution.py
+++ b/solution.py
@@ -83,14 +83,22 @@
     ]
     for copy in copies:
         copy.start()
-    for copy in copies:
-        copy.wait()
+    copies[0].wait()
     q_block, k_block = placed(own_index())
     place_q, rank_q = rank_matrices(pos_ref[pl.ds(q_block, 1), :].astype(F32))
     place_k, _ = rank_matrices(pos_ref[pl.ds(k_block, 1), :].astype(F32))
     low_q = place_q.astype(BF16)
     low_k = place_k.astype(BF16)
+    copies[1].wait()
+    copies[2].wait()
+    k_sorted = jnp.dot(low_k, k_ref[...], preferred_element_type=F32).astype(BF16)
+    v_sorted = jnp.dot(low_k, v_ref[...], preferred_element_type=F32).astype(BF16)
+    kv = jnp.concatenate([k_sorted, v_sorted], axis=1)
+    for i in range(16):
+        kv_ref[i] = kv
+    copies[3].wait()
     q_sorted = jnp.dot(low_q, q_ref[...], preferred_element_type=F32).astype(BF16)
+    copies[4].wait()
     g_sorted = jnp.dot(low_q, g_ref[...], preferred_element_type=F32).astype(BF16)
     for h in range(HEADS):
         for band in range(BANDS):
@@ -99,6 +107,8 @@
             cols = slice(h * WIDTH, (h + 1) * WIDTH)
             pay_ref[at : at + BAND, :] = q_sorted[rows, cols]
             pay_ref[HALF + at : HALF + at + BAND, :] = g_sorted[rows, cols]
+    copies[5].wait()
+    copies[6].wait()
     product = g_ref[...].astype(F32) * o_ref[...].astype(F32)
     columns = [
         jnp.sum(product[:, h * WIDTH : (h + 1) * WIDTH], axis=1, keepdims=True)
@@ -114,11 +124,6 @@
     pay_ref[1024:1056, :] = jnp.concatenate([ln_hi, ln_mid, ln_low, fill], axis=0)
     d_hi, d_mid, d_low = split3(pack_rows(-delta, place_q, rank_q))
     pay_ref[HALF + 1024 : HALF + 1056, :] = jnp.concatenate([d_hi, d_mid, d_low, fill], axis=0)
-    k_sorted = jnp.dot(low_k, k_ref[...], preferred_element_type=F32).astype(BF16)
-    v_sorted = jnp.dot(low_k, v_ref[...], preferred_element_type=F32).astype(BF16)
-    kv = jnp.concatenate([k_sorted, v_sorted], axis=1)
-    for i in range(16):
-        kv_ref[i] = kv
 
 
 def prep(q, g, o, ln, k, v, pos):
@@ -144,7 +149,7 @@
     )(q, g, o, ln, k, v, pos)
 
 
-def sorted_kernel(pos_ref, pay_ref, out_ref, copy_ref, qpt, kps, kx, vx):
+def sorted_kernel(pos_ref, pay_ref, seen_ref, copy_ref, qpt, kps, kx, vx):
     ylo, x, core, yhi, z = own_index()
     rows = []
     for key_yhi in range(2):
@@ -164,7 +169,12 @@
         ordered = ordered + jnp.where(
             pltpu.roll(rank, s, 1) == lane, pltpu.roll(pos, s, 1), 0.0
         )
-    out_ref[...] = ordered
+    first = jnp.min(ordered[:KRUNS], axis=0, keepdims=True)
+    last = jnp.max(ordered[KRUNS:], axis=0, keepdims=True)
+    first = jnp.broadcast_to(first, (RUN, RUN)).T
+    starts = lax.broadcasted_iota(jnp.int32, (RUN, RUN), 0) % BAND == 0
+    seen = (starts & (first <= last)).astype(F32)
+    seen_ref[...] = jnp.sum(seen, axis=0, keepdims=True).astype(jnp.int32)
     copy_ref[...] = pay_ref[...]
     query_pos = jnp.concatenate(
         [ordered[KRUNS : KRUNS + QRUNS, :], jnp.zeros((RUN - QRUNS, RUN), F32)], axis=0
@@ -187,7 +197,7 @@
     return pl.pallas_call(
         sorted_kernel,
         out_shape=(
-            jax.ShapeDtypeStruct((KRUNS + QRUNS, RUN), F32),
+            jax.ShapeDtypeStruct((1, RUN), jnp.int32),
             jax.ShapeDtypeStruct(payload.shape, payload.dtype),
             jax.ShapeDtypeStruct((BANDS, QRUNS * BAND, WIDTH), F32),
             jax.ShapeDtypeStruct((BANDS, KROWS), F32),
@@ -200,7 +210,7 @@
 
 
 def main_kernel(*refs):
-    spos, qpt, kps, kx, vx = refs[:5]
+    counts, qpt, kps, kx, vx = refs[:5]
     runs = []
     for core in range(2):
         near, left, right, far_q, far_g = refs[5 + core * 5 : 10 + core * 5]
@@ -287,15 +297,7 @@
         dqs[...] += jnp.dot(grad_scores, key, preferred_element_type=F32)
 
     def query_band(u, carry):
-        last = spos[KRUNS, u * BAND + BAND - 1]
-        for run in range(1, QRUNS):
-            last = jnp.maximum(last, spos[KRUNS + run, u * BAND + BAND - 1])
-        seen = 0
-        for t in range(BANDS):
-            first = spos[0, t * BAND]
-            for run in range(1, KRUNS):
-                first = jnp.minimum(first, spos[run, t * BAND])
-            seen = seen + jnp.where(last >= first, 1, 0)
+        seen = counts[0, u * BAND + BAND - 1]
         dqs[...] = jnp.zeros_like(dqs)
         done = lax.div(seen, MERGE) * MERGE
 
@@ -332,7 +334,7 @@
             dkv_ref[run, rows, WIDTH:] = value_part[run * BAND : (run + 1) * BAND]
 
 
-def main(runs, tables, payloads, kv):
+def main(counts, tables, payloads, kv):
     vmem = pl.BlockSpec(memory_space=pltpu.VMEM)
     return pl.pallas_call(
         main_kernel,
@@ -351,7 +353,7 @@
         ],
         compiler_params=pltpu.CompilerParams(vmem_limit_bytes=56 * 1024 * 1024),
         name="block_grads",
-    )(runs, *tables, *payloads, kv)
+    )(counts, *tables, *payloads, kv)
 
 
 def add_kernel(own_ref, in_ref, *out_refs):
@@ -399,10 +401,10 @@
     far_q = along_z(from_left[:HALF], 1)
     far_g = along_z(from_right[HALF:], 3)
     mine = (payload, from_left, from_right, far_q, far_g)
-    runs, handed, *tables = sort_runs(pos, payload)
+    counts, handed, *tables = sort_runs(pos, payload)
     payloads = mine + (cross(handed),) + tuple(cross(array) for array in mine[1:])
     kv = lax.all_to_all(kv_out, PLANE, 0, 0, tiled=True)
-    dq_near, dq_own, dq_other, dkv = main(runs, tables, payloads, kv)
+    dq_near, dq_own, dq_other, dkv = main(counts, tables, payloads, kv)
     dkv_parts = lax.all_to_all(dkv, PLANE, 0, 0, tiled=True)
     dq_in = cross(dq_other)
     sums = pl.pallas_call(

time: 98 us -> 97.1 us (level)
  no operation moved by 1% of the time
where the time goes in v4:
time: 97.1 us; the launch traced here: 96.5 us
  Pallas kernels  43.2 us (44%)
  waiting for transfers between devices  26.6 us (27%)
  starting transfers between devices  24.1 us (25%)
  local copies, waits for them, and re-layouts  1.87 us (2%)
    pallas_call x1, Pallas kernels, main(): pl.pallas_call(main_kernel, in_specs=[pl.BlockSpec(memory_space=pltpu.SME...  35.9 us
    all_to_all x1, waiting for transfers between devices, shards(): dkv_parts = lax.all_to_all(dkv, PLANE, 0, 0, tiled=True)  15.6 us
    ppermute x7, starting transfers between devices, along_z(): return lax.ppermute(array, 'z', [(i, (i + step) % 4) for i in range(4)])  9.95 us
    ppermute x7, waiting for transfers between devices, along_z(): return lax.ppermute(array, 'z', [(i, (i + step) % 4) for i in range(4)])  9.16 us
    all_to_all x1, starting transfers between devices, shards(): kv = lax.all_to_all(kv_out, PLANE, 0, 0, tiled=True)  7.16 us
    all_to_all x1, starting transfers between devices, shards(): dkv_parts = lax.all_to_all(dkv, PLANE, 0, 0, tiled=True)  6.3 us
    pallas_call x1, Pallas kernels, prep(): pl.pallas_call(prep_kernel, in_specs=[pl.BlockSpec(memory_space=pl.ANY)]...  3.2 us
  transfers between devices with their start and end apart: 15, of which 6 were waited for; matrix products, arithmetic and copies ran while one was open for 0% of the time, Pallas kernels for 3%

profile of v4, /device:TPU:0, one launch (start us, length us, event | category | flops | bytes accessed | tf_op | source)
XLA Modules:
  0.0 96.5 jit_solution(5672393741123202122)
XLA Ops:
  0.6 3.2 %prep.1 = (bf16[2112,128]{1,0:T(8,128)(2,1)}, bf16[16,128,256]{2,1,0:T(8,128)(2,1)}) custom-call(bf16[128,1024]{1,0:T(8,128)(2,1)} %q_hbm.1, bf16[128,1024]{1,0:T(8,128)(2,1)} %g_hbm.1, bf16[128,1024]{1,0:T(8,128)(2,1)} %o_hbm.1, f32[8,128]{1,0:T(8,128)} %ln_hbm.1, bf16[128,128]{1,0:T(8,128)(2,1)} %k_hbm.1, bf16[128,128]{1,0:T(8,128)(2,1)} %v_hbm.1, ...), custom_call_target="tpu_custom_call" | custom-call | tf_op jit(solution)/shard_map/prep/pallas_call | solution.py:130
  3.8 4.2 %collective-permute-start.1 = (bf16[2112,128]{1,0:T(8,128)(2,1)}, bf16[2112,128]{1,0:T(8,128)(2,1)S(1)}, u32[]{:S(2)}, u32[]{:S(2)}) collective-permute-start(bf16[2112,128]{1,0:T(8,128)(2,1)} %get-tuple-element.18.pay_ref.refs_5_), channel_id=1, source_target_pairs={{0,3},{1,0},{2,1},{3,2},{4,7},{5,4},{6,5},{7,6},{8,11},{9,8},{10,9... | collective-permute-start | bytes 1622024 | tf_op jit(solution)/shard_map/ppermute | solution.py:394
  8.0 0.0 collective-permute-start
  8.0 0.0 copy-start
  8.0 0.0 copy-start.2
  8.0 7.2 %all-to-all-start = ((bf16[16,128,256]{2,1,0:T(8,128)(2,1)}), bf16[16,128,256]{2,1,0:T(8,128)(2,1)S(1)}, u32[]{:S(2)}, u32[]{:S(2)}) async-start(bf16[16,128,256]{2,1,0:T(8,128)(2,1)} %get-tuple-element.25), calls=%async_computation | async-start | bytes 2097152 | tf_op jit(solution)/shard_map/all_to_all | solution.py:406
  15.2 0.0 copy-done
  15.2 0.0 copy-done.2
  15.2 1.5 %sort_runs.1 = (s32[1,128]{1,0:T(1,128)S(1)}, bf16[2112,128]{1,0:T(8,128)(2,1)S(1)}, f32[8,128,128]{2,1,0:T(8,128)S(1)}, f32[8,256]{1,0:T(8,128)S(1)}, bf16[8,16...) custom-call(s32[128,128]{1,0:T(8,128)S(1)} %bitcast.2, bf16[2112,128]{1,0:T(8,128)(2,1)S(1)} %copy-done), custom_call_target="tpu_custom_call" | custom-call | tf_op jit(solution)/shard_map/sort_runs/pallas_call | solution.py:197
  16.7 0.0 copy-start.5
  16.7 0.6 copy-done.5
  17.3 0.0 copy-start.6
  17.3 0.6 copy-done.6
  17.9 0.0 copy-start.8
  17.9 0.6 copy-done.8
  18.5 0.0 copy-start.7
  18.5 0.0 collective-permute-start.4
  18.5 1.4 %collective-permute-done.1.refs_7_ = bf16[2112,128]{1,0:T(8,128)(2,1)S(1)} collective-permute-done((bf16[2112,128]{1,0:T(8,128)(2,1)}, bf16[2112,128]{1,0:T(8,128)(2,1)S(1)}, u32[]{:S(2)}, u32[]{:S(2)}) %collective-permute-start.1) | collective-permute-done | bytes 540704 | tf_op jit(solution)/shard_map/ppermute | solution.py:394
  19.9 0.0 copy-start.10
  19.9 0.0 copy-done.7
  19.9 3.7 %collective-permute-start.3 = (bf16[1056,128]{1,0:T(8,128)(2,1)S(1)}, bf16[1056,128]{1,0:T(8,128)(2,1)S(1)}, u32[]{:S(2)}, u32[]{:S(2)}) collective-permute-start(bf16[1056,128]{1,0:T(8,128)(2,1)S(1)} %slice.9), channel_id=1, source_target_pairs={{0,3},{1,0},{2,1},{3,2},{4,7},{5,4},{6,5},{7,6},{8,11},{9,8},{10,9... | collective-permute-start | bytes 811016 | tf_op jit(solution)/shard_map/ppermute | solution.py:394
  23.6 0.0 collective-permute-done.refs_6_
  23.6 0.0 copy-start.11
  23.6 0.0 copy-done.3
  23.6 0.1 collective-permute-start.2
  23.7 0.0 copy-done.10
  23.7 0.1 collective-permute-start.6
  23.8 0.5 collective-permute-start.5
  24.3 4.1 %collective-permute-done.3.refs_9_ = bf16[1056,128]{1,0:T(8,128)(2,1)S(1)} collective-permute-done((bf16[1056,128]{1,0:T(8,128)(2,1)S(1)}, bf16[1056,128]{1,0:T(8,128)(2,1)S(1)}, u32[]{:S(2)}, u32[]{:S(2)}) %collective-permute-start.3) | collective-permute-done | bytes 270368 | tf_op jit(solution)/shard_map/ppermute | solution.py:394
  28.4 0.0 copy-start.14
  28.4 0.0 collective-permute-start.8
  28.4 3.6 %collective-permute-done.2.refs_8_ = bf16[1056,128]{1,0:T(8,128)(2,1)} collective-permute-done((bf16[1056,128]{1,0:T(8,128)(2,1)S(1)}, bf16[1056,128]{1,0:T(8,128)(2,1)}, u32[]{:S(2)}, u32[]{:S(2)}) %collective-permute-start.2) | collective-permute-done | bytes 270368 | tf_op jit(solution)/shard_map/ppermute | solution.py:394
  32.1 0.0 collective-permute-start.7
  32.1 0.0 collective-permute-done.4.refs_10_
  32.1 0.0 copy-start.12
  32.1 0.5 all-to-all-done.refs_15_
  32.5 0.0 copy-start.9
  32.5 0.0 collective-permute-done.8.refs_14_
  32.5 0.0 collective-permute-done.6.refs_12_
  32.5 0.0 copy-start.13
  32.6 1.4 %collective-permute-done.7.refs_13_ = bf16[1056,128]{1,0:T(8,128)(2,1)} collective-permute-done((bf16[1056,128]{1,0:T(8,128)(2,1)}, bf16[1056,128]{1,0:T(8,128)(2,1)}, u32[]{:S(2)}, u32[]{:S(2)}) %collective-permute-start.7) | collective-permute-done | bytes 270368 | tf_op jit(solution)/shard_map/ppermute | solution.py:397
  33.9 0.0 collective-permute-done.5.refs_11_
  34.0 0.0 copy-done.11
  34.0 0.0 copy-done.14
  34.0 0.0 copy-done.12
  34.0 0.0 copy-done.9
  34.0 0.0 copy-done.13
  34.0 35.9 %block_grads.1 = (f32[1024,128]{1,0:T(8,128)}, bf16[3,1024,128]{2,1,0:T(8,128)(2,1)}, bf16[4,1024,128]{2,1,0:T(8,128)(2,1)}, bf16[16,128,256]{2,1,0:T(8,128)(2,1)}) custom-call(s32[1,128]{1,0:T(1,128)} %copy-done.8, f32[8,128,128]{2,1,0:T(8,128)} %copy-done.3, f32[8,256]{1,0:T(8,128)} %copy-done.7, bf16[8,16,128]{2,1,0:T(8,128)(2,1)} %copy-done.5, ...), custom_call_target="tpu_custom_call" | custom-call | tf_op jit(solution)/shard_map/block_grads/pallas_call | solution.py:339
  69.9 0.1 collective-permute-start.9
  69.9 0.0 copy-start.1
  69.9 6.3 %all-to-all-start.1 = ((bf16[16,128,256]{2,1,0:T(8,128)(2,1)}), bf16[16,128,256]{2,1,0:T(8,128)(2,1)S(1)}, u32[]{:S(2)}, u32[]{:S(2)}) async-start(bf16[16,128,256]{2,1,0:T(8,128)(2,1)} %get-tuple-element.32), calls=%async_computation.1 | async-start | bytes 2097152 | tf_op jit(solution)/shard_map/all_to_all | solution.py:408
  76.2 0.0 collective-permute-done.9.in_ref
  76.3 0.0 copy-done.1
  76.3 0.0 copy-start.4
  76.3 1.0 %core_sum.1 = (bf16[1024,128]{1,0:T(8,128)(2,1)}, bf16[1024,128]{1,0:T(8,128)(2,1)}, bf16[1024,128]{1,0:T(8,128)(2,1)}) custom-call(bf16[3,1024,128]{2,1,0:T(8,128)(2,1)S(1)} %copy-done.1, bf16[4,1024,128]{2,1,0:T(8,128)(2,1)S(1)} %collective-permute-done.9.in_ref), custom_call_target="tpu_custom_call" | custom-call | tf_op jit(solution)/shard_map/core_sum/pallas_call | solution.py:410
  77.3 0.1 collective-permute-start.10
  77.4 1.9 %collective-permute-start.11 = (bf16[1024,128]{1,0:T(8,128)(2,1)}, bf16[1024,128]{1,0:T(8,128)(2,1)S(1)}, u32[]{:S(2)}, u32[]{:S(2)}) collective-permute-start(bf16[1024,128]{1,0:T(8,128)(2,1)} %get-tuple-element.30), channel_id=1, source_target_pairs={{0,1},{1,2},{2,3},{3,0},{4,5},{5,6},{6,7},{7,4},{8,9},{9,10},{10,1... | collective-permute-start | bytes 786440 | tf_op jit(solution)/shard_map/ppermute | solution.py:394
  79.3 0.0 collective-permute-start.12
  79.3 15.6 %all-to-all-done.1.parts_ref = bf16[16,128,256]{2,1,0:T(8,128)(2,1)S(1)} async-done(((bf16[16,128,256]{2,1,0:T(8,128)(2,1)}), bf16[16,128,256]{2,1,0:T(8,128)(2,1)S(1)}, u32[]{:S(2)}, u32[]{:S(2)}) %all-to-all-start.1) | async-done | bytes 1048608 | tf_op jit(solution)/shard_map/all_to_all | solution.py:408
  94.9 0.0 collective-permute-done.10.b_ref
  94.9 0.0 collective-permute-done.11.c_ref
  94.9 0.0 collective-permute-done.12.d_ref
  94.9 0.0 copy-done.4
  94.9 1.6 %final_sums.1 = (f32[128,1024]{1,0:T(8,128)}, f32[128,128]{1,0:T(8,128)}, f32[128,128]{1,0:T(8,128)}) custom-call(f32[1024,128]{1,0:T(8,128)S(1)} %copy-done.4, bf16[4,1024,128]{2,1,0:T(8,128)(2,1)S(1)} %collective-permute-done.9.in_ref, bf16[1024,128]{1,0:T(8,128)(2,1)S(1)} %collective-permute-done.10.b_ref, ...), custom_call_target="tpu_custom_call" | custom-call | tf_op jit(solution)/shard_map/final_sums/pallas_call | solution.py:419
  (3 shorter events, 0.0 us)
Async XLA Ops:
  3.8 16.0 %collective-permute-start.1 = (bf16[2112,128]{1,0:T(8,128)(2,1)}, bf16[2112,128]{1,0:T(8,128)(2,1)S(1)}, u32[]{:S(2)}, u32[]{:S(2)}) collective-permute-start(bf16[2112,128]{1,0:T(8,128)(2,1)} %get-tuple-element.18.pay_ref.refs_5_), channel_id=1, source_target_pairs={{0,3},{1,0},{2,1},{3,2},{4,7},{5,4},{6,5},{7,6},{8,11},{9,8},{10,9... | collective-permute-start | bytes 1622024 | tf_op jit(solution)/shard_map/ppermute | solution.py:394
  8.0 15.5 %collective-permute-start = (bf16[2112,128]{1,0:T(8,128)(2,1)}, bf16[2112,128]{1,0:T(8,128)(2,1)S(1)}, u32[]{:S(2)}, u32[]{:S(2)}) collective-permute-start(bf16[2112,128]{1,0:T(8,128)(2,1)} %get-tuple-element.18.pay_ref.refs_5_), channel_id=1, source_target_pairs={{0,1},{1,2},{2,3},{3,0},{4,5},{5,6},{6,7},{7,4},{8,9},{9,10},{10,1... | collective-permute-start | bytes 1622024 | tf_op jit(solution)/shard_map/ppermute | solution.py:394
  8.0 7.2 %copy-start = (bf16[2112,128]{1,0:T(8,128)(2,1)S(1)}, bf16[2112,128]{1,0:T(8,128)(2,1)}, u32[]{:S(2)}) copy-start(bf16[2112,128]{1,0:T(8,128)(2,1)} %get-tuple-element.18.pay_ref.refs_5_) | copy-start | bytes 1622020
  8.0 7.2 %copy-start.2 = (s32[16384]{0:T(1024)S(1)}, s32[16384]{0:T(1024)}, u32[]{:S(2)}) copy-start(s32[16384]{0:T(1024)} %param.13) | copy-start | bytes 196612
  8.0 24.5 %all-to-all-start = ((bf16[16,128,256]{2,1,0:T(8,128)(2,1)}), bf16[16,128,256]{2,1,0:T(8,128)(2,1)S(1)}, u32[]{:S(2)}, u32[]{:S(2)}) async-start(bf16[16,128,256]{2,1,0:T(8,128)(2,1)} %get-tuple-element.25), calls=%async_computation | async-start | bytes 2097152 | tf_op jit(solution)/shard_map/all_to_all | solution.py:406
  16.7 0.6 copy-start.5
  17.3 0.6 copy-start.6
  17.9 0.6 copy-start.8
  18.5 1.4 %copy-start.7 = (f32[8,256]{1,0:T(8,128)}, f32[8,256]{1,0:T(8,128)S(1)}, u32[]{:S(2)}) copy-start(f32[8,256]{1,0:T(8,128)S(1)} %get-tuple-element.21.refs_2_) | copy-start | bytes 24580
  18.5 5.1 %copy-start.3 = (f32[8,128,128]{2,1,0:T(8,128)}, f32[8,128,128]{2,1,0:T(8,128)S(1)}, u32[]{:S(2)}) copy-start(f32[8,128,128]{2,1,0:T(8,128)S(1)} %get-tuple-element.20.refs_1_) | copy-start | bytes 1572868
  18.5 13.6 %collective-permute-start.4 = (bf16[2112,128]{1,0:T(8,128)(2,1)S(1)}, bf16[2112,128]{1,0:T(8,128)(2,1)S(1)}, u32[]{:S(2)}, u32[]{:S(2)}) collective-permute-start(bf16[2112,128]{1,0:T(8,128)(2,1)S(1)} %get-tuple-element.24), channel_id=1, source_target_pairs={{0,8},{8,0},{1,9},{9,1},{2,10},{10,2},{3,11},{11,3},{4,12},{12,4},... | collective-permute-start | bytes 1622024 | tf_op jit(solution)/shard_map/ppermute | solution.py:397
  19.9 3.8 %copy-start.10 = (bf16[2112,128]{1,0:T(8,128)(2,1)}, bf16[2112,128]{1,0:T(8,128)(2,1)S(1)}, u32[]{:S(2)}) copy-start(bf16[2112,128]{1,0:T(8,128)(2,1)S(1)} %collective-permute-done.1.refs_7_) | copy-start | bytes 1622020
  19.9 8.5 %collective-permute-start.3 = (bf16[1056,128]{1,0:T(8,128)(2,1)S(1)}, bf16[1056,128]{1,0:T(8,128)(2,1)S(1)}, u32[]{:S(2)}, u32[]{:S(2)}) collective-permute-start(bf16[1056,128]{1,0:T(8,128)(2,1)S(1)} %slice.9), channel_id=1, source_target_pairs={{0,3},{1,0},{2,1},{3,2},{4,7},{5,4},{6,5},{7,6},{8,11},{9,8},{10,9... | collective-permute-start | bytes 811016 | tf_op jit(solution)/shard_map/ppermute | solution.py:394
  23.6 10.4 %copy-start.11 = (bf16[2112,128]{1,0:T(8,128)(2,1)}, bf16[2112,128]{1,0:T(8,128)(2,1)S(1)}, u32[]{:S(2)}) copy-start(bf16[2112,128]{1,0:T(8,128)(2,1)S(1)} %collective-permute-done.refs_6_) | copy-start | bytes 1622020
  23.6 8.5 %collective-permute-start.2 = (bf16[1056,128]{1,0:T(8,128)(2,1)S(1)}, bf16[1056,128]{1,0:T(8,128)(2,1)}, u32[]{:S(2)}, u32[]{:S(2)}) collective-permute-start(bf16[1056,128]{1,0:T(8,128)(2,1)S(1)} %slice.8), channel_id=1, source_target_pairs={{0,1},{1,2},{2,3},{3,0},{4,5},{5,6},{6,7},{7,4},{8,9},{9,10},{10,1... | collective-permute-start | bytes 811016 | tf_op jit(solution)/shard_map/ppermute | solution.py:394
  23.7 8.8 %collective-permute-start.6 = (bf16[2112,128]{1,0:T(8,128)(2,1)S(1)}, bf16[2112,128]{1,0:T(8,128)(2,1)S(1)}, u32[]{:S(2)}, u32[]{:S(2)}) collective-permute-start(bf16[2112,128]{1,0:T(8,128)(2,1)S(1)} %collective-permute-done.1.refs_7_), channel_id=1, source_target_pairs={{0,8},{8,0},{1,9},{9,1},{2,10},{10,2},{3,11},{11,3},{4,12},{12,4},... | collective-permute-start | bytes 1622024 | tf_op jit(solution)/shard_map/ppermute | solution.py:397
  23.8 10.2 %collective-permute-start.5 = (bf16[2112,128]{1,0:T(8,128)(2,1)S(1)}, bf16[2112,128]{1,0:T(8,128)(2,1)}, u32[]{:S(2)}, u32[]{:S(2)}) collective-permute-start(bf16[2112,128]{1,0:T(8,128)(2,1)S(1)} %collective-permute-done.refs_6_), channel_id=1, source_target_pairs={{0,8},{8,0},{1,9},{9,1},{2,10},{10,2},{3,11},{11,3},{4,12},{12,4},... | collective-permute-start | bytes 1622024 | tf_op jit(solution)/shard_map/ppermute | solution.py:397
  28.4 5.5 %copy-start.14 = (bf16[1056,128]{1,0:T(8,128)(2,1)}, bf16[1056,128]{1,0:T(8,128)(2,1)S(1)}, u32[]{:S(2)}) copy-start(bf16[1056,128]{1,0:T(8,128)(2,1)S(1)} %collective-permute-done.3.refs_9_) | copy-start | bytes 811012
  28.4 4.1 %collective-permute-start.8 = (bf16[1056,128]{1,0:T(8,128)(2,1)S(1)}, bf16[1056,128]{1,0:T(8,128)(2,1)}, u32[]{:S(2)}, u32[]{:S(2)}) collective-permute-start(bf16[1056,128]{1,0:T(8,128)(2,1)S(1)} %collective-permute-done.3.refs_9_), channel_id=1, source_target_pairs={{0,8},{8,0},{1,9},{9,1},{2,10},{10,2},{3,11},{11,3},{4,12},{12,4},... | collective-permute-start | bytes 811016 | tf_op jit(solution)/shard_map/ppermute | solution.py:397
  32.1 1.9 %collective-permute-start.7 = (bf16[1056,128]{1,0:T(8,128)(2,1)}, bf16[1056,128]{1,0:T(8,128)(2,1)}, u32[]{:S(2)}, u32[]{:S(2)}) collective-permute-start(bf16[1056,128]{1,0:T(8,128)(2,1)} %collective-permute-done.2.refs_8_), channel_id=1, source_target_pairs={{0,8},{8,0},{1,9},{9,1},{2,10},{10,2},{3,11},{11,3},{4,12},{12,4},... | collective-permute-start | bytes 811016 | tf_op jit(solution)/shard_map/ppermute | solution.py:397
  32.1 1.9 %copy-start.12 = (bf16[2112,128]{1,0:T(8,128)(2,1)}, bf16[2112,128]{1,0:T(8,128)(2,1)S(1)}, u32[]{:S(2)}) copy-start(bf16[2112,128]{1,0:T(8,128)(2,1)S(1)} %collective-permute-done.4.refs_10_) | copy-start | bytes 1622020
  32.5 1.4 %copy-start.9 = (bf16[16,128,256]{2,1,0:T(8,128)(2,1)}, bf16[16,128,256]{2,1,0:T(8,128)(2,1)S(1)}, u32[]{:S(2)}) copy-start(bf16[16,128,256]{2,1,0:T(8,128)(2,1)S(1)} %all-to-all-done.refs_15_) | copy-start | bytes 3145732
  32.5 1.4 %copy-start.13 = (bf16[2112,128]{1,0:T(8,128)(2,1)}, bf16[2112,128]{1,0:T(8,128)(2,1)S(1)}, u32[]{:S(2)}) copy-start(bf16[2112,128]{1,0:T(8,128)(2,1)S(1)} %collective-permute-done.6.refs_12_) | copy-start | bytes 1622020
  69.9 6.4 %collective-permute-start.9 = (bf16[4,1024,128]{2,1,0:T(8,128)(2,1)}, bf16[4,1024,128]{2,1,0:T(8,128)(2,1)S(1)}, u32[]{:S(2)}, u32[]{:S(2)}) collective-permute-start(bf16[4,1024,128]{2,1,0:T(8,128)(2,1)} %get-tuple-element.27), channel_id=1, source_target_pairs={{0,8},{8,0},{1,9},{9,1},{2,10},{10,2},{3,11},{11,3},{4,12},{12,4},... | collective-permute-start | bytes 3145736 | tf_op jit(solution)/shard_map/ppermute | solution.py:397
  69.9 6.3 %copy-start.1 = (bf16[3,1024,128]{2,1,0:T(8,128)(2,1)S(1)}, bf16[3,1024,128]{2,1,0:T(8,128)(2,1)}, u32[]{:S(2)}) copy-start(bf16[3,1024,128]{2,1,0:T(8,128)(2,1)} %get-tuple-element.28.own_ref) | copy-start | bytes 2359300
  69.9 24.9 %all-to-all-start.1 = ((bf16[16,128,256]{2,1,0:T(8,128)(2,1)}), bf16[16,128,256]{2,1,0:T(8,128)(2,1)S(1)}, u32[]{:S(2)}, u32[]{:S(2)}) async-start(bf16[16,128,256]{2,1,0:T(8,128)(2,1)} %get-tuple-element.32), calls=%async_computation.1 | async-start | bytes 2097152 | tf_op jit(solution)/shard_map/all_to_all | solution.py:408
  76.3 18.6 %copy-start.4 = (f32[1024,128]{1,0:T(8,128)S(1)}, f32[1024,128]{1,0:T(8,128)}, u32[]{:S(2)}) copy-start(f32[1024,128]{1,0:T(8,128)} %get-tuple-element.26.own_ref) | copy-start | bytes 1572868
  77.3 17.6 %collective-permute-start.10 = (bf16[1024,128]{1,0:T(8,128)(2,1)}, bf16[1024,128]{1,0:T(8,128)(2,1)S(1)}, u32[]{:S(2)}, u32[]{:S(2)}) collective-permute-start(bf16[1024,128]{1,0:T(8,128)(2,1)} %get-tuple-element.29), channel_id=1, source_target_pairs={{0,3},{1,0},{2,1},{3,2},{4,7},{5,4},{6,5},{7,6},{8,11},{9,8},{10,9... | collective-permute-start | bytes 786440 | tf_op jit(solution)/shard_map/ppermute | solution.py:394
  77.4 17.5 %collective-permute-start.11 = (bf16[1024,128]{1,0:T(8,128)(2,1)}, bf16[1024,128]{1,0:T(8,128)(2,1)S(1)}, u32[]{:S(2)}, u32[]{:S(2)}) collective-permute-start(bf16[1024,128]{1,0:T(8,128)(2,1)} %get-tuple-element.30), channel_id=1, source_target_pairs={{0,1},{1,2},{2,3},{3,0},{4,5},{5,6},{6,7},{7,4},{8,9},{9,10},{10,1... | collective-permute-start | bytes 786440 | tf_op jit(solution)/shard_map/ppermute | solution.py:394
  79.3 15.6 %collective-permute-start.12 = (bf16[1024,128]{1,0:T(8,128)(2,1)}, bf16[1024,128]{1,0:T(8,128)(2,1)S(1)}, u32[]{:S(2)}, u32[]{:S(2)}) collective-permute-start(bf16[1024,128]{1,0:T(8,128)(2,1)} %get-tuple-element.31), channel_id=1, source_target_pairs={{0,2},{1,3},{2,0},{3,1},{4,6},{5,7},{6,4},{7,5},{8,10},{9,11},{10,... | collective-permute-start | bytes 786440 | tf_op jit(solution)/shard_map/ppermute | solution.py:394

commit v5 on v4

--- a/solution.py
+++ b/solution.py
@@ -51,13 +51,21 @@
     ordered = lax.dot_general(
         values, place, (((1,), (1,)), ((), ())), precision=HIGH, preferred_element_type=F32
     )
-    pieces = []
-    for band in range(BANDS):
-        row = jnp.concatenate(
-            [ordered[h : h + 1, band * BAND : (band + 1) * BAND] for h in range(HEADS)], axis=1
-        )
-        pieces.append(row)
-    return jnp.concatenate(pieces, axis=0)
+    row = lax.broadcasted_iota(jnp.int32, (BANDS, RUN), 0)
+    piece = lax.broadcasted_iota(jnp.int32, (BANDS, RUN), 1) // BAND
+    turned = jnp.zeros((BANDS, RUN), F32)
+    for s in range(BANDS):
+        moved = ordered if s == 0 else pltpu.roll(pltpu.roll(ordered, BAND * s, 1), BANDS - s, 0)
+        turned = jnp.where(piece == (row + s) % BANDS, moved, turned)
+    return turned
+
+
+def unsort(place, rows):
+    back = place.T.astype(BF16)
+    low, mid, high = (
+        jnp.dot(back, part, preferred_element_type=F32) for part in split3(rows)[::-1]
+    )
+    return (low + mid) + high
 
 
 def placed(index):
@@ -327,8 +335,8 @@
     lax.fori_loop(0, BANDS, query_band, 0)
     for band in range(BANDS):
         rows = slice(band * BAND, (band + 1) * BAND)
-        key_part = (dks[band] * INV_ROOT).T.astype(BF16)
-        value_part = dvs[band].T.astype(BF16)
+        key_part = (dks[band] * INV_ROOT).astype(BF16).T
+        value_part = dvs[band].astype(BF16).T
         for run in range(KRUNS):
             dkv_ref[run, rows, :WIDTH] = key_part[run * BAND : (run + 1) * BAND]
             dkv_ref[run, rows, WIDTH:] = value_part[run * BAND : (run + 1) * BAND]
@@ -370,18 +378,14 @@
     for ref in (b_ref, c_ref, d_ref):
         total = total + ref[...].astype(F32)
     total = total.reshape(BANDS, HEADS, BAND, WIDTH)
-    for h in range(HEADS):
-        dq_ref[:, h * WIDTH : (h + 1) * WIDTH] = lax.dot_general(
-            place, total[:, h].reshape(RUN, WIDTH), (((0,), (0,)), ((), ())),
-            precision=HIGH, preferred_element_type=F32,
-        )
+    dq_ref[...] = unsort(
+        place, jnp.concatenate([total[:, h].reshape(RUN, WIDTH) for h in range(HEADS)], axis=1)
+    )
     place, _ = rank_matrices(pos_ref[pl.ds(k_block, 1), :].astype(F32))
     total = parts_ref[0].astype(F32)
     for i in range(1, 16):
         total = total + parts_ref[i].astype(F32)
-    result = lax.dot_general(
-        place, total, (((0,), (0,)), ((), ())), precision=HIGH, preferred_element_type=F32
-    )
+    result = unsort(place, total)
     dk_ref[...] = result[:, :WIDTH]
     dv_ref[...] = result[:, WIDTH:]
 

time: 97.1 us -> 98.1 us (1.010)
  starting transfers between devices: 24.1 us -> 26.4 us
    all_to_all x1, starting transfers between devices: 6.3 us -> 8.49 us  [shards(): dkv_parts = lax.all_to_all(dkv, PLANE, 0, 0, tiled=True)]
where the time goes in v5:
time: 98.1 us; the launch traced here: 97.7 us
  Pallas kernels  42.3 us (43%)
  starting transfers between devices  26.4 us (27%)
  waiting for transfers between devices  26.4 us (27%)
  local copies, waits for them, and re-layouts  1.87 us (2%)
    pallas_call x1, Pallas kernels, main(): pl.pallas_call(main_kernel, in_specs=[pl.BlockSpec(memory_space=pltpu.SME...  35.1 us
    all_to_all x1, waiting for transfers between devices, shards(): dkv_parts = lax.all_to_all(dkv, PLANE, 0, 0, tiled=True)  15.4 us
    ppermute x7, starting transfers between devices, along_z(): return lax.ppermute(array, 'z', [(i, (i + step) % 4) for i in range(4)])  10.1 us
    ppermute x7, waiting for transfers between devices, along_z(): return lax.ppermute(array, 'z', [(i, (i + step) % 4) for i in range(4)])  9.15 us
    all_to_all x1, starting transfers between devices, shards(): dkv_parts = lax.all_to_all(dkv, PLANE, 0, 0, tiled=True)  8.49 us
    all_to_all x1, starting transfers between devices, shards(): kv = lax.all_to_all(kv_out, PLANE, 0, 0, tiled=True)  7.17 us
    pallas_call x1, Pallas kernels, prep(): pl.pallas_call(prep_kernel, in_specs=[pl.BlockSpec(memory_space=pl.ANY)]...  3.15 us
  transfers between devices with their start and end apart: 15, of which 6 were waited for; matrix products, arithmetic and copies ran while one was open for 0% of the time, Pallas kernels for 3%

profile of v5, /device:TPU:0, one launch (start us, length us, event | category | flops | bytes accessed | tf_op | source)
XLA Modules:
  0.0 97.7 jit_solution(5144407294206927023)
XLA Ops:
  0.6 3.1 %prep.1 = (bf16[2112,128]{1,0:T(8,128)(2,1)}, bf16[16,128,256]{2,1,0:T(8,128)(2,1)}) custom-call(bf16[128,1024]{1,0:T(8,128)(2,1)} %q_hbm.1, bf16[128,1024]{1,0:T(8,128)(2,1)} %g_hbm.1, bf16[128,1024]{1,0:T(8,128)(2,1)} %o_hbm.1, f32[8,128]{1,0:T(8,128)} %ln_hbm.1, bf16[128,128]{1,0:T(8,128)(2,1)} %k_hbm.1, bf16[128,128]{1,0:T(8,128)(2,1)} %v_hbm.1, ...), custom_call_target="tpu_custom_call" | custom-call | tf_op jit(solution)/shard_map/prep/pallas_call | solution.py:138
  3.8 4.2 %collective-permute-start.1 = (bf16[2112,128]{1,0:T(8,128)(2,1)}, bf16[2112,128]{1,0:T(8,128)(2,1)S(1)}, u32[]{:S(2)}, u32[]{:S(2)}) collective-permute-start(bf16[2112,128]{1,0:T(8,128)(2,1)} %get-tuple-element.18.pay_ref.refs_5_), channel_id=1, source_target_pairs={{0,3},{1,0},{2,1},{3,2},{4,7},{5,4},{6,5},{7,6},{8,11},{9,8},{10,9... | collective-permute-start | bytes 1622024 | tf_op jit(solution)/shard_map/ppermute | solution.py:398
  8.0 0.0 collective-permute-start
  8.0 0.0 copy-start
  8.0 0.0 copy-start.2
  8.0 7.2 %all-to-all-start = ((bf16[16,128,256]{2,1,0:T(8,128)(2,1)}), bf16[16,128,256]{2,1,0:T(8,128)(2,1)S(1)}, u32[]{:S(2)}, u32[]{:S(2)}) async-start(bf16[16,128,256]{2,1,0:T(8,128)(2,1)} %get-tuple-element.25), calls=%async_computation | async-start | bytes 2097152 | tf_op jit(solution)/shard_map/all_to_all | solution.py:410
  15.2 0.0 copy-done
  15.2 0.0 copy-done.2
  15.2 1.5 %sort_runs.1 = (s32[1,128]{1,0:T(1,128)S(1)}, bf16[2112,128]{1,0:T(8,128)(2,1)S(1)}, f32[8,128,128]{2,1,0:T(8,128)S(1)}, f32[8,256]{1,0:T(8,128)S(1)}, bf16[8,16...) custom-call(s32[128,128]{1,0:T(8,128)S(1)} %bitcast.2, bf16[2112,128]{1,0:T(8,128)(2,1)S(1)} %copy-done), custom_call_target="tpu_custom_call" | custom-call | tf_op jit(solution)/shard_map/sort_runs/pallas_call | solution.py:205
  16.7 0.0 copy-start.5
  16.7 0.6 copy-done.5
  17.3 0.0 copy-start.6
  17.3 0.6 copy-done.6
  17.9 0.0 copy-start.8
  17.9 0.6 copy-done.8
  18.4 0.0 copy-start.7
  18.5 0.0 copy-start.3
  18.5 0.0 collective-permute-start.4
  18.5 1.4 %collective-permute-done.1.refs_7_ = bf16[2112,128]{1,0:T(8,128)(2,1)S(1)} collective-permute-done((bf16[2112,128]{1,0:T(8,128)(2,1)}, bf16[2112,128]{1,0:T(8,128)(2,1)S(1)}, u32[]{:S(2)}, u32[]{:S(2)}) %collective-permute-start.1) | collective-permute-done | bytes 540704 | tf_op jit(solution)/shard_map/ppermute | solution.py:398
  19.8 0.0 copy-start.10
  19.9 0.0 copy-done.7
  19.9 3.7 %collective-permute-start.3 = (bf16[1056,128]{1,0:T(8,128)(2,1)S(1)}, bf16[1056,128]{1,0:T(8,128)(2,1)S(1)}, u32[]{:S(2)}, u32[]{:S(2)}) collective-permute-start(bf16[1056,128]{1,0:T(8,128)(2,1)S(1)} %slice.9), channel_id=1, source_target_pairs={{0,3},{1,0},{2,1},{3,2},{4,7},{5,4},{6,5},{7,6},{8,11},{9,8},{10,9... | collective-permute-start | bytes 811016 | tf_op jit(solution)/shard_map/ppermute | solution.py:398
  23.5 0.0 collective-permute-done.refs_6_
  23.5 0.0 copy-start.11
  23.5 0.0 copy-done.3
  23.6 0.1 collective-permute-start.2
  23.6 0.0 copy-done.10
  23.6 0.1 collective-permute-start.6
  23.7 0.5 collective-permute-start.5
  24.2 4.1 %collective-permute-done.3.refs_9_ = bf16[1056,128]{1,0:T(8,128)(2,1)S(1)} collective-permute-done((bf16[1056,128]{1,0:T(8,128)(2,1)S(1)}, bf16[1056,128]{1,0:T(8,128)(2,1)S(1)}, u32[]{:S(2)}, u32[]{:S(2)}) %collective-permute-start.3) | collective-permute-done | bytes 270368 | tf_op jit(solution)/shard_map/ppermute | solution.py:398
  28.4 0.0 copy-start.14
  28.4 0.0 collective-permute-start.8
  28.4 3.6 %collective-permute-done.2.refs_8_ = bf16[1056,128]{1,0:T(8,128)(2,1)} collective-permute-done((bf16[1056,128]{1,0:T(8,128)(2,1)S(1)}, bf16[1056,128]{1,0:T(8,128)(2,1)}, u32[]{:S(2)}, u32[]{:S(2)}) %collective-permute-start.2) | collective-permute-done | bytes 270368 | tf_op jit(solution)/shard_map/ppermute | solution.py:398
  32.0 0.0 collective-permute-start.7
  32.0 0.0 collective-permute-done.4.refs_10_
  32.0 0.0 copy-start.12
  32.0 0.5 all-to-all-done.refs_15_
  32.5 0.0 collective-permute-done.8.refs_14_
  32.5 0.0 collective-permute-done.6.refs_12_
  32.5 0.0 copy-start.13
  32.5 1.4 %collective-permute-done.7.refs_13_ = bf16[1056,128]{1,0:T(8,128)(2,1)} collective-permute-done((bf16[1056,128]{1,0:T(8,128)(2,1)}, bf16[1056,128]{1,0:T(8,128)(2,1)}, u32[]{:S(2)}, u32[]{:S(2)}) %collective-permute-start.7) | collective-permute-done | bytes 270368 | tf_op jit(solution)/shard_map/ppermute | solution.py:401
  33.9 0.0 collective-permute-done.5.refs_11_
  33.9 0.0 copy-done.11
  33.9 0.0 copy-done.14
  33.9 0.0 copy-done.12
  33.9 0.0 copy-done.9
  33.9 0.0 copy-done.13
  33.9 35.1 %block_grads.1 = (f32[1024,128]{1,0:T(8,128)}, bf16[3,1024,128]{2,1,0:T(8,128)(2,1)}, bf16[4,1024,128]{2,1,0:T(8,128)(2,1)}, bf16[16,128,256]{2,1,0:T(8,128)(2,1)}) custom-call(s32[1,128]{1,0:T(1,128)} %copy-done.8, f32[8,128,128]{2,1,0:T(8,128)} %copy-done.3, f32[8,256]{1,0:T(8,128)} %copy-done.7, bf16[8,16,128]{2,1,0:T(8,128)(2,1)} %copy-done.5, ...), custom_call_target="tpu_custom_call" | custom-call | tf_op jit(solution)/shard_map/block_grads/pallas_call | solution.py:347
  69.1 0.0 collective-permute-start.9
  69.1 0.0 copy-start.1
  69.1 8.5 %all-to-all-start.1 = ((bf16[16,128,256]{2,1,0:T(8,128)(2,1)}), bf16[16,128,256]{2,1,0:T(8,128)(2,1)S(1)}, u32[]{:S(2)}, u32[]{:S(2)}) async-start(bf16[16,128,256]{2,1,0:T(8,128)(2,1)} %get-tuple-element.32), calls=%async_computation.1 | async-start | bytes 2097152 | tf_op jit(solution)/shard_map/all_to_all | solution.py:412
  77.6 0.0 collective-permute-done.9.in_ref
  77.6 0.0 copy-done.1
  77.6 0.0 copy-start.4
  77.6 1.0 %core_sum.1 = (bf16[1024,128]{1,0:T(8,128)(2,1)}, bf16[1024,128]{1,0:T(8,128)(2,1)}, bf16[1024,128]{1,0:T(8,128)(2,1)}) custom-call(bf16[3,1024,128]{2,1,0:T(8,128)(2,1)S(1)} %copy-done.1, bf16[4,1024,128]{2,1,0:T(8,128)(2,1)S(1)} %collective-permute-done.9.in_ref), custom_call_target="tpu_custom_call" | custom-call | tf_op jit(solution)/shard_map/core_sum/pallas_call | solution.py:414
  78.6 0.8 collective-permute-start.10
  79.4 1.3 %collective-permute-start.11 = (bf16[1024,128]{1,0:T(8,128)(2,1)}, bf16[1024,128]{1,0:T(8,128)(2,1)S(1)}, u32[]{:S(2)}, u32[]{:S(2)}) collective-permute-start(bf16[1024,128]{1,0:T(8,128)(2,1)} %get-tuple-element.30), channel_id=1, source_target_pairs={{0,1},{1,2},{2,3},{3,0},{4,5},{5,6},{6,7},{7,4},{8,9},{9,10},{10,1... | collective-permute-start | bytes 786440 | tf_op jit(solution)/shard_map/ppermute | solution.py:398
  80.6 0.2 collective-permute-start.12
  80.8 15.4 %all-to-all-done.1.parts_ref = bf16[16,128,256]{2,1,0:T(8,128)(2,1)S(1)} async-done(((bf16[16,128,256]{2,1,0:T(8,128)(2,1)}), bf16[16,128,256]{2,1,0:T(8,128)(2,1)S(1)}, u32[]{:S(2)}, u32[]{:S(2)}) %all-to-all-start.1) | async-done | bytes 1048608 | tf_op jit(solution)/shard_map/all_to_all | solution.py:412
  96.2 0.0 collective-permute-done.10.b_ref
  96.2 0.0 collective-permute-done.11.c_ref
  96.2 0.0 collective-permute-done.12.d_ref
  96.2 0.0 copy-done.4
  96.2 1.5 %final_sums.1 = (f32[128,1024]{1,0:T(8,128)}, f32[128,128]{1,0:T(8,128)}, f32[128,128]{1,0:T(8,128)}) custom-call(f32[1024,128]{1,0:T(8,128)S(1)} %copy-done.4, bf16[4,1024,128]{2,1,0:T(8,128)(2,1)S(1)} %collective-permute-done.9.in_ref, bf16[1024,128]{1,0:T(8,128)(2,1)S(1)} %collective-permute-done.10.b_ref, ...), custom_call_target="tpu_custom_call" | custom-call | tf_op jit(solution)/shard_map/final_sums/pallas_call | solution.py:423
  (3 shorter events, 0.0 us)
Async XLA Ops:
  3.8 16.0 %collective-permute-start.1 = (bf16[2112,128]{1,0:T(8,128)(2,1)}, bf16[2112,128]{1,0:T(8,128)(2,1)S(1)}, u32[]{:S(2)}, u32[]{:S(2)}) collective-permute-start(bf16[2112,128]{1,0:T(8,128)(2,1)} %get-tuple-element.18.pay_ref.refs_5_), channel_id=1, source_target_pairs={{0,3},{1,0},{2,1},{3,2},{4,7},{5,4},{6,5},{7,6},{8,11},{9,8},{10,9... | collective-permute-start | bytes 1622024 | tf_op jit(solution)/shard_map/ppermute | solution.py:398
  8.0 15.5 %collective-permute-start = (bf16[2112,128]{1,0:T(8,128)(2,1)}, bf16[2112,128]{1,0:T(8,128)(2,1)S(1)}, u32[]{:S(2)}, u32[]{:S(2)}) collective-permute-start(bf16[2112,128]{1,0:T(8,128)(2,1)} %get-tuple-element.18.pay_ref.refs_5_), channel_id=1, source_target_pairs={{0,1},{1,2},{2,3},{3,0},{4,5},{5,6},{6,7},{7,4},{8,9},{9,10},{10,1... | collective-permute-start | bytes 1622024 | tf_op jit(solution)/shard_map/ppermute | solution.py:398
  8.0 7.2 %copy-start = (bf16[2112,128]{1,0:T(8,128)(2,1)S(1)}, bf16[2112,128]{1,0:T(8,128)(2,1)}, u32[]{:S(2)}) copy-start(bf16[2112,128]{1,0:T(8,128)(2,1)} %get-tuple-element.18.pay_ref.refs_5_) | copy-start | bytes 1622020
  8.0 7.2 %copy-start.2 = (s32[16384]{0:T(1024)S(1)}, s32[16384]{0:T(1024)}, u32[]{:S(2)}) copy-start(s32[16384]{0:T(1024)} %param.13) | copy-start | bytes 196612
  8.0 24.5 %all-to-all-start = ((bf16[16,128,256]{2,1,0:T(8,128)(2,1)}), bf16[16,128,256]{2,1,0:T(8,128)(2,1)S(1)}, u32[]{:S(2)}, u32[]{:S(2)}) async-start(bf16[16,128,256]{2,1,0:T(8,128)(2,1)} %get-tuple-element.25), calls=%async_computation | async-start | bytes 2097152 | tf_op jit(solution)/shard_map/all_to_all | solution.py:410
  16.7 0.6 copy-start.5
  17.3 0.6 copy-start.6
  17.9 0.6 copy-start.8
  18.4 1.4 %copy-start.7 = (f32[8,256]{1,0:T(8,128)}, f32[8,256]{1,0:T(8,128)S(1)}, u32[]{:S(2)}) copy-start(f32[8,256]{1,0:T(8,128)S(1)} %get-tuple-element.21.refs_2_) | copy-start | bytes 24580
  18.5 5.1 %copy-start.3 = (f32[8,128,128]{2,1,0:T(8,128)}, f32[8,128,128]{2,1,0:T(8,128)S(1)}, u32[]{:S(2)}) copy-start(f32[8,128,128]{2,1,0:T(8,128)S(1)} %get-tuple-element.20.refs_1_) | copy-start | bytes 1572868
  18.5 13.6 %collective-permute-start.4 = (bf16[2112,128]{1,0:T(8,128)(2,1)S(1)}, bf16[2112,128]{1,0:T(8,128)(2,1)S(1)}, u32[]{:S(2)}, u32[]{:S(2)}) collective-permute-start(bf16[2112,128]{1,0:T(8,128)(2,1)S(1)} %get-tuple-element.24), channel_id=1, source_target_pairs={{0,8},{8,0},{1,9},{9,1},{2,10},{10,2},{3,11},{11,3},{4,12},{12,4},... | collective-permute-start | bytes 1622024 | tf_op jit(solution)/shard_map/ppermute | solution.py:401
  19.8 3.8 %copy-start.10 = (bf16[2112,128]{1,0:T(8,128)(2,1)}, bf16[2112,128]{1,0:T(8,128)(2,1)S(1)}, u32[]{:S(2)}) copy-start(bf16[2112,128]{1,0:T(8,128)(2,1)S(1)} %collective-permute-done.1.refs_7_) | copy-start | bytes 1622020
  19.9 8.5 %collective-permute-start.3 = (bf16[1056,128]{1,0:T(8,128)(2,1)S(1)}, bf16[1056,128]{1,0:T(8,128)(2,1)S(1)}, u32[]{:S(2)}, u32[]{:S(2)}) collective-permute-start(bf16[1056,128]{1,0:T(8,128)(2,1)S(1)} %slice.9), channel_id=1, source_target_pairs={{0,3},{1,0},{2,1},{3,2},{4,7},{5,4},{6,5},{7,6},{8,11},{9,8},{10,9... | collective-permute-start | bytes 811016 | tf_op jit(solution)/shard_map/ppermute | solution.py:398
  23.5 10.4 %copy-start.11 = (bf16[2112,128]{1,0:T(8,128)(2,1)}, bf16[2112,128]{1,0:T(8,128)(2,1)S(1)}, u32[]{:S(2)}) copy-start(bf16[2112,128]{1,0:T(8,128)(2,1)S(1)} %collective-permute-done.refs_6_) | copy-start | bytes 1622020
  23.6 8.5 %collective-permute-start.2 = (bf16[1056,128]{1,0:T(8,128)(2,1)S(1)}, bf16[1056,128]{1,0:T(8,128)(2,1)}, u32[]{:S(2)}, u32[]{:S(2)}) collective-permute-start(bf16[1056,128]{1,0:T(8,128)(2,1)S(1)} %slice.8), channel_id=1, source_target_pairs={{0,1},{1,2},{2,3},{3,0},{4,5},{5,6},{6,7},{7,4},{8,9},{9,10},{10,1... | collective-permute-start | bytes 811016 | tf_op jit(solution)/shard_map/ppermute | solution.py:398
  23.6 8.8 %collective-permute-start.6 = (bf16[2112,128]{1,0:T(8,128)(2,1)S(1)}, bf16[2112,128]{1,0:T(8,128)(2,1)S(1)}, u32[]{:S(2)}, u32[]{:S(2)}) collective-permute-start(bf16[2112,128]{1,0:T(8,128)(2,1)S(1)} %collective-permute-done.1.refs_7_), channel_id=1, source_target_pairs={{0,8},{8,0},{1,9},{9,1},{2,10},{10,2},{3,11},{11,3},{4,12},{12,4},... | collective-permute-start | bytes 1622024 | tf_op jit(solution)/shard_map/ppermute | solution.py:401
  23.7 10.2 %collective-permute-start.5 = (bf16[2112,128]{1,0:T(8,128)(2,1)S(1)}, bf16[2112,128]{1,0:T(8,128)(2,1)}, u32[]{:S(2)}, u32[]{:S(2)}) collective-permute-start(bf16[2112,128]{1,0:T(8,128)(2,1)S(1)} %collective-permute-done.refs_6_), channel_id=1, source_target_pairs={{0,8},{8,0},{1,9},{9,1},{2,10},{10,2},{3,11},{11,3},{4,12},{12,4},... | collective-permute-start | bytes 1622024 | tf_op jit(solution)/shard_map/ppermute | solution.py:401
  28.4 5.5 %copy-start.14 = (bf16[1056,128]{1,0:T(8,128)(2,1)}, bf16[1056,128]{1,0:T(8,128)(2,1)S(1)}, u32[]{:S(2)}) copy-start(bf16[1056,128]{1,0:T(8,128)(2,1)S(1)} %collective-permute-done.3.refs_9_) | copy-start | bytes 811012
  28.4 4.1 %collective-permute-start.8 = (bf16[1056,128]{1,0:T(8,128)(2,1)S(1)}, bf16[1056,128]{1,0:T(8,128)(2,1)}, u32[]{:S(2)}, u32[]{:S(2)}) collective-permute-start(bf16[1056,128]{1,0:T(8,128)(2,1)S(1)} %collective-permute-done.3.refs_9_), channel_id=1, source_target_pairs={{0,8},{8,0},{1,9},{9,1},{2,10},{10,2},{3,11},{11,3},{4,12},{12,4},... | collective-permute-start | bytes 811016 | tf_op jit(solution)/shard_map/ppermute | solution.py:401
  32.0 1.9 %collective-permute-start.7 = (bf16[1056,128]{1,0:T(8,128)(2,1)}, bf16[1056,128]{1,0:T(8,128)(2,1)}, u32[]{:S(2)}, u32[]{:S(2)}) collective-permute-start(bf16[1056,128]{1,0:T(8,128)(2,1)} %collective-permute-done.2.refs_8_), channel_id=1, source_target_pairs={{0,8},{8,0},{1,9},{9,1},{2,10},{10,2},{3,11},{11,3},{4,12},{12,4},... | collective-permute-start | bytes 811016 | tf_op jit(solution)/shard_map/ppermute | solution.py:401
  32.0 1.9 %copy-start.12 = (bf16[2112,128]{1,0:T(8,128)(2,1)}, bf16[2112,128]{1,0:T(8,128)(2,1)S(1)}, u32[]{:S(2)}) copy-start(bf16[2112,128]{1,0:T(8,128)(2,1)S(1)} %collective-permute-done.4.refs_10_) | copy-start | bytes 1622020
  32.5 1.4 %copy-start.9 = (bf16[16,128,256]{2,1,0:T(8,128)(2,1)}, bf16[16,128,256]{2,1,0:T(8,128)(2,1)S(1)}, u32[]{:S(2)}) copy-start(bf16[16,128,256]{2,1,0:T(8,128)(2,1)S(1)} %all-to-all-done.refs_15_) | copy-start | bytes 3145732
  32.5 1.4 %copy-start.13 = (bf16[2112,128]{1,0:T(8,128)(2,1)}, bf16[2112,128]{1,0:T(8,128)(2,1)S(1)}, u32[]{:S(2)}) copy-start(bf16[2112,128]{1,0:T(8,128)(2,1)S(1)} %collective-permute-done.6.refs_12_) | copy-start | bytes 1622020
  69.1 8.5 %collective-permute-start.9 = (bf16[4,1024,128]{2,1,0:T(8,128)(2,1)}, bf16[4,1024,128]{2,1,0:T(8,128)(2,1)S(1)}, u32[]{:S(2)}, u32[]{:S(2)}) collective-permute-start(bf16[4,1024,128]{2,1,0:T(8,128)(2,1)} %get-tuple-element.27), channel_id=1, source_target_pairs={{0,8},{8,0},{1,9},{9,1},{2,10},{10,2},{3,11},{11,3},{4,12},{12,4},... | collective-permute-start | bytes 3145736 | tf_op jit(solution)/shard_map/ppermute | solution.py:401
  69.1 8.5 %copy-start.1 = (bf16[3,1024,128]{2,1,0:T(8,128)(2,1)S(1)}, bf16[3,1024,128]{2,1,0:T(8,128)(2,1)}, u32[]{:S(2)}) copy-start(bf16[3,1024,128]{2,1,0:T(8,128)(2,1)} %get-tuple-element.28.own_ref) | copy-start | bytes 2359300
  69.1 27.1 %all-to-all-start.1 = ((bf16[16,128,256]{2,1,0:T(8,128)(2,1)}), bf16[16,128,256]{2,1,0:T(8,128)(2,1)S(1)}, u32[]{:S(2)}, u32[]{:S(2)}) async-start(bf16[16,128,256]{2,1,0:T(8,128)(2,1)} %get-tuple-element.32), calls=%async_computation.1 | async-start | bytes 2097152 | tf_op jit(solution)/shard_map/all_to_all | solution.py:412
  77.6 18.6 %copy-start.4 = (f32[1024,128]{1,0:T(8,128)S(1)}, f32[1024,128]{1,0:T(8,128)}, u32[]{:S(2)}) copy-start(f32[1024,128]{1,0:T(8,128)} %get-tuple-element.26.own_ref) | copy-start | bytes 1572868
  78.6 17.6 %collective-permute-start.10 = (bf16[1024,128]{1,0:T(8,128)(2,1)}, bf16[1024,128]{1,0:T(8,128)(2,1)S(1)}, u32[]{:S(2)}, u32[]{:S(2)}) collective-permute-start(bf16[1024,128]{1,0:T(8,128)(2,1)} %get-tuple-element.29), channel_id=1, source_target_pairs={{0,3},{1,0},{2,1},{3,2},{4,7},{5,4},{6,5},{7,6},{8,11},{9,8},{10,9... | collective-permute-start | bytes 786440 | tf_op jit(solution)/shard_map/ppermute | solution.py:398
  79.4 16.8 %collective-permute-start.11 = (bf16[1024,128]{1,0:T(8,128)(2,1)}, bf16[1024,128]{1,0:T(8,128)(2,1)S(1)}, u32[]{:S(2)}, u32[]{:S(2)}) collective-permute-start(bf16[1024,128]{1,0:T(8,128)(2,1)} %get-tuple-element.30), channel_id=1, source_target_pairs={{0,1},{1,2},{2,3},{3,0},{4,5},{5,6},{6,7},{7,4},{8,9},{9,10},{10,1... | collective-permute-start | bytes 786440 | tf_op jit(solution)/shard_map/ppermute | solution.py:398
  80.6 15.6 %collective-permute-start.12 = (bf16[1024,128]{1,0:T(8,128)(2,1)}, bf16[1024,128]{1,0:T(8,128)(2,1)S(1)}, u32[]{:S(2)}, u32[]{:S(2)}) collective-permute-start(bf16[1024,128]{1,0:T(8,128)(2,1)} %get-tuple-element.31), channel_id=1, source_target_pairs={{0,2},{1,3},{2,0},{3,1},{4,6},{5,7},{6,4},{7,5},{8,10},{9,11},{10,... | collective-permute-start | bytes 786440 | tf_op jit(solution)/shard_map/ppermute | solution.py:398
